TPU v7x, 768 devices: a whole 4x8x12 slice. The times are simulated.
768 devices in a mesh: row: 96 (over y_hi, z, x), col: 8 (over y_lo, core).
Axes of the slice: x: 4, y: 8 (y_hi: 2, y_lo: 4; y = y_hi * 4 + y_lo), z: 12, core: 2. Of those that a mesh axis runs over, the one named last changes fastest.
Arguments:
- features: bfloat16 [8, 6144, 256], P('col', 'row'), may hold values from -6 to 6
- weight: bfloat16 [256, 256], replicated, may hold values from -0.375 to 0.375
- cotangent: bfloat16 [96, 512, 256], P('row', 'col'), may hold values from -6 to 6
- tile_values: bfloat16 [96, 8, 32, 128, 128], P('row', 'col'), may hold values from -0.21875 to 0.21875
- tile_rows: int32 [96, 8, 32], P('row', 'col'), may hold values from 0 to 3
- tile_cols: int32 [96, 8, 32], P('row', 'col'), may hold values from 0 to 47
- tile_count: int32 [96, 8], P('row', 'col'), may hold values from 8 to 32, as said below
Outputs:
- output: bfloat16 [96, 512, 256], P('row', 'col')
- grad_features: bfloat16 [8, 6144, 256], P('col', 'row')
- grad_weight: float32 [256, 256], replicated
Inputs may be any that keep to these rules, and one draw needn't show every extreme that they name: `tile_count`: some grid block has all 32 slots live in every draw.
All inputs are finite; a program needn't handle non-finite values.
Results may differ from a plain program's by a relative error of at most 0.0063.
Values may be sent and summed in bfloat16 or wider, within the bound.
No kernel may reach another device: no remote copies, remote signals or barrier semaphores. Data moves between devices by JAX's collectives and lax.ppermute only.
A program may use at most 32 MiB of HBM per device.

v0:
```python
import jax
import jax.numpy as jnp
from jax import lax
from jax.sharding import PartitionSpec as P


def silu_slope(pre_act):
    sig = jax.nn.sigmoid(pre_act)
    return sig * (1.0 + pre_act * (1.0 - sig))


def on_device(features, weight, cotangent, tile_values, tile_rows, tile_cols, tile_count):
    own_rows = features[0]
    per_dev = own_rows.shape[0]
    slot_total = tile_values.shape[2]
    tile_size = tile_values.shape[3]
    row_devs = lax.axis_size("row")
    col_devs = lax.axis_size("col")
    row_tiles = per_dev * col_devs // tile_size
    col_tiles = per_dev * row_devs // tile_size
    row_index = tile_rows[0, 0]
    col_index = tile_cols[0, 0]
    live_mask = (jnp.arange(slot_total, dtype=jnp.int32) < tile_count[0, 0]).astype(jnp.bfloat16)
    blocks = tile_values[0, 0] * live_mask[:, None, None]
    row_hot = (row_index[:, None] == jnp.arange(row_tiles, dtype=jnp.int32)[None, :]).astype(
        jnp.float32
    )
    col_hot = (col_index[:, None] == jnp.arange(col_tiles, dtype=jnp.int32)[None, :]).astype(
        jnp.float32
    )
    column_feats = lax.all_gather(own_rows, "row", axis=0, tiled=True)
    cols_wide = column_feats.shape[1]
    picked = column_feats.reshape(col_tiles, tile_size, cols_wide)[col_index]
    products = jnp.einsum("sij,sjf->sif", blocks, picked, preferred_element_type=jnp.float32)
    spread = jnp.einsum("sr,sif->rif", row_hot, products, precision=lax.Precision.HIGHEST)
    partial_rows = spread.reshape(row_tiles * tile_size, cols_wide)
    aggregated = lax.psum_scatter(partial_rows, "col", scatter_dimension=0, tiled=True).astype(
        jnp.bfloat16
    )
    pre_act = jnp.dot(aggregated, weight, preferred_element_type=jnp.float32)
    output_rows = jax.nn.silu(pre_act).astype(jnp.bfloat16)
    grad_pre = (cotangent[0].astype(jnp.float32) * silu_slope(pre_act)).astype(jnp.bfloat16)
    weight_term = jnp.dot(aggregated.T, grad_pre, preferred_element_type=jnp.float32)
    grad_agg = lax.dot_general(
        grad_pre, weight, (((1,), (1,)), ((), ())), preferred_element_type=jnp.float32
    ).astype(jnp.bfloat16)
    row_grad_all = lax.all_gather(grad_agg, "col", axis=0, tiled=True)
    cols_wide = row_grad_all.shape[1]
    picked = row_grad_all.reshape(row_tiles, tile_size, cols_wide)[row_index]
    products = jnp.einsum("sji,sjf->sif", blocks, picked, preferred_element_type=jnp.float32)
    spread = jnp.einsum("sc,sif->cif", col_hot, products, precision=lax.Precision.HIGHEST)
    grad_rows = lax.psum_scatter(
        spread.reshape(col_tiles * tile_size, cols_wide), "row", scatter_dimension=0, tiled=True
    )
    node_total = per_dev * row_devs * col_devs
    grad_weight = lax.psum(weight_term, ("row", "col")) * node_total ** (-0.5)
    return (output_rows[None], grad_rows.astype(jnp.bfloat16)[None], grad_weight)


def solution(mesh):
    return jax.shard_map(
        on_device,
        mesh=mesh,
        in_specs=(
            P("col", "row", None),
            P(),
            P("row", "col", None),
            P("row", "col", None, None, None),
            P("row", "col", None),
            P("row", "col", None),
            P("row", "col"),
        ),
        out_specs=(P("row", "col", None), P("col", "row", None), P()),
        check_vma=False,
    )
```

profile of v0, /device:TPU:8, one launch (start us, length us, event | category | flops | bytes accessed | tf_op | source)
XLA Modules:
  0.0 1424.0 jit_solution(12308860409287008094)
XLA Ops:
  7.2 0.7 all-gather.3.cloned.1.call-update
  7.9 0.0 reduce-scatter.3.cloned.1.call-start
  8.6 0.7 fusion.20
  9.3 203.8 %all-gather.3.cloned.1.call-done = bf16[1,6144,256]{2,1,0:T(8,128)(2,1)} async-done(((bf16[1,64,256]{2,1,0:T(8,128)(2,1)}), bf16[1,6144,256]{2,1,0:T(8,128)(2,1)}) %all-gather.3.cloned.1.call-update) | async-done | bytes 3145744 | tf_op jit(solution)/shard_map/all_gather | solution.py:31
  213.1 2.6 gather_fusion
  215.7 0.8 fusion.5
  216.5 3.8 fusion.2
  220.3 0.9 copy.10
  221.2 0.0 all-reduce.2.cloned.1.call-start
  221.3 31.8 %reduce-scatter.3.cloned.1.call-done = f32[64,256]{1,0:T(8,128)} async-done(((f32[512,256]{1,0:T(8,128)}), f32[64,256]{1,0:T(8,128)}) %reduce-scatter.3.cloned.1.call-update) | async-done | bytes 65552 | tf_op jit(solution)/shard_map/reduce_scatter | solution.py:37
  253.1 1.0 fusion.12
  254.1 0.2 convolution_convert_fusion
  254.3 14.6 %all_gather.7 = bf16[512,256]{1,0:T(8,128)(2,1)S(1)} all-gather(bf16[64,256]{1,0:T(8,128)(2,1)S(1)} %convolution_convert_fusion), channel_id=1, replica_groups=mesh['row'=96,'col'=8] {'col'}, dimensions={0}, use_global_device_ids=true | all-gather | bytes 294912 | tf_op jit(solution)/shard_map/all_gather | solution.py:47
  269.0 0.7 gather_fusion.1
  269.7 3.1 fusion.4
  272.8 0.9 fusion.10
  273.7 0.2 reduce-scatter.5.cloned.1.call-start
  274.0 7.8 fusion
  281.8 6.3 copy.11
  288.1 0.6 fusion.9
  288.7 449.8 %all-reduce.2.cloned.1.call-done = f32[256,256]{1,0:T(8,128)} async-done(((f32[256,256]{1,0:T(8,128)}), f32[256,256]{1,0:T(8,128)}) %all-reduce.2.cloned.1.call-update) | async-done | bytes 262160 | tf_op jit(solution)/shard_map/psum | solution.py:56
  738.5 1.7 broadcast_multiply_fusion
  740.2 675.8 %reduce-scatter.5.cloned.1.call-done = f32[64,256]{1,0:T(8,128)} async-done(((f32[6144,256]{1,0:T(8,128)}), f32[64,256]{1,0:T(8,128)}) %reduce-scatter.5.cloned.1.call-update) | async-done | bytes 65552 | tf_op jit(solution)/shard_map/reduce_scatter | solution.py:52
  1416.0 1.5 convert_bitcast_fusion
  (26 shorter events, 0.2 us)
Async XLA Ops:
  7.2 246.0 %copy-start = (bf16[256,256]{1,0:T(8,128)(2,1)S(1)}, bf16[256,256]{1,0:T(8,128)(2,1)}, u32[]{:S(2)}) copy-start(bf16[256,256]{1,0:T(8,128)(2,1)} %param.8) | copy-start | bytes 393220
  7.2 208.5 %copy-start.1 = (bf16[1,1,32,128,128]{4,3,2,1,0:T(8,128)(2,1)S(1)}, bf16[1,1,32,128,128]{4,3,2,1,0:T(8,128)(2,1)}, u32[]{:S(2)}) copy-start(bf16[1,1,32,128,128]{4,3,2,1,0:T(8,128)(2,1)} %param.10) | copy-start | bytes 3145732
  7.2 205.9 %all-gather.3.cloned.1.call-start = ((), (), s32[]{:S(2)}) async-start(), calls=%async_computation.5 | async-start | bytes 3178496 | tf_op jit(solution)/shard_map/all_gather | solution.py:31
  7.9 245.2 %reduce-scatter.3.cloned.1.call-start = ((), (), s32[]{:S(2)}) async-start(), calls=%async_computation.2 | async-start | bytes 589824 | tf_op jit(solution)/shard_map/reduce_scatter | solution.py:37
  215.7 0.8 copy-start.7
  216.5 37.6 %copy-start.5 = (bf16[1,64,256]{2,1,0:T(8,128)(2,1)S(1)}, bf16[1,64,256]{2,1,0:T(8,128)(2,1)}, u32[]{:S(2)}) copy-start(bf16[1,64,256]{2,1,0:T(8,128)(2,1)} %param.9) | copy-start | bytes 98308
  221.2 517.3 %all-reduce.2.cloned.1.call-start = ((), (), s32[]{:S(2)}) async-start(), calls=%async_computation.4 | async-start | bytes 524288 | tf_op jit(solution)/shard_map/psum | solution.py:56
  254.1 14.8 %copy-start.2 = (f32[64,256]{1,0:T(8,128)}, f32[64,256]{1,0:T(8,128)S(1)}, u32[]{:S(2)}) copy-start(f32[64,256]{1,0:T(8,128)S(1)} %fusion.12) | copy-start | bytes 196612
  269.6 3.1 copy-start.3
  269.7 3.1 copy-start.4
  269.7 3.1 copy-start.6
  269.7 4.3 copy-start.8
  273.7 1142.3 %reduce-scatter.5.cloned.1.call-start = ((), (), s32[]{:S(2)}) async-start(), calls=%async_computation.3 | async-start | bytes 6356992 | tf_op jit(solution)/shard_map/reduce_scatter | solution.py:52
Sparse Core Ops, SparseCore 0:
  13.4 199.6 all-gather.2
  221.4 31.7 reduce-scatter.2
  273.8 464.6 all-reduce.1
  741.5 674.5 reduce-scatter.4
where the time goes:
time: 1420 us
  waiting for transfers between devices  1360 us (96%)
  matrix products  17.5 us (1%)
  blocking collectives  14.6 us (1%)
  between operations  14.6 us (1%)
    reduce_scatter x1, waiting for transfers between devices, on_device(): lax.psum_scatter(spread.reshape(col_tiles * tile_size, cols_wide), 'row',...  676 us
    psum x1, waiting for transfers between devices, on_device(): grad_weight = lax.psum(weight_term, ('row', 'col')) * node_total ** (-0.5)  450 us
    all_gather x1, waiting for transfers between devices, on_device(): column_feats = lax.all_gather(own_rows, 'row', axis=0, tiled=True)  204 us
    reduce_scatter x1, waiting for transfers between devices, on_device(): lax.psum_scatter(partial_rows, 'col', scatter_dimension=0, tiled=True)  31.8 us
  transfers between devices with their start and end apart: 4, of which 4 were waited for; matrix products, arithmetic and copies ran while one was open for 1% of the time, Pallas kernels for 0%

commit v1 on v0

v1 whole, which is shorter than its diff:
```python
import functools

import jax
import jax.numpy as jnp
from jax import lax
from jax.experimental import pallas as pl
from jax.experimental.pallas import tpu as pltpu
from jax.sharding import Mesh
from jax.sharding import PartitionSpec as P

BF = jnp.bfloat16
F32 = jnp.float32
TILE = 128
STRIP = 64
SPLIT = (2, 12, 4, 4, 2)
NAMES = ("yh", "z", "x", "yl", "core")
ROW = ("yh", "z", "x")
COL = ("yl", "core")
VMEM_LIMIT = 40 * 1024 * 1024


def spec(space):
    return pl.BlockSpec(memory_space=space)


def pack_kernel(info, tiles, cot, meta, same, other):
    slots = tiles.shape[0]
    odd = info[0] == 1

    def one(s, carry):
        turned = tiles[s].T
        low, high = turned[:STRIP], turned[STRIP:]
        same[s] = jnp.where(odd, high, low)
        other[s] = jnp.where(odd, low, high)
        return carry

    lax.fori_loop(0, slots, one, 0, unroll=4)
    for ref in (same, other):
        ref[slots] = cot[:, :TILE]
        ref[slots + 1] = cot[:, TILE:]
        ref[slots + 2] = jnp.broadcast_to(meta[...], (STRIP, TILE)).astype(BF)


def fwd_kernel(slots, nz, codes, info, s0, s1, s2, s3, feats, o0, o1, o2, o3, acc):
    rows = o0.shape[0]
    mine, my_yh = info[1], info[2]
    acc[...] = jnp.zeros_like(acc)
    for j, strips in enumerate((s0, s1, s2, s3)):

        def one(s, carry, j=j, strips=strips):
            code = codes[j, s]
            col, row = code >> 2, code & 3

            @pl.when((code >= 0) & ((col & 1) == mine))
            def _():
                q = col >> 1
                far = (q >= nz).astype(jnp.int32)
                place = (q - far * nz) * 2 + (far ^ my_yh)
                block = feats[pl.ds(pl.multiple_of(place * STRIP, STRIP), STRIP), :]
                term = lax.dot_general(strips[s], block, (((0,), (0,)), ((), ())), preferred_element_type=F32)
                at = pl.ds(pl.multiple_of(j * rows + row * TILE, TILE), TILE)
                acc[at, :] = acc[at, :] + term

            return carry

        lax.fori_loop(0, slots, one, 0)
    for j, ref in enumerate((o0, o1, o2, o3)):
        ref[...] = acc[j * rows : (j + 1) * rows, :].astype(ref.dtype)


def bwd_kernel(slots, codes, info, s0, s1, s2, s3, a0, a1, a2, a3, cot, w, out, chunks, ga, acc, gw, act):
    rows, feat = a0.shape
    mine, col_pos = info[1], info[3]
    share = feat // cot.shape[0]
    acc[...] = jnp.zeros_like(acc)
    for j, agg in enumerate((a0, a1, a2, a3)):
        pre = jnp.dot(agg[...], w[...], preferred_element_type=F32)
        sig = jax.nn.sigmoid(pre)
        if j == 0:
            act[...] = pre * sig
        slope = sig * (1.0 + pre * (1.0 - sig))
        cot_j = cot[:, j].reshape(rows, feat).astype(F32)
        gp = (cot_j * slope).astype(BF)
        term = lax.dot_general(agg[...], gp, (((0,), (0,)), ((), ())), preferred_element_type=F32)
        gw[...] = term if j == 0 else gw[...] + term
        ga[j * rows : (j + 1) * rows, :] = lax.dot_general(
            gp, w[...], (((1,), (1,)), ((), ())), preferred_element_type=F32
        ).astype(BF)
    out[...] = act[pl.ds(pl.multiple_of(col_pos * STRIP, STRIP), STRIP), :].astype(BF)
    for j, strips in enumerate((s0, s1, s2, s3)):

        def one(s, carry, j=j, strips=strips):
            code = codes[j, s]
            col, row = code >> 2, code & 3

            @pl.when((code >= 0) & ((col & 1) == mine))
            def _():
                block = ga[pl.ds(pl.multiple_of(j * rows + row * TILE, TILE), TILE), :]
                term = jnp.dot(strips[s], block, preferred_element_type=F32)
                at = pl.ds(pl.multiple_of((col >> 1) * STRIP, STRIP), STRIP)
                acc[at, :] = acc[at, :] + term

            return carry

        lax.fori_loop(0, slots, one, 0)
    part = gw[pl.ds(pl.multiple_of(col_pos * share, share), share), :].astype(BF)
    for q in range(chunks.shape[0]):
        chunks[q, :STRIP, :] = acc[q * STRIP : (q + 1) * STRIP, :].astype(BF)
        chunks[q, STRIP:, :] = part


def shift(value, axis, by):
    n = lax.axis_size(axis)
    return lax.ppermute(value, axis, [(i, (i + by) % n) for i in range(n)])


def on_device(features, weight, cotangent, tile_values, tile_rows, tile_cols, tile_count):
    own = features[0]
    per_dev, feat = own.shape
    slots = tile_values.shape[2]
    nz = lax.axis_size("z")
    groups = 2 * nz
    col_devs = lax.axis_size(COL)
    rows = per_dev * col_devs
    x = lax.axis_index("x")
    share = feat // col_devs
    info = jnp.stack([x % 2, x // 2, lax.axis_index("yh"), lax.axis_index(COL)]).astype(jnp.int32)
    params = pltpu.CompilerParams(vmem_limit_bytes=VMEM_LIMIT)
    vmem, smem = spec(pltpu.VMEM), spec(pltpu.SMEM)

    live = jnp.arange(slots, dtype=jnp.int32) < tile_count[0, 0]
    code = jnp.where(live, tile_rows[0, 0] + 4 * tile_cols[0, 0], -1)
    meta = jnp.pad(code.astype(F32), (0, TILE - slots))[None]

    facing = shift(own, "yh", 1)
    near = jnp.concatenate([own, facing], axis=0)

    parcel = jax.ShapeDtypeStruct((slots + 3, STRIP, TILE), BF)
    same, other = pl.pallas_call(
        pack_kernel,
        out_shape=(parcel, parcel),
        in_specs=[smem, vmem, vmem, vmem],
        out_specs=(vmem, vmem),
        compiler_params=params,
        name="pack",
    )(info, tile_values[0, 0], cotangent[0], meta)
    strips = [same] + [shift(same if d == 2 else other, "x", d) for d in (1, 2, 3)]

    column = lax.all_gather(near, "z", axis=0, tiled=True)

    codes = jnp.stack([code] + [s[slots + 2, 0, :slots].astype(jnp.int32) for s in strips[1:]])
    cots = jnp.stack([jnp.concatenate([s[slots], s[slots + 1]], axis=1) for s in strips])
    cot_all = lax.all_gather(cots.reshape(4 * STRIP, feat), COL, axis=0, tiled=True)
    cot_all = cot_all.reshape(col_devs, 4, STRIP, feat)

    half = jax.ShapeDtypeStruct((rows, feat), BF)
    parts = pl.pallas_call(
        functools.partial(fwd_kernel, slots, nz),
        out_shape=(jax.ShapeDtypeStruct((rows, feat), F32), half, half, half),
        in_specs=[smem, smem] + [vmem] * 5,
        out_specs=(vmem,) * 4,
        scratch_shapes=[pltpu.VMEM((4 * rows, feat), F32)],
        compiler_params=params,
        name="forward_tiles",
    )(codes, info, *strips, column)

    back = [shift(parts[d], "x", -d) for d in (1, 2, 3)]
    block_sum = (parts[0] + (back[0].astype(F32) + back[1].astype(F32) + back[2].astype(F32))).astype(BF)
    pieces = lax.all_to_all(block_sum, COL, split_axis=0, concat_axis=0, tiled=True)
    agg = jnp.sum(pieces.reshape(col_devs, per_dev, feat).astype(F32), axis=0).astype(BF)
    block_agg = lax.all_gather(agg, COL, axis=0, tiled=True)
    aggs = [block_agg] + [shift(block_agg, "x", d) for d in (1, 2, 3)]

    output_rows, chunks = pl.pallas_call(
        functools.partial(bwd_kernel, slots),
        out_shape=(
            jax.ShapeDtypeStruct((per_dev, feat), BF),
            jax.ShapeDtypeStruct((groups, STRIP + share, feat), BF),
        ),
        in_specs=[smem, smem] + [vmem] * 10,
        out_specs=(vmem, vmem),
        scratch_shapes=[
            pltpu.VMEM((4 * rows, feat), BF),
            pltpu.VMEM((groups * STRIP, feat), F32),
            pltpu.VMEM((feat, feat), F32),
            pltpu.VMEM((rows, feat), F32),
        ],
        compiler_params=params,
        name="backward_tiles",
    )(codes, info, *strips, *aggs, cot_all, weight)

    arrived = lax.all_to_all(chunks, ("yh", "z"), split_axis=0, concat_axis=0, tiled=True)
    total = jnp.sum(arrived.astype(F32), axis=0)
    node_total = per_dev * lax.axis_size(ROW) * col_devs
    grad_weight = lax.all_gather(total[STRIP:] * node_total ** (-0.5), COL, axis=0, tiled=True)
    return output_rows[None], total[:STRIP].astype(BF)[None], grad_weight


def build(mesh, split):
    grid = Mesh(mesh.devices.reshape(split), NAMES)
    return jax.shard_map(
        on_device,
        mesh=grid,
        in_specs=(
            P(COL, ROW, None),
            P(),
            P(ROW, COL, None),
            P(ROW, COL, None, None, None),
            P(ROW, COL, None),
            P(ROW, COL, None),
            P(ROW, COL),
        ),
        out_specs=(P(ROW, COL, None), P(COL, ROW, None), P()),
        check_vma=False,
    )


def solution(mesh):
    return build(mesh, SPLIT)
```

time: 1420 us -> 234 us (0.16)
  the two profiles are of different devices: /device:TPU:8 before, /device:TPU:1 now
where the time goes in v1:
time: 234 us
  blocking collectives  141 us (60%)
  starting transfers between devices  34.9 us (15%)
  waiting for transfers between devices  18.4 us (8%)
  Pallas kernels  17.8 us (8%)
  between operations  15 us (6%)
  local copies, waits for them, and re-layouts  4.57 us (2%)
    all_to_all x1, blocking collectives, on_device(): lax.all_to_all(chunks, ('yh', 'z'), split_axis=0, concat_axis=0, tiled=True)  53.8 us
    ppermute x10, starting transfers between devices, shift(): return lax.ppermute(value, axis, [(i, (i + by) % n) for i in range(n)])  34.9 us
    all_gather x1, blocking collectives, on_device(): column = lax.all_gather(near, 'z', axis=0, tiled=True)  32.3 us
    all_gather x1, blocking collectives, on_device(): lax.all_gather(total[STRIP:] * node_total ** (-0.5), COL, axis=0, tiled=T...  20.4 us
    all_to_all x1, blocking collectives, on_device(): lax.all_to_all(block_sum, COL, split_axis=0, concat_axis=0, tiled=True)  20 us
    ppermute x10, waiting for transfers between devices, shift(): return lax.ppermute(value, axis, [(i, (i + by) % n) for i in range(n)])  18.4 us
    all_gather x1, blocking collectives, on_device(): block_agg = lax.all_gather(agg, COL, axis=0, tiled=True)  14.7 us
    pallas_call x1, Pallas kernels, on_device(): pl.pallas_call(functools.partial(fwd_kernel, slots, nz), out_shape=(jax.S...  8.68 us
  transfers between devices with their start and end apart: 11, of which 5 were waited for; matrix products, arithmetic and copies ran while one was open for 0% of the time, Pallas kernels for 4%

profile of v1, /device:TPU:1, one launch (start us, length us, event | category | flops | bytes accessed | tf_op | source)
XLA Modules:
  0.0 233.8 jit_solution(12952630252307382338)
XLA Ops:
  8.7 1.2 copy-done
  10.7 1.3 pack.1
  11.9 5.2 %collective-permute-start.2 = (bf16[35,64,128]{2,1,0:T(8,128)(2,1)S(1)}, bf16[35,64,128]{2,1,0:T(8,128)(2,1)S(1)}, u32[]{:S(2)}, u32[]{:S(2)}) collective-permute-start(bf16[35,64,128]{2,1,0:T(8,128)(2,1)S(1)} %get-tuple-element.11), channel_id=1, source_target_pairs={{0,24},{8,0},{16,8},{24,16},{1,25},{9,1},{17,9},{25,17},{2,26},{10... | collective-permute-start | bytes 1720328 | tf_op jit(solution)/shard_map/ppermute | solution.py:114
  17.2 1.9 collective-permute-start
  19.1 7.5 %collective-permute-start.3 = (bf16[64,256]{1,0:T(8,128)(2,1)}, bf16[64,256]{1,0:T(8,128)(2,1)S(1)}, u32[]{:S(2)}, u32[]{:S(2)}) collective-permute-start(bf16[64,256]{1,0:T(8,128)(2,1)} %bitcast.66), channel_id=1, source_target_pairs={{0,384},{384,0},{1,385},{385,1},{2,386},{386,2},{3,387},{387,3},{4... | collective-permute-start | bytes 98312 | tf_op jit(solution)/shard_map/ppermute | solution.py:114
  26.6 3.6 %collective-permute-start.1 = (bf16[35,64,128]{2,1,0:T(8,128)(2,1)S(1)}, bf16[35,64,128]{2,1,0:T(8,128)(2,1)S(1)}, u32[]{:S(2)}, u32[]{:S(2)}) collective-permute-start(bf16[35,64,128]{2,1,0:T(8,128)(2,1)S(1)} %get-tuple-element.12.s0), channel_id=1, source_target_pairs={{0,16},{8,24},{16,0},{24,8},{1,17},{9,25},{17,1},{25,9},{2,18},{10... | collective-permute-start | bytes 1720328 | tf_op jit(solution)/shard_map/ppermute | solution.py:114
  30.3 32.3 %all_gather.12.feats = bf16[1536,256]{1,0:T(8,128)(2,1)S(1)} all-gather(bf16[128,256]{1,0:T(8,128)(2,1)S(1)} %pad_maximum_fusion.1), channel_id=1, replica_groups=mesh['yh'=2,'z'=12,'x'=4,'yl'=4,'core'=2] {'z'}, dimensions={0}, use_global_device_ids=true | all-gather | bytes 851968 | tf_op jit(solution)/shard_map/all_gather | solution.py:149
  63.5 8.7 %forward_tiles.1 = (f32[512,256]{1,0:T(8,128)S(1)}, bf16[512,256]{1,0:T(8,128)(2,1)S(1)}, bf16[512,256]{1,0:T(8,128)(2,1)S(1)}, bf16[512,256]{1,0:T(8,128)(2,1)S(1)}) custom-call(s32[4,32]{1,0:T(4,128)S(1)} %pad_add_fusion.codes, s32[4]{0:T(128)S(1)} %pad_add_fusion.1.info, bf16[35,64,128]{2,1,0:T(8,128)(2,1)S(1)} %get-tuple-element.12.s0, ...), custom_call_target="tpu_custom_call" | custom-call | tf_op jit(solution)/shard_map/forward_tiles/pallas_call | solution.py:157
  72.1 2.2 collective-permute-start.4
  74.4 4.7 %collective-permute-start.5 = (bf16[512,256]{1,0:T(8,128)(2,1)S(1)}, bf16[512,256]{1,0:T(8,128)(2,1)S(1)}, u32[]{:S(2)}, u32[]{:S(2)}) collective-permute-start(bf16[512,256]{1,0:T(8,128)(2,1)S(1)} %get-tuple-element.15), channel_id=1, source_target_pairs={{0,16},{8,24},{16,0},{24,8},{1,17},{9,25},{17,1},{25,9},{2,18},{10... | collective-permute-start | bytes 786440 | tf_op jit(solution)/shard_map/ppermute | solution.py:114
  79.1 1.9 collective-permute-start.6
  81.0 2.0 collective-permute-done.5
  83.0 4.8 %collective-permute-done.6 = bf16[512,256]{1,0:T(8,128)(2,1)S(1)} collective-permute-done((bf16[512,256]{1,0:T(8,128)(2,1)S(1)}, bf16[512,256]{1,0:T(8,128)(2,1)S(1)}, u32[]{:S(2)}, u32[]{:S(2)}) %collective-permute-start.6) | collective-permute-done | bytes 262176 | tf_op jit(solution)/shard_map/ppermute | solution.py:114
  87.9 20.0 %all_to_all.14 = bf16[8,64,256]{2,1,0:T(8,128)(2,1)S(1)} all-to-all(bf16[8,64,256]{2,1,0:T(8,128)(2,1)S(1)} %bitcast.64), channel_id=1, replica_groups=mesh['yh'=2,'z'=12,'x'=4,'yl'=4,'core'=2] {'yl','core'}, dimensions={0} | all-to-all | bytes 524288 | tf_op jit(solution)/shard_map/all_to_all | solution.py:169
  108.0 14.7 %all_gather.13.a0 = bf16[512,256]{1,0:T(8,128)(2,1)S(1)} all-gather(bf16[64,256]{1,0:T(8,128)(2,1)S(1)} %reduce_sum.21), channel_id=1, replica_groups=mesh['yh'=2,'z'=12,'x'=4,'yl'=4,'core'=2] {'yl','core'}, dimensions={0}, use_global_device_ids=true | all-gather | bytes 294912 | tf_op jit(solution)/shard_map/all_gather | solution.py:171
  122.7 2.2 collective-permute-start.9
  124.9 3.2 %collective-permute-start.8 = (bf16[512,256]{1,0:T(8,128)(2,1)S(1)}, bf16[512,256]{1,0:T(8,128)(2,1)S(1)}, u32[]{:S(2)}, u32[]{:S(2)}) collective-permute-start(bf16[512,256]{1,0:T(8,128)(2,1)S(1)} %all_gather.13.a0), channel_id=1, source_target_pairs={{0,16},{8,24},{16,0},{24,8},{1,17},{9,25},{17,1},{25,9},{2,18},{10... | collective-permute-start | bytes 786440 | tf_op jit(solution)/shard_map/ppermute | solution.py:114
  128.1 2.5 %collective-permute-start.7 = (bf16[512,256]{1,0:T(8,128)(2,1)S(1)}, bf16[512,256]{1,0:T(8,128)(2,1)S(1)}, u32[]{:S(2)}, u32[]{:S(2)}) collective-permute-start(bf16[512,256]{1,0:T(8,128)(2,1)S(1)} %all_gather.13.a0), channel_id=1, source_target_pairs={{0,8},{8,16},{16,24},{24,0},{1,9},{9,17},{17,25},{25,1},{2,10},{10... | collective-permute-start | bytes 786440 | tf_op jit(solution)/shard_map/ppermute | solution.py:114
  130.6 1.8 collective-permute-done.9.a3
  132.3 3.4 %collective-permute-done.8.a2 = bf16[512,256]{1,0:T(8,128)(2,1)S(1)} collective-permute-done((bf16[512,256]{1,0:T(8,128)(2,1)S(1)}, bf16[512,256]{1,0:T(8,128)(2,1)S(1)}, u32[]{:S(2)}, u32[]{:S(2)}) %collective-permute-start.8) | collective-permute-done | bytes 262176 | tf_op jit(solution)/shard_map/ppermute | solution.py:114
  135.7 6.4 %collective-permute-done.7.a1 = bf16[512,256]{1,0:T(8,128)(2,1)S(1)} collective-permute-done((bf16[512,256]{1,0:T(8,128)(2,1)S(1)}, bf16[512,256]{1,0:T(8,128)(2,1)S(1)}, u32[]{:S(2)}, u32[]{:S(2)}) %collective-permute-start.7) | collective-permute-done | bytes 262176 | tf_op jit(solution)/shard_map/ppermute | solution.py:114
  143.4 7.9 %backward_tiles.1 = (bf16[64,256]{1,0:T(8,128)(2,1)}, bf16[24,96,256]{2,1,0:T(8,128)(2,1)S(1)}) custom-call(s32[4,32]{1,0:T(4,128)S(1)} %pad_add_fusion.codes, s32[4]{0:T(128)S(1)} %pad_add_fusion.1.info, bf16[35,64,128]{2,1,0:T(8,128)(2,1)S(1)} %get-tuple-element.12.s0, bf16[35,64,128]{2,1,0:T(8,128)(2,1)S(1)} %collective-permute-done.s1, ...), custom_call_target="tpu_custom_call" | custom-call | tf_op jit(solution)/shard_map/backward_tiles/pallas_call | solution.py:174
  151.2 53.8 %all_to_all.15 = bf16[24,96,256]{2,1,0:T(8,128)(2,1)S(1)} all-to-all(bf16[24,96,256]{2,1,0:T(8,128)(2,1)S(1)} %get-tuple-element.18), channel_id=1, replica_groups=mesh['yh'=2,'z'=12,'x'=4,'yl'=4,'core'=2] {'yh','z'}, dimensions={0} | all-to-all | bytes 2359296 | tf_op jit(solution)/shard_map/all_to_all | solution.py:192
  205.9 20.4 %all_gather.15 = f32[256,256]{1,0:T(8,128)S(1)} all-gather(f32[32,256]{1,0:T(8,128)S(1)} %slice_multiply_fusion), channel_id=1, replica_groups=mesh['yh'=2,'z'=12,'x'=4,'yl'=4,'core'=2] {'yl','core'}, dimensions={0}, use_global_device_ids=true | all-gather | bytes 294912 | tf_op jit(solution)/shard_map/all_gather | solution.py:195
  (43 shorter events, 5.2 us)
Async XLA Ops:
  7.2 23.0 %copy-start.6 = (s32[1,1,32]{2,1,0:T(1,128)S(1)}, s32[1,1,32]{2,1,0:T(1,128)}, u32[]{:S(2)}) copy-start(s32[1,1,32]{2,1,0:T(1,128)} %param.12) | copy-start | bytes 388
  7.2 23.0 %copy-start.5 = (s32[1,1,32]{2,1,0:T(1,128)S(1)}, s32[1,1,32]{2,1,0:T(1,128)}, u32[]{:S(2)}) copy-start(s32[1,1,32]{2,1,0:T(1,128)} %param.11) | copy-start | bytes 388
  7.2 23.1 %copy-start.4 = (bf16[1,64,256]{2,1,0:T(8,128)(2,1)S(1)}, bf16[1,64,256]{2,1,0:T(8,128)(2,1)}, u32[]{:S(2)}) copy-start(bf16[1,64,256]{2,1,0:T(8,128)(2,1)} %param.7) | copy-start | bytes 98308
  7.2 134.9 %all-gather.2.cloned.1.call-start = ((), (), s32[]{:S(2)}) async-start(), calls=%async_computation.2 | async-start | bytes 1179648 | tf_op jit(solution)/shard_map/all_gather | solution.py:153
  8.7 1.2 copy-start
  9.9 0.8 copy-start.3
  11.9 50.7 %collective-permute-start.2 = (bf16[35,64,128]{2,1,0:T(8,128)(2,1)S(1)}, bf16[35,64,128]{2,1,0:T(8,128)(2,1)S(1)}, u32[]{:S(2)}, u32[]{:S(2)}) collective-permute-start(bf16[35,64,128]{2,1,0:T(8,128)(2,1)S(1)} %get-tuple-element.11), channel_id=1, source_target_pairs={{0,24},{8,0},{16,8},{24,16},{1,25},{9,1},{17,9},{25,17},{2,26},{10... | collective-permute-start | bytes 1720328 | tf_op jit(solution)/shard_map/ppermute | solution.py:114
  17.2 45.5 %collective-permute-start = (bf16[35,64,128]{2,1,0:T(8,128)(2,1)S(1)}, bf16[35,64,128]{2,1,0:T(8,128)(2,1)S(1)}, u32[]{:S(2)}, u32[]{:S(2)}) collective-permute-start(bf16[35,64,128]{2,1,0:T(8,128)(2,1)S(1)} %get-tuple-element.11), channel_id=1, source_target_pairs={{0,8},{8,16},{16,24},{24,0},{1,9},{9,17},{17,25},{25,1},{2,10},{10... | collective-permute-start | bytes 1720328 | tf_op jit(solution)/shard_map/ppermute | solution.py:114
  19.1 11.1 %collective-permute-start.3 = (bf16[64,256]{1,0:T(8,128)(2,1)}, bf16[64,256]{1,0:T(8,128)(2,1)S(1)}, u32[]{:S(2)}, u32[]{:S(2)}) collective-permute-start(bf16[64,256]{1,0:T(8,128)(2,1)} %bitcast.66), channel_id=1, source_target_pairs={{0,384},{384,0},{1,385},{385,1},{2,386},{386,2},{3,387},{387,3},{4... | collective-permute-start | bytes 98312 | tf_op jit(solution)/shard_map/ppermute | solution.py:114
  26.6 36.1 %collective-permute-start.1 = (bf16[35,64,128]{2,1,0:T(8,128)(2,1)S(1)}, bf16[35,64,128]{2,1,0:T(8,128)(2,1)S(1)}, u32[]{:S(2)}, u32[]{:S(2)}) collective-permute-start(bf16[35,64,128]{2,1,0:T(8,128)(2,1)S(1)} %get-tuple-element.12.s0), channel_id=1, source_target_pairs={{0,16},{8,24},{16,0},{24,8},{1,17},{9,25},{17,1},{25,9},{2,18},{10... | collective-permute-start | bytes 1720328 | tf_op jit(solution)/shard_map/ppermute | solution.py:114
  72.1 8.9 %collective-permute-start.4 = (bf16[512,256]{1,0:T(8,128)(2,1)S(1)}, bf16[512,256]{1,0:T(8,128)(2,1)S(1)}, u32[]{:S(2)}, u32[]{:S(2)}) collective-permute-start(bf16[512,256]{1,0:T(8,128)(2,1)S(1)} %get-tuple-element.14), channel_id=1, source_target_pairs={{0,24},{8,0},{16,8},{24,16},{1,25},{9,1},{17,9},{25,17},{2,26},{10... | collective-permute-start | bytes 786440 | tf_op jit(solution)/shard_map/ppermute | solution.py:114
  74.4 8.6 %collective-permute-start.5 = (bf16[512,256]{1,0:T(8,128)(2,1)S(1)}, bf16[512,256]{1,0:T(8,128)(2,1)S(1)}, u32[]{:S(2)}, u32[]{:S(2)}) collective-permute-start(bf16[512,256]{1,0:T(8,128)(2,1)S(1)} %get-tuple-element.15), channel_id=1, source_target_pairs={{0,16},{8,24},{16,0},{24,8},{1,17},{9,25},{17,1},{25,9},{2,18},{10... | collective-permute-start | bytes 786440 | tf_op jit(solution)/shard_map/ppermute | solution.py:114
  79.1 8.7 %collective-permute-start.6 = (bf16[512,256]{1,0:T(8,128)(2,1)S(1)}, bf16[512,256]{1,0:T(8,128)(2,1)S(1)}, u32[]{:S(2)}, u32[]{:S(2)}) collective-permute-start(bf16[512,256]{1,0:T(8,128)(2,1)S(1)} %get-tuple-element.16), channel_id=1, source_target_pairs={{0,8},{8,16},{16,24},{24,0},{1,9},{9,17},{17,25},{25,1},{2,10},{10... | collective-permute-start | bytes 786440 | tf_op jit(solution)/shard_map/ppermute | solution.py:114
  87.8 54.3 %copy-start.2 = (bf16[256,256]{1,0:T(8,128)(2,1)S(1)}, bf16[256,256]{1,0:T(8,128)(2,1)}, u32[]{:S(2)}) copy-start(bf16[256,256]{1,0:T(8,128)(2,1)} %w.1) | copy-start | bytes 393220
  122.7 9.6 %collective-permute-start.9 = (bf16[512,256]{1,0:T(8,128)(2,1)S(1)}, bf16[512,256]{1,0:T(8,128)(2,1)S(1)}, u32[]{:S(2)}, u32[]{:S(2)}) collective-permute-start(bf16[512,256]{1,0:T(8,128)(2,1)S(1)} %all_gather.13.a0), channel_id=1, source_target_pairs={{0,24},{8,0},{16,8},{24,16},{1,25},{9,1},{17,9},{25,17},{2,26},{10... | collective-permute-start | bytes 786440 | tf_op jit(solution)/shard_map/ppermute | solution.py:114
  124.9 10.9 %collective-permute-start.8 = (bf16[512,256]{1,0:T(8,128)(2,1)S(1)}, bf16[512,256]{1,0:T(8,128)(2,1)S(1)}, u32[]{:S(2)}, u32[]{:S(2)}) collective-permute-start(bf16[512,256]{1,0:T(8,128)(2,1)S(1)} %all_gather.13.a0), channel_id=1, source_target_pairs={{0,16},{8,24},{16,0},{24,8},{1,17},{9,25},{17,1},{25,9},{2,18},{10... | collective-permute-start | bytes 786440 | tf_op jit(solution)/shard_map/ppermute | solution.py:114
  128.1 14.0 %collective-permute-start.7 = (bf16[512,256]{1,0:T(8,128)(2,1)S(1)}, bf16[512,256]{1,0:T(8,128)(2,1)S(1)}, u32[]{:S(2)}, u32[]{:S(2)}) collective-permute-start(bf16[512,256]{1,0:T(8,128)(2,1)S(1)} %all_gather.13.a0), channel_id=1, source_target_pairs={{0,8},{8,16},{16,24},{24,0},{1,9},{9,17},{17,25},{25,1},{2,10},{10... | collective-permute-start | bytes 786440 | tf_op jit(solution)/shard_map/ppermute | solution.py:114
  142.1 1.2 copy-start.1
Sparse Core Ops, SparseCore 0:
  63.5 40.3 all-gather.1

commit v2 on v1

v2 whole, which is shorter than its diff:
```python
import functools

import jax
import jax.numpy as jnp
from jax import lax
from jax.experimental import pallas as pl
from jax.experimental.pallas import tpu as pltpu
from jax.sharding import Mesh
from jax.sharding import PartitionSpec as P

BF = jnp.bfloat16
F32 = jnp.float32
TILE = 128
STRIP = 64
SPLIT = (2, 12, 4, 4, 2)
NAMES = ("yh", "z", "x", "yl", "core")
ROW = ("yh", "z", "x")
COL = ("yl", "core")
VMEM_LIMIT = 40 * 1024 * 1024


def spec(space):
    return pl.BlockSpec(memory_space=space)


def pack_kernel(info, tiles, cot, meta, same, other):
    slots = tiles.shape[0]
    odd = info[0] == 1

    def one(s, carry):
        turned = tiles[s].T
        low, high = turned[:STRIP], turned[STRIP:]
        same[s] = jnp.where(odd, high, low)
        other[s] = jnp.where(odd, low, high)
        return carry

    lax.fori_loop(0, slots, one, 0, unroll=4)
    for ref in (same, other):
        ref[slots] = cot[:, :TILE]
        ref[slots + 1] = cot[:, TILE:]
        ref[slots + 2] = jnp.broadcast_to(meta[...], (STRIP, TILE)).astype(BF)


def fwd_kernel(slots, nz, codes, info, places, s0, s1, s2, s3, f0, f1, f2, o0, o1, o2, o3, feats, acc):
    rows = o0.shape[0]
    mine, my_yh, my_z = info[1], info[2], info[4]
    acc[...] = jnp.zeros_like(acc)
    part = f0.shape[0]
    for i, ref in enumerate((f0, f1, f2)):
        feats[i * part : (i + 1) * part, :] = ref[...]
    for j, strips in enumerate((s0, s1, s2, s3)):

        def one(s, carry, j=j, strips=strips):
            code = codes[j, s]
            col, row = code >> 2, code & 3

            @pl.when((code >= 0) & ((col & 1) == mine))
            def _():
                q = col >> 1
                far = (q >= nz).astype(jnp.int32)
                away = q - far * nz - my_z
                away = jnp.where(away < 0, away + nz, away)
                place = places[away] * 2 + (far ^ my_yh)
                block = feats[pl.ds(pl.multiple_of(place * STRIP, STRIP), STRIP), :]
                term = lax.dot_general(strips[s], block, (((0,), (0,)), ((), ())), preferred_element_type=F32)
                at = pl.ds(pl.multiple_of(j * rows + row * TILE, TILE), TILE)
                acc[at, :] = acc[at, :] + term

            return carry

        lax.fori_loop(0, slots, one, 0)
    for j, ref in enumerate((o0, o1, o2, o3)):
        ref[...] = acc[j * rows : (j + 1) * rows, :].astype(ref.dtype)


def bwd_kernel(
    slots, nz, codes, info, s0, s1, s2, s3, a0, a1, a2, a3, cot, w, out, keep, up, down, ga, acc, gw4, gw, act
):
    rows, feat = a0.shape
    mine, my_yh, col_pos, my_z, my_x = info[1], info[2], info[3], info[4], info[5]
    third = gw.shape[0] // 3
    acc[...] = jnp.zeros_like(acc)
    for j, agg in enumerate((a0, a1, a2, a3)):
        pre = jnp.dot(agg[...], w[...], preferred_element_type=F32)
        sig = jax.nn.sigmoid(pre)
        if j == 0:
            act[...] = pre * sig
        slope = sig * (1.0 + pre * (1.0 - sig))
        cot_j = cot[:, j].reshape(rows, feat).astype(F32)
        gp = (cot_j * slope).astype(BF)
        gw4[(my_x - j) & 3] = lax.dot_general(agg[...], gp, (((0,), (0,)), ((), ())), preferred_element_type=F32)
        ga[j * rows : (j + 1) * rows, :] = lax.dot_general(
            gp, w[...], (((1,), (1,)), ((), ())), preferred_element_type=F32
        ).astype(BF)
    out[...] = act[pl.ds(pl.multiple_of(col_pos * STRIP, STRIP), STRIP), :].astype(BF)
    gw[:feat, :] = (gw4[0] + gw4[1]) + (gw4[2] + gw4[3])
    gw[feat:, :] = jnp.zeros((gw.shape[0] - feat, feat), F32)
    for j, strips in enumerate((s0, s1, s2, s3)):

        def one(s, carry, j=j, strips=strips):
            code = codes[j, s]
            col, row = code >> 2, code & 3

            @pl.when((code >= 0) & ((col & 1) == mine))
            def _():
                block = ga[pl.ds(pl.multiple_of(j * rows + row * TILE, TILE), TILE), :]
                term = jnp.dot(strips[s], block, preferred_element_type=F32)
                at = pl.ds(pl.multiple_of((col >> 1) * STRIP, STRIP), STRIP)
                acc[at, :] = acc[at, :] + term

            return carry

        lax.fori_loop(0, slots, one, 0)
    for base, ref in ((0, keep), (1, up), (-1, down)):
        for k, stride in enumerate((0, 3, -3, 6)):
            to_z = lax.rem(my_z + (base + stride + nz), nz)
            for i in range(2):
                q = (my_yh ^ i) * nz + to_z
                at = (2 * k + i) * STRIP
                ref[at : at + STRIP, :] = acc[pl.ds(pl.multiple_of(q * STRIP, STRIP), STRIP), :].astype(ref.dtype)
        which = lax.rem(my_z + (base + 3), 3)
        ref[8 * STRIP :, :] = gw[pl.ds(pl.multiple_of(which * third, third), third), :].astype(ref.dtype)


def near_kernel(keep, up, down, p1, p2, p3, own, weight_own):
    block = 2 * STRIP

    def total(lo, hi):
        return keep[lo:hi, :] + up[lo:hi, :].astype(F32) + down[lo:hi, :].astype(F32)

    tail = total(4 * block, keep.shape[0]).astype(BF)
    own[...] = total(0, block)
    weight_own[...] = tail
    for k, ref in enumerate((p1, p2, p3)):
        ref[:block, :] = total((k + 1) * block, (k + 2) * block).astype(BF)
        ref[block:, :] = tail


def far_kernel(info, own, weight_own, r1, r2, r3, send, keep, weight_sum, terms):
    block = 2 * STRIP
    group = lax.div(info[4], 3)
    total = own[...]
    terms[group] = weight_own[...].astype(F32)
    for ref, step in ((r1, 3), (r2, 1), (r3, 2)):
        total = total + ref[:block, :].astype(F32)
        terms[(group + step) & 3] = ref[block:, :].astype(F32)
    summed = ((terms[0] + terms[1]) + (terms[2] + terms[3])).astype(BF)
    keep[...] = total[:STRIP]
    send[:STRIP, :] = total[STRIP:].astype(BF)
    send[STRIP:, :] = summed
    weight_sum[...] = summed


def last_kernel(scale, keep, weight_sum, arrived, grads, weight_third):
    grads[...] = (keep[...] + arrived[:STRIP, :].astype(F32)).astype(BF)
    weight_third[...] = (weight_sum[...].astype(F32) + arrived[STRIP:, :].astype(F32)) * scale


def join_kernel(info, own, below, above, out, whole):
    third = own.shape[0]
    for ref, step in ((own, 0), (below, 2), (above, 1)):
        which = lax.rem(info[4] + step, 3)
        whole[pl.ds(pl.multiple_of(which * third, third), third), :] = ref[...]
    out[...] = whole[: out.shape[0], :]


def shift(value, axis, by):
    n = lax.axis_size(axis)
    return lax.ppermute(value, axis, [(i, (i + by) % n) for i in range(n)])


def on_device(features, weight, cotangent, tile_values, tile_rows, tile_cols, tile_count):
    own = features[0]
    per_dev, feat = own.shape
    slots = tile_values.shape[2]
    nz = lax.axis_size("z")
    groups = 2 * nz
    col_devs = lax.axis_size(COL)
    rows = per_dev * col_devs
    x, z = lax.axis_index("x"), lax.axis_index("z")
    info = jnp.stack([x % 2, x // 2, lax.axis_index("yh"), lax.axis_index(COL), z, x]).astype(jnp.int32)
    params = pltpu.CompilerParams(vmem_limit_bytes=VMEM_LIMIT)
    vmem, smem = spec(pltpu.VMEM), spec(pltpu.SMEM)

    def call(kernel, name, ins, outs, scratch, *args):
        return pl.pallas_call(
            kernel,
            out_shape=tuple(jax.ShapeDtypeStruct(s, t) for s, t in outs),
            in_specs=ins,
            out_specs=(vmem,) * len(outs),
            scratch_shapes=[pltpu.VMEM(s, t) for s, t in scratch],
            compiler_params=params,
            name=name,
        )(*args)

    live = jnp.arange(slots, dtype=jnp.int32) < tile_count[0, 0]
    code = jnp.where(live, tile_rows[0, 0] + 4 * tile_cols[0, 0], -1)
    meta = jnp.pad(code.astype(F32), (0, TILE - slots))[None]

    facing = shift(own, "yh", 1)
    near = jnp.concatenate([own, facing], axis=0)
    group = jnp.concatenate([near] + [shift(near, "z", d) for d in (3, -3, 6)], axis=0)
    below, above = shift(group, "z", 1), shift(group, "z", -1)
    places = jnp.array([0, 8, 6, 2, 10, 7, 3, 11, 5, 1, 9, 4], jnp.int32)

    parcel = ((slots + 3, STRIP, TILE), BF)
    same, other = call(
        pack_kernel, "pack", [smem, vmem, vmem, vmem], [parcel] * 2, [], info, tile_values[0, 0], cotangent[0], meta
    )
    strips = [same] + [shift(same if d == 2 else other, "x", d) for d in (1, 2, 3)]
    codes = jnp.stack([code] + [s[slots + 2, 0, :slots].astype(jnp.int32) for s in strips[1:]])
    cots = jnp.stack([jnp.concatenate([s[slots], s[slots + 1]], axis=1) for s in strips])
    cot_all = lax.all_gather(cots.reshape(4 * STRIP, feat), COL, axis=0, tiled=True)
    cot_all = cot_all.reshape(col_devs, 4, STRIP, feat)

    parts = call(
        functools.partial(fwd_kernel, slots, nz),
        "forward_tiles",
        [smem, smem, smem] + [vmem] * 7,
        [((rows, feat), F32)] + [((rows, feat), BF)] * 3,
        [((groups * STRIP, feat), BF), ((4 * rows, feat), F32)],
        codes, info, places, *strips, group, below, above,
    )

    back = [shift(parts[d], "x", -d) for d in (1, 2, 3)]
    block_sum = (parts[0] + (back[0].astype(F32) + back[1].astype(F32) + back[2].astype(F32))).astype(BF)
    pieces = lax.all_to_all(block_sum, COL, split_axis=0, concat_axis=0, tiled=True)
    agg = jnp.sum(pieces.reshape(col_devs, per_dev, feat).astype(F32), axis=0).astype(BF)
    block_agg = lax.all_gather(agg, COL, axis=0, tiled=True)
    aggs = [block_agg] + [shift(block_agg, "x", d) for d in (1, 2, 3)]

    third = -(-feat // 48) * 16
    group_rows = 8 * STRIP + third
    output_rows, keep, up, down = call(
        functools.partial(bwd_kernel, slots, nz),
        "backward_tiles",
        [smem, smem] + [vmem] * 10,
        [((per_dev, feat), BF), ((group_rows, feat), F32), ((group_rows, feat), BF), ((group_rows, feat), BF)],
        [
            ((4 * rows, feat), BF),
            ((groups * STRIP, feat), F32),
            ((4, feat, feat), F32),
            ((3 * third, feat), F32),
            ((rows, feat), F32),
        ],
        codes, info, *strips, *aggs, cot_all, weight,
    )

    message = ((2 * STRIP + third, feat), BF)
    p1, p2, p3, own_rows, weight_own = call(
        near_kernel,
        "near_sum",
        [vmem] * 3,
        [message] * 3 + [((2 * STRIP, feat), F32), ((third, feat), BF)],
        [],
        keep, shift(up, "z", 1), shift(down, "z", -1),
    )
    send, keep_rows, weight_sum = call(
        far_kernel,
        "far_sum",
        [smem] + [vmem] * 5,
        [((STRIP + third, feat), BF), ((STRIP, feat), F32), ((third, feat), BF)],
        [((4, third, feat), F32)],
        info, own_rows, weight_own, shift(p1, "z", 3), shift(p2, "z", -3), shift(p3, "z", 6),
    )
    node_total = per_dev * lax.axis_size(ROW) * col_devs
    grads, weight_third = call(
        functools.partial(last_kernel, node_total ** (-0.5)),
        "last_sum",
        [vmem] * 3,
        [((STRIP, feat), BF), ((third, feat), F32)],
        [],
        keep_rows, weight_sum, shift(send, "yh", 1),
    )
    (grad_weight,) = call(
        join_kernel,
        "join_weight",
        [smem] + [vmem] * 3,
        [((feat, feat), F32)],
        [((3 * third, feat), F32)],
        info, weight_third, shift(weight_third, "z", 1), shift(weight_third, "z", -1),
    )
    return output_rows[None], grads[None], grad_weight


def build(mesh, split):
    grid = Mesh(mesh.devices.reshape(split), NAMES)
    return jax.shard_map(
        on_device,
        mesh=grid,
        in_specs=(
            P(COL, ROW, None),
            P(),
            P(ROW, COL, None),
            P(ROW, COL, None, None, None),
            P(ROW, COL, None),
            P(ROW, COL, None),
            P(ROW, COL),
        ),
        out_specs=(P(ROW, COL, None), P(COL, ROW, None), P()),
        check_vma=False,
    )


def solution(mesh):
    return build(mesh, SPLIT)
```

time: 234 us -> 233 us (level); the launches traced: 234 us -> 229 us
  blocking collectives: 141 us -> 31.1 us
  starting transfers between devices: 34.9 us -> 111 us
  waiting for transfers between devices: 18.4 us -> 49.3 us
    ppermute x10 -> x23, starting transfers between devices: 34.9 us -> 111 us  [shift(): return lax.ppermute(value, axis, [(i, (i + by) % n) for i in range(n)])]
    all_to_all x1 -> x0, blocking collectives: 53.8 us -> none  [on_device(): lax.all_to_all(chunks, ('yh', 'z'), split_axis=0, concat_axis=0, tiled=True)]
    all_gather x2 -> x0, blocking collectives: 52.7 us -> none  [the longest x1 32.3 us: on_device(): column = lax.all_gather(near, 'z', axis=0, tiled=True)]
    ppermute x10 -> x23, waiting for transfers between devices: 18.4 us -> 49.3 us  [shift(): return lax.ppermute(value, axis, [(i, (i + by) % n) for i in range(n)])]
    all_to_all x1, blocking collectives: 20 us -> 15.8 us  [on_device(): lax.all_to_all(block_sum, COL, split_axis=0, concat_axis=0, tiled=True)]
    pallas_call x3 -> x7, Pallas kernels: 17.8 us -> 17.3 us  [call(): pl.pallas_call(kernel, out_shape=tuple((jax.ShapeDtypeStruct(s, t) for s,...]
  transfers between devices with their start and end apart: 11 -> 24, of which waited for: 5 -> 15; matrix products, arithmetic and copies ran while one was open for 0% -> 0% of each run, Pallas kernels for 4% -> 3%
where the time goes in v2:
time: 233 us; the launch traced here: 229 us
  starting transfers between devices  111 us (48%)
  waiting for transfers between devices  49.3 us (21%)
  blocking collectives  31.1 us (13%)
  Pallas kernels  17.3 us (7%)
  between operations  15.2 us (7%)
  local copies, waits for them, and re-layouts  3.27 us (1%)
    ppermute x23, starting transfers between devices, shift(): return lax.ppermute(value, axis, [(i, (i + by) % n) for i in range(n)])  111 us
    ppermute x23, waiting for transfers between devices, shift(): return lax.ppermute(value, axis, [(i, (i + by) % n) for i in range(n)])  49.3 us
    pallas_call x7, Pallas kernels, call(): pl.pallas_call(kernel, out_shape=tuple((jax.ShapeDtypeStruct(s, t) for s,...  17.3 us
    all_to_all x1, blocking collectives, on_device(): lax.all_to_all(block_sum, COL, split_axis=0, concat_axis=0, tiled=True)  15.8 us
    all_gather x1, blocking collectives, on_device(): block_agg = lax.all_gather(agg, COL, axis=0, tiled=True)  15.2 us
  transfers between devices with their start and end apart: 24, of which 15 were waited for; matrix products, arithmetic and copies ran while one was open for 0% of the time, Pallas kernels for 3%

profile of v2, /device:TPU:1, one launch (start us, length us, event | category | flops | bytes accessed | tf_op | source)
XLA Modules:
  0.0 228.6 jit_solution(15420531469626528527)
XLA Ops:
  11.2 5.2 %collective-permute-start.2 = (bf16[35,64,128]{2,1,0:T(8,128)(2,1)S(1)}, bf16[35,64,128]{2,1,0:T(8,128)(2,1)S(1)}, u32[]{:S(2)}, u32[]{:S(2)}) collective-permute-start(bf16[35,64,128]{2,1,0:T(8,128)(2,1)S(1)} %get-tuple-element.23), channel_id=1, source_target_pairs={{0,24},{8,0},{16,8},{24,16},{1,25},{9,1},{17,9},{25,17},{2,26},{10... | collective-permute-start | bytes 1720328 | tf_op jit(solution)/shard_map/ppermute | solution.py:169
  18.4 7.5 %collective-permute-start.3 = (bf16[64,256]{1,0:T(8,128)(2,1)S(1)}, bf16[64,256]{1,0:T(8,128)(2,1)S(1)}, u32[]{:S(2)}, u32[]{:S(2)}) collective-permute-start(bf16[64,256]{1,0:T(8,128)(2,1)S(1)} %bitcast.68), channel_id=1, source_target_pairs={{0,384},{384,0},{1,385},{385,1},{2,386},{386,2},{3,387},{387,3},{4... | collective-permute-start | bytes 98312 | tf_op jit(solution)/shard_map/ppermute | solution.py:169
  29.5 14.9 %collective-permute-start.6 = (bf16[128,256]{1,0:T(8,128)(2,1)S(1)}, bf16[128,256]{1,0:T(8,128)(2,1)S(1)}, u32[]{:S(2)}, u32[]{:S(2)}) collective-permute-start(bf16[128,256]{1,0:T(8,128)(2,1)S(1)} %pad_maximum_fusion.1), channel_id=1, source_target_pairs={{0,192},{32,224},{64,256},{96,288},{128,320},{160,352},{192,0},{22... | collective-permute-start | bytes 196616 | tf_op jit(solution)/shard_map/ppermute | solution.py:169
  44.4 4.9 %collective-permute-start.4 = (bf16[128,256]{1,0:T(8,128)(2,1)S(1)}, bf16[128,256]{1,0:T(8,128)(2,1)S(1)}, u32[]{:S(2)}, u32[]{:S(2)}) collective-permute-start(bf16[128,256]{1,0:T(8,128)(2,1)S(1)} %pad_maximum_fusion.1), channel_id=1, source_target_pairs={{0,96},{32,128},{64,160},{96,192},{128,224},{160,256},{192,288},{2... | collective-permute-start | bytes 196616 | tf_op jit(solution)/shard_map/ppermute | solution.py:169
  49.3 4.2 %collective-permute-done.4 = bf16[128,256]{1,0:T(8,128)(2,1)S(1)} collective-permute-done((bf16[128,256]{1,0:T(8,128)(2,1)S(1)}, bf16[128,256]{1,0:T(8,128)(2,1)S(1)}, u32[]{:S(2)}, u32[]{:S(2)}) %collective-permute-start.4) | collective-permute-done | bytes 65568 | tf_op jit(solution)/shard_map/ppermute | solution.py:169
  55.4 4.9 %collective-permute-done.5 = bf16[128,256]{1,0:T(8,128)(2,1)S(1)} collective-permute-done((bf16[128,256]{1,0:T(8,128)(2,1)S(1)}, bf16[128,256]{1,0:T(8,128)(2,1)S(1)}, u32[]{:S(2)}, u32[]{:S(2)}) %collective-permute-start.5) | collective-permute-done | bytes 65568 | tf_op jit(solution)/shard_map/ppermute | solution.py:169
  60.3 6.9 %collective-permute-start.8 = (bf16[512,256]{1,0:T(8,128)(2,1)S(1)}, bf16[512,256]{1,0:T(8,128)(2,1)S(1)}, u32[]{:S(2)}, u32[]{:S(2)}) collective-permute-start(bf16[512,256]{1,0:T(8,128)(2,1)S(1)} %constant_dynamic-update-slice_fusion.f0), channel_id=1, source_target_pairs={{0,352},{32,0},{64,32},{96,64},{128,96},{160,128},{192,160},{224,1... | collective-permute-start | bytes 786440 | tf_op jit(solution)/shard_map/ppermute | solution.py:169
  71.9 5.0 %collective-permute-done.7.f1 = bf16[512,256]{1,0:T(8,128)(2,1)S(1)} collective-permute-done((bf16[512,256]{1,0:T(8,128)(2,1)S(1)}, bf16[512,256]{1,0:T(8,128)(2,1)S(1)}, u32[]{:S(2)}, u32[]{:S(2)}) %collective-permute-start.7) | collective-permute-done | bytes 262176 | tf_op jit(solution)/shard_map/ppermute | solution.py:169
  76.9 6.5 %forward_tiles.1 = (f32[512,256]{1,0:T(8,128)S(1)}, bf16[512,256]{1,0:T(8,128)(2,1)S(1)}, bf16[512,256]{1,0:T(8,128)(2,1)S(1)}, bf16[512,256]{1,0:T(8,128)(2,1)S(1)}) custom-call(s32[4,32]{1,0:T(4,128)S(1)} %pad_add_fusion.codes, s32[6]{0:T(128)S(1)} %stack.49.info, s32[12]{0:T(128)S(1)} %copy-done.4, bf16[35,64,128]{2,1,0:T(8,128)(2,1)S(1)} %get-tuple-element.24.s0, ...), custom_call_target="tpu_custom_call" | custom-call | tf_op jit(solution)/shard_map/forward_tiles/pallas_call | solution.py:186
  86.8 4.3 %collective-permute-start.10 = (bf16[512,256]{1,0:T(8,128)(2,1)S(1)}, bf16[512,256]{1,0:T(8,128)(2,1)S(1)}, u32[]{:S(2)}, u32[]{:S(2)}) collective-permute-start(bf16[512,256]{1,0:T(8,128)(2,1)S(1)} %get-tuple-element.27), channel_id=1, source_target_pairs={{0,16},{8,24},{16,0},{24,8},{1,17},{9,25},{17,1},{25,9},{2,18},{10... | collective-permute-start | bytes 786440 | tf_op jit(solution)/shard_map/ppermute | solution.py:169
  95.4 7.3 %collective-permute-done.11 = bf16[512,256]{1,0:T(8,128)(2,1)S(1)} collective-permute-done((bf16[512,256]{1,0:T(8,128)(2,1)S(1)}, bf16[512,256]{1,0:T(8,128)(2,1)S(1)}, u32[]{:S(2)}, u32[]{:S(2)}) %collective-permute-start.11) | collective-permute-done | bytes 262176 | tf_op jit(solution)/shard_map/ppermute | solution.py:169
  102.8 15.8 %all_to_all.9 = bf16[8,64,256]{2,1,0:T(8,128)(2,1)S(1)} all-to-all(bf16[8,64,256]{2,1,0:T(8,128)(2,1)S(1)} %bitcast.66), channel_id=1, replica_groups=mesh['yh'=2,'z'=12,'x'=4,'yl'=4,'core'=2] {'yl','core'}, dimensions={0} | all-to-all | bytes 524288 | tf_op jit(solution)/shard_map/all_to_all | solution.py:227
  118.7 15.2 %all_gather.6.a0 = bf16[512,256]{1,0:T(8,128)(2,1)S(1)} all-gather(bf16[64,256]{1,0:T(8,128)(2,1)S(1)} %reduce_sum.12), channel_id=1, replica_groups=mesh['yh'=2,'z'=12,'x'=4,'yl'=4,'core'=2] {'yl','core'}, dimensions={0}, use_global_device_ids=true | all-gather | bytes 294912 | tf_op jit(solution)/shard_map/all_gather | solution.py:229
  136.1 4.3 %collective-permute-start.13 = (bf16[512,256]{1,0:T(8,128)(2,1)S(1)}, bf16[512,256]{1,0:T(8,128)(2,1)S(1)}, u32[]{:S(2)}, u32[]{:S(2)}) collective-permute-start(bf16[512,256]{1,0:T(8,128)(2,1)S(1)} %all_gather.6.a0), channel_id=1, source_target_pairs={{0,16},{8,24},{16,0},{24,8},{1,17},{9,25},{17,1},{25,9},{2,18},{10... | collective-permute-start | bytes 786440 | tf_op jit(solution)/shard_map/ppermute | solution.py:169
  147.0 6.3 %collective-permute-done.12.a1 = bf16[512,256]{1,0:T(8,128)(2,1)S(1)} collective-permute-done((bf16[512,256]{1,0:T(8,128)(2,1)S(1)}, bf16[512,256]{1,0:T(8,128)(2,1)S(1)}, u32[]{:S(2)}, u32[]{:S(2)}) %collective-permute-start.12) | collective-permute-done | bytes 262176 | tf_op jit(solution)/shard_map/ppermute | solution.py:169
  154.5 6.8 %backward_tiles.1 = (bf16[64,256]{1,0:T(8,128)(2,1)}, f32[608,256]{1,0:T(8,128)S(1)}, bf16[608,256]{1,0:T(8,128)(2,1)S(1)}, bf16[608,256]{1,0:T(8,128)(2,1)S(1)}) custom-call(s32[4,32]{1,0:T(4,128)S(1)} %pad_add_fusion.codes, s32[6]{0:T(128)S(1)} %stack.49.info, bf16[35,64,128]{2,1,0:T(8,128)(2,1)S(1)} %get-tuple-element.24.s0, ...), custom_call_target="tpu_custom_call" | custom-call | tf_op jit(solution)/shard_map/backward_tiles/pallas_call | solution.py:186
  163.2 4.6 %collective-permute-start.16 = (bf16[608,256]{1,0:T(8,128)(2,1)S(1)}, bf16[608,256]{1,0:T(8,128)(2,1)S(1)}, u32[]{:S(2)}, u32[]{:S(2)}) collective-permute-start(bf16[608,256]{1,0:T(8,128)(2,1)S(1)} %get-tuple-element.32), channel_id=1, source_target_pairs={{0,352},{32,0},{64,32},{96,64},{128,96},{160,128},{192,160},{224,1... | collective-permute-start | bytes 933896 | tf_op jit(solution)/shard_map/ppermute | solution.py:169
  172.7 5.3 %collective-permute-start.17 = (bf16[224,256]{1,0:T(8,128)(2,1)S(1)}, bf16[224,256]{1,0:T(8,128)(2,1)S(1)}, u32[]{:S(2)}, u32[]{:S(2)}) collective-permute-start(bf16[224,256]{1,0:T(8,128)(2,1)S(1)} %get-tuple-element.35), channel_id=1, source_target_pairs={{0,96},{32,128},{64,160},{96,192},{128,224},{160,256},{192,288},{2... | collective-permute-start | bytes 344072 | tf_op jit(solution)/shard_map/ppermute | solution.py:169
  178.0 5.0 %collective-permute-start.18 = (bf16[224,256]{1,0:T(8,128)(2,1)S(1)}, bf16[224,256]{1,0:T(8,128)(2,1)S(1)}, u32[]{:S(2)}, u32[]{:S(2)}) collective-permute-start(bf16[224,256]{1,0:T(8,128)(2,1)S(1)} %get-tuple-element.36), channel_id=1, source_target_pairs={{0,288},{32,320},{64,352},{96,0},{128,32},{160,64},{192,96},{224,1... | collective-permute-start | bytes 344072 | tf_op jit(solution)/shard_map/ppermute | solution.py:169
  183.0 8.3 %collective-permute-start.19 = (bf16[224,256]{1,0:T(8,128)(2,1)S(1)}, bf16[224,256]{1,0:T(8,128)(2,1)S(1)}, u32[]{:S(2)}, u32[]{:S(2)}) collective-permute-start(bf16[224,256]{1,0:T(8,128)(2,1)S(1)} %get-tuple-element.37), channel_id=1, source_target_pairs={{0,192},{32,224},{64,256},{96,288},{128,320},{160,352},{192,0},{22... | collective-permute-start | bytes 344072 | tf_op jit(solution)/shard_map/ppermute | solution.py:169
  191.4 4.6 %collective-permute-done.19.r3 = bf16[224,256]{1,0:T(8,128)(2,1)S(1)} collective-permute-done((bf16[224,256]{1,0:T(8,128)(2,1)S(1)}, bf16[224,256]{1,0:T(8,128)(2,1)S(1)}, u32[]{:S(2)}, u32[]{:S(2)}) %collective-permute-start.19) | collective-permute-done | bytes 114720 | tf_op jit(solution)/shard_map/ppermute | solution.py:169
  196.6 6.7 %collective-permute-start.20 = (bf16[160,256]{1,0:T(8,128)(2,1)S(1)}, bf16[160,256]{1,0:T(8,128)(2,1)S(1)}, u32[]{:S(2)}, u32[]{:S(2)}) collective-permute-start(bf16[160,256]{1,0:T(8,128)(2,1)S(1)} %get-tuple-element.40), channel_id=1, source_target_pairs={{0,384},{384,0},{1,385},{385,1},{2,386},{386,2},{3,387},{387,3},{4... | collective-permute-start | bytes 245768 | tf_op jit(solution)/shard_map/ppermute | solution.py:169
  206.3 5.9 %collective-permute-start.22 = (f32[96,256]{1,0:T(8,128)S(1)}, f32[96,256]{1,0:T(8,128)S(1)}, u32[]{:S(2)}, u32[]{:S(2)}) collective-permute-start(f32[96,256]{1,0:T(8,128)S(1)} %get-tuple-element.42.own), channel_id=1, source_target_pairs={{0,352},{32,0},{64,32},{96,64},{128,96},{160,128},{192,160},{224,1... | collective-permute-start | bytes 294920 | tf_op jit(solution)/shard_map/ppermute | solution.py:169
  212.2 6.6 %collective-permute-start.21 = (f32[96,256]{1,0:T(8,128)S(1)}, f32[96,256]{1,0:T(8,128)S(1)}, u32[]{:S(2)}, u32[]{:S(2)}) collective-permute-start(f32[96,256]{1,0:T(8,128)S(1)} %get-tuple-element.42.own), channel_id=1, source_target_pairs={{0,32},{32,64},{64,96},{96,128},{128,160},{160,192},{192,224},{224... | collective-permute-start | bytes 294920 | tf_op jit(solution)/shard_map/ppermute | solution.py:169
  (73 shorter events, 46.4 us)
Async XLA Ops:
  7.2 146.1 %all-gather.2.cloned.1.call-start = ((), (), s32[]{:S(2)}) async-start(), calls=%async_computation.1 | async-start | bytes 1179648 | tf_op jit(solution)/shard_map/all_gather | solution.py:213
  11.2 58.0 %collective-permute-start.2 = (bf16[35,64,128]{2,1,0:T(8,128)(2,1)S(1)}, bf16[35,64,128]{2,1,0:T(8,128)(2,1)S(1)}, u32[]{:S(2)}, u32[]{:S(2)}) collective-permute-start(bf16[35,64,128]{2,1,0:T(8,128)(2,1)S(1)} %get-tuple-element.23), channel_id=1, source_target_pairs={{0,24},{8,0},{16,8},{24,16},{1,25},{9,1},{17,9},{25,17},{2,26},{10... | collective-permute-start | bytes 1720328 | tf_op jit(solution)/shard_map/ppermute | solution.py:169
  16.4 52.7 %collective-permute-start = (bf16[35,64,128]{2,1,0:T(8,128)(2,1)S(1)}, bf16[35,64,128]{2,1,0:T(8,128)(2,1)S(1)}, u32[]{:S(2)}, u32[]{:S(2)}) collective-permute-start(bf16[35,64,128]{2,1,0:T(8,128)(2,1)S(1)} %get-tuple-element.23), channel_id=1, source_target_pairs={{0,8},{8,16},{16,24},{24,0},{1,9},{9,17},{17,25},{25,1},{2,10},{10... | collective-permute-start | bytes 1720328 | tf_op jit(solution)/shard_map/ppermute | solution.py:169
  18.4 11.1 %collective-permute-start.3 = (bf16[64,256]{1,0:T(8,128)(2,1)S(1)}, bf16[64,256]{1,0:T(8,128)(2,1)S(1)}, u32[]{:S(2)}, u32[]{:S(2)}) collective-permute-start(bf16[64,256]{1,0:T(8,128)(2,1)S(1)} %bitcast.68), channel_id=1, source_target_pairs={{0,384},{384,0},{1,385},{385,1},{2,386},{386,2},{3,387},{387,3},{4... | collective-permute-start | bytes 98312 | tf_op jit(solution)/shard_map/ppermute | solution.py:169
  25.8 43.4 %collective-permute-start.1 = (bf16[35,64,128]{2,1,0:T(8,128)(2,1)S(1)}, bf16[35,64,128]{2,1,0:T(8,128)(2,1)S(1)}, u32[]{:S(2)}, u32[]{:S(2)}) collective-permute-start(bf16[35,64,128]{2,1,0:T(8,128)(2,1)S(1)} %get-tuple-element.24.s0), channel_id=1, source_target_pairs={{0,16},{8,24},{16,0},{24,8},{1,17},{9,25},{17,1},{25,9},{2,18},{10... | collective-permute-start | bytes 1720328 | tf_op jit(solution)/shard_map/ppermute | solution.py:169
  29.5 30.8 %collective-permute-start.6 = (bf16[128,256]{1,0:T(8,128)(2,1)S(1)}, bf16[128,256]{1,0:T(8,128)(2,1)S(1)}, u32[]{:S(2)}, u32[]{:S(2)}) collective-permute-start(bf16[128,256]{1,0:T(8,128)(2,1)S(1)} %pad_maximum_fusion.1), channel_id=1, source_target_pairs={{0,192},{32,224},{64,256},{96,288},{128,320},{160,352},{192,0},{22... | collective-permute-start | bytes 196616 | tf_op jit(solution)/shard_map/ppermute | solution.py:169
  44.4 9.1 %collective-permute-start.4 = (bf16[128,256]{1,0:T(8,128)(2,1)S(1)}, bf16[128,256]{1,0:T(8,128)(2,1)S(1)}, u32[]{:S(2)}, u32[]{:S(2)}) collective-permute-start(bf16[128,256]{1,0:T(8,128)(2,1)S(1)} %pad_maximum_fusion.1), channel_id=1, source_target_pairs={{0,96},{32,128},{64,160},{96,192},{128,224},{160,256},{192,288},{2... | collective-permute-start | bytes 196616 | tf_op jit(solution)/shard_map/ppermute | solution.py:169
  53.5 6.8 %collective-permute-start.5 = (bf16[128,256]{1,0:T(8,128)(2,1)S(1)}, bf16[128,256]{1,0:T(8,128)(2,1)S(1)}, u32[]{:S(2)}, u32[]{:S(2)}) collective-permute-start(bf16[128,256]{1,0:T(8,128)(2,1)S(1)} %pad_maximum_fusion.1), channel_id=1, source_target_pairs={{0,288},{32,320},{64,352},{96,0},{128,32},{160,64},{192,96},{224,1... | collective-permute-start | bytes 196616 | tf_op jit(solution)/shard_map/ppermute | solution.py:169
  60.3 11.5 %collective-permute-start.8 = (bf16[512,256]{1,0:T(8,128)(2,1)S(1)}, bf16[512,256]{1,0:T(8,128)(2,1)S(1)}, u32[]{:S(2)}, u32[]{:S(2)}) collective-permute-start(bf16[512,256]{1,0:T(8,128)(2,1)S(1)} %constant_dynamic-update-slice_fusion.f0), channel_id=1, source_target_pairs={{0,352},{32,0},{64,32},{96,64},{128,96},{160,128},{192,160},{224,1... | collective-permute-start | bytes 786440 | tf_op jit(solution)/shard_map/ppermute | solution.py:169
  67.2 9.7 %collective-permute-start.7 = (bf16[512,256]{1,0:T(8,128)(2,1)S(1)}, bf16[512,256]{1,0:T(8,128)(2,1)S(1)}, u32[]{:S(2)}, u32[]{:S(2)}) collective-permute-start(bf16[512,256]{1,0:T(8,128)(2,1)S(1)} %constant_dynamic-update-slice_fusion.f0), channel_id=1, source_target_pairs={{0,32},{32,64},{64,96},{96,128},{128,160},{160,192},{192,224},{224... | collective-permute-start | bytes 786440 | tf_op jit(solution)/shard_map/ppermute | solution.py:169
  83.4 9.6 %collective-permute-start.9 = (bf16[512,256]{1,0:T(8,128)(2,1)S(1)}, bf16[512,256]{1,0:T(8,128)(2,1)S(1)}, u32[]{:S(2)}, u32[]{:S(2)}) collective-permute-start(bf16[512,256]{1,0:T(8,128)(2,1)S(1)} %get-tuple-element.26), channel_id=1, source_target_pairs={{0,24},{8,0},{16,8},{24,16},{1,25},{9,1},{17,9},{25,17},{2,26},{10... | collective-permute-start | bytes 786440 | tf_op jit(solution)/shard_map/ppermute | solution.py:169
  86.8 8.6 %collective-permute-start.10 = (bf16[512,256]{1,0:T(8,128)(2,1)S(1)}, bf16[512,256]{1,0:T(8,128)(2,1)S(1)}, u32[]{:S(2)}, u32[]{:S(2)}) collective-permute-start(bf16[512,256]{1,0:T(8,128)(2,1)S(1)} %get-tuple-element.27), channel_id=1, source_target_pairs={{0,16},{8,24},{16,0},{24,8},{1,17},{9,25},{17,1},{25,9},{2,18},{10... | collective-permute-start | bytes 786440 | tf_op jit(solution)/shard_map/ppermute | solution.py:169
  91.1 11.6 %collective-permute-start.11 = (bf16[512,256]{1,0:T(8,128)(2,1)S(1)}, bf16[512,256]{1,0:T(8,128)(2,1)S(1)}, u32[]{:S(2)}, u32[]{:S(2)}) collective-permute-start(bf16[512,256]{1,0:T(8,128)(2,1)S(1)} %get-tuple-element.28), channel_id=1, source_target_pairs={{0,8},{8,16},{16,24},{24,0},{1,9},{9,17},{17,25},{25,1},{2,10},{10... | collective-permute-start | bytes 786440 | tf_op jit(solution)/shard_map/ppermute | solution.py:169
  134.0 9.6 %collective-permute-start.14 = (bf16[512,256]{1,0:T(8,128)(2,1)S(1)}, bf16[512,256]{1,0:T(8,128)(2,1)S(1)}, u32[]{:S(2)}, u32[]{:S(2)}) collective-permute-start(bf16[512,256]{1,0:T(8,128)(2,1)S(1)} %all_gather.6.a0), channel_id=1, source_target_pairs={{0,24},{8,0},{16,8},{24,16},{1,25},{9,1},{17,9},{25,17},{2,26},{10... | collective-permute-start | bytes 786440 | tf_op jit(solution)/shard_map/ppermute | solution.py:169
  136.1 10.8 %collective-permute-start.13 = (bf16[512,256]{1,0:T(8,128)(2,1)S(1)}, bf16[512,256]{1,0:T(8,128)(2,1)S(1)}, u32[]{:S(2)}, u32[]{:S(2)}) collective-permute-start(bf16[512,256]{1,0:T(8,128)(2,1)S(1)} %all_gather.6.a0), channel_id=1, source_target_pairs={{0,16},{8,24},{16,0},{24,8},{1,17},{9,25},{17,1},{25,9},{2,18},{10... | collective-permute-start | bytes 786440 | tf_op jit(solution)/shard_map/ppermute | solution.py:169
  140.5 12.8 %collective-permute-start.12 = (bf16[512,256]{1,0:T(8,128)(2,1)S(1)}, bf16[512,256]{1,0:T(8,128)(2,1)S(1)}, u32[]{:S(2)}, u32[]{:S(2)}) collective-permute-start(bf16[512,256]{1,0:T(8,128)(2,1)S(1)} %all_gather.6.a0), channel_id=1, source_target_pairs={{0,8},{8,16},{16,24},{24,0},{1,9},{9,17},{17,25},{25,1},{2,10},{10... | collective-permute-start | bytes 786440 | tf_op jit(solution)/shard_map/ppermute | solution.py:169
  161.3 10.3 %collective-permute-start.15 = (bf16[608,256]{1,0:T(8,128)(2,1)S(1)}, bf16[608,256]{1,0:T(8,128)(2,1)S(1)}, u32[]{:S(2)}, u32[]{:S(2)}) collective-permute-start(bf16[608,256]{1,0:T(8,128)(2,1)S(1)} %get-tuple-element.31), channel_id=1, source_target_pairs={{0,32},{32,64},{64,96},{96,128},{128,160},{160,192},{192,224},{224... | collective-permute-start | bytes 933896 | tf_op jit(solution)/shard_map/ppermute | solution.py:169
  163.2 9.3 %collective-permute-start.16 = (bf16[608,256]{1,0:T(8,128)(2,1)S(1)}, bf16[608,256]{1,0:T(8,128)(2,1)S(1)}, u32[]{:S(2)}, u32[]{:S(2)}) collective-permute-start(bf16[608,256]{1,0:T(8,128)(2,1)S(1)} %get-tuple-element.32), channel_id=1, source_target_pairs={{0,352},{32,0},{64,32},{96,64},{128,96},{160,128},{192,160},{224,1... | collective-permute-start | bytes 933896 | tf_op jit(solution)/shard_map/ppermute | solution.py:169
  172.7 18.7 %collective-permute-start.17 = (bf16[224,256]{1,0:T(8,128)(2,1)S(1)}, bf16[224,256]{1,0:T(8,128)(2,1)S(1)}, u32[]{:S(2)}, u32[]{:S(2)}) collective-permute-start(bf16[224,256]{1,0:T(8,128)(2,1)S(1)} %get-tuple-element.35), channel_id=1, source_target_pairs={{0,96},{32,128},{64,160},{96,192},{128,224},{160,256},{192,288},{2... | collective-permute-start | bytes 344072 | tf_op jit(solution)/shard_map/ppermute | solution.py:169
  178.0 13.4 %collective-permute-start.18 = (bf16[224,256]{1,0:T(8,128)(2,1)S(1)}, bf16[224,256]{1,0:T(8,128)(2,1)S(1)}, u32[]{:S(2)}, u32[]{:S(2)}) collective-permute-start(bf16[224,256]{1,0:T(8,128)(2,1)S(1)} %get-tuple-element.36), channel_id=1, source_target_pairs={{0,288},{32,320},{64,352},{96,0},{128,32},{160,64},{192,96},{224,1... | collective-permute-start | bytes 344072 | tf_op jit(solution)/shard_map/ppermute | solution.py:169
  183.0 13.0 %collective-permute-start.19 = (bf16[224,256]{1,0:T(8,128)(2,1)S(1)}, bf16[224,256]{1,0:T(8,128)(2,1)S(1)}, u32[]{:S(2)}, u32[]{:S(2)}) collective-permute-start(bf16[224,256]{1,0:T(8,128)(2,1)S(1)} %get-tuple-element.37), channel_id=1, source_target_pairs={{0,192},{32,224},{64,256},{96,288},{128,320},{160,352},{192,0},{22... | collective-permute-start | bytes 344072 | tf_op jit(solution)/shard_map/ppermute | solution.py:169
  196.6 9.1 %collective-permute-start.20 = (bf16[160,256]{1,0:T(8,128)(2,1)S(1)}, bf16[160,256]{1,0:T(8,128)(2,1)S(1)}, u32[]{:S(2)}, u32[]{:S(2)}) collective-permute-start(bf16[160,256]{1,0:T(8,128)(2,1)S(1)} %get-tuple-element.40), channel_id=1, source_target_pairs={{0,384},{384,0},{1,385},{385,1},{2,386},{386,2},{3,387},{387,3},{4... | collective-permute-start | bytes 245768 | tf_op jit(solution)/shard_map/ppermute | solution.py:169
  206.3 12.5 %collective-permute-start.22 = (f32[96,256]{1,0:T(8,128)S(1)}, f32[96,256]{1,0:T(8,128)S(1)}, u32[]{:S(2)}, u32[]{:S(2)}) collective-permute-start(f32[96,256]{1,0:T(8,128)S(1)} %get-tuple-element.42.own), channel_id=1, source_target_pairs={{0,352},{32,0},{64,32},{96,64},{128,96},{160,128},{192,160},{224,1... | collective-permute-start | bytes 294920 | tf_op jit(solution)/shard_map/ppermute | solution.py:169
  212.2 8.2 %collective-permute-start.21 = (f32[96,256]{1,0:T(8,128)S(1)}, f32[96,256]{1,0:T(8,128)S(1)}, u32[]{:S(2)}, u32[]{:S(2)}) collective-permute-start(f32[96,256]{1,0:T(8,128)S(1)} %get-tuple-element.42.own), channel_id=1, source_target_pairs={{0,32},{32,64},{64,96},{96,128},{128,160},{160,192},{192,224},{224... | collective-permute-start | bytes 294920 | tf_op jit(solution)/shard_map/ppermute | solution.py:169
  (8 other events, 55.1 us)
Sparse Core Ops, SparseCore 0:
  70.1 39.9 all-gather.1

commit v3 on v1

v3 whole, which is shorter than its diff:
```python
import functools

import jax
import jax.numpy as jnp
from jax import lax
from jax.experimental import pallas as pl
from jax.experimental.pallas import tpu as pltpu
from jax.sharding import Mesh
from jax.sharding import PartitionSpec as P

BF = jnp.bfloat16
F32 = jnp.float32
TILE = 128
STRIP = 64
SPLIT = (2, 4, 3, 4, 4, 2)
NAMES = ("yh", "za", "zb", "x", "yl", "core")
ROW = ("yh", "za", "zb", "x")
Z = ("za", "zb")
STEP = 4
COL = ("yl", "core")
VMEM_LIMIT = 40 * 1024 * 1024


def spec(space):
    return pl.BlockSpec(memory_space=space)


def pack_kernel(info, tiles, cot, meta, same, other):
    slots = tiles.shape[0]
    odd = info[0] == 1

    def one(s, carry):
        turned = tiles[s].T
        low, high = turned[:STRIP], turned[STRIP:]
        same[s] = jnp.where(odd, high, low)
        other[s] = jnp.where(odd, low, high)
        return carry

    lax.fori_loop(0, slots, one, 0, unroll=4)
    for ref in (same, other):
        ref[slots] = cot[:, :TILE]
        ref[slots + 1] = cot[:, TILE:]
        ref[slots + 2] = jnp.broadcast_to(meta[...], (STRIP, TILE)).astype(BF)


def live_list(codes, mine, place_of, table, strips, pool):
    slots = codes.shape[1]
    for j, ref in enumerate(strips):
        pool[j * slots : (j + 1) * slots] = ref[:slots]
    pool[4 * slots] = jnp.zeros((STRIP, TILE), BF)
    count = jnp.int32(0)
    for j in range(4):

        def one(s, n, j=j):
            code = codes[j, s]
            col, row = code >> 2, code & 3
            table[0, n] = j * slots + s
            table[1, n] = j * 4 + row
            table[2, n] = place_of(col >> 1)
            return n + ((code >= 0) & ((col & 1) == mine)).astype(jnp.int32)

        count = lax.fori_loop(0, slots, one, count, unroll=4)
    for i in range(STEP):
        table[0, count + i] = 4 * slots
        table[1, count + i] = 0
        table[2, count + i] = 0
    return count


def fwd_kernel(nz, codes, info, s0, s1, s2, s3, feats, o0, o1, o2, o3, table, pool, acc):
    rows = o0.shape[0]
    mine, my_yh = info[1], info[2]

    def place_of(q):
        far = (q >= nz).astype(jnp.int32)
        return (q - far * nz) * 2 + (far ^ my_yh)

    count = live_list(codes, mine, place_of, table, (s0, s1, s2, s3), pool)
    acc[...] = jnp.zeros_like(acc)

    def several(t, carry):
        terms = []
        for i in range(STEP):
            at = t * STEP + i
            block = feats[pl.ds(pl.multiple_of(table[2, at] * STRIP, STRIP), STRIP), :]
            term = lax.dot_general(
                pool[table[0, at]], block, (((0,), (0,)), ((), ())), preferred_element_type=F32
            )
            terms.append((pl.ds(pl.multiple_of(table[1, at] * TILE, TILE), TILE), term))
        for at, term in terms:
            acc[at, :] = acc[at, :] + term
        return carry

    lax.fori_loop(0, (count + (STEP - 1)) // STEP, several, 0)
    per = 4 * TILE
    for j, ref in enumerate((o0, o1, o2, o3)):
        ref[...] = acc[j * per : j * per + rows, :].astype(ref.dtype)


def bwd_kernel(
    nz, codes, info, s0, s1, s2, s3, a0, a1, a2, a3, cot, w, out, keep, up, down, table, pool, ga, acc, gw4, act
):
    rows, feat = a0.shape
    mine, col_pos, my_zb, my_x = info[1], info[3], info[4], info[5]
    share = feat // cot.shape[0]
    count = live_list(codes, mine, lambda q: q, table, (s0, s1, s2, s3), pool)
    acc[...] = jnp.zeros_like(acc)
    per = 4 * TILE
    for j, agg in enumerate((a0, a1, a2, a3)):
        pre = jnp.dot(agg[...], w[...], preferred_element_type=F32)
        sig = jax.nn.sigmoid(pre)
        if j == 0:
            act[...] = pre * sig
        slope = sig * (1.0 + pre * (1.0 - sig))
        cot_j = cot[:, j].reshape(rows, feat).astype(F32)
        gp = (cot_j * slope).astype(BF)
        gw4[(my_x - j) & 3] = lax.dot_general(agg[...], gp, (((0,), (0,)), ((), ())), preferred_element_type=F32)
        ga[j * per : j * per + rows, :] = lax.dot_general(
            gp, w[...], (((1,), (1,)), ((), ())), preferred_element_type=F32
        ).astype(BF)
    out[...] = act[pl.ds(pl.multiple_of(col_pos * STRIP, STRIP), STRIP), :].astype(BF)

    def several(t, carry):
        terms = []
        for i in range(STEP):
            at = t * STEP + i
            block = ga[pl.ds(pl.multiple_of(table[1, at] * TILE, TILE), TILE), :]
            term = jnp.dot(pool[table[0, at]], block, preferred_element_type=F32)
            terms.append((pl.ds(pl.multiple_of(table[2, at] * STRIP, STRIP), STRIP), term))
        for at, term in terms:
            acc[at, :] = acc[at, :] + term
        return carry

    lax.fori_loop(0, (count + (STEP - 1)) // STEP, several, 0)
    mine_rows = pl.ds(pl.multiple_of(col_pos * share, share), share)
    part = (gw4[0, mine_rows, :] + gw4[1, mine_rows, :]) + (gw4[2, mine_rows, :] + gw4[3, mine_rows, :])
    high = part.astype(BF)
    low = (part - high.astype(F32)).astype(BF)
    n_chunks = acc.shape[0] // (3 * STRIP)
    n_za = nz // 3
    for base, ref in ((0, keep), (1, up), (2, down)):
        which = lax.rem(my_zb + base, 3)
        for i in range(n_chunks):
            q = (i // n_za) * nz + 3 * (i % n_za) + which
            block = acc[pl.ds(pl.multiple_of(q * STRIP, STRIP), STRIP), :]
            ref[i * STRIP : (i + 1) * STRIP, :] = block.astype(ref.dtype)
    end = n_chunks * STRIP
    keep[end:, :] = part
    for ref in (up, down):
        ref[end : end + share, :] = high
        ref[end + share :, :] = low


def near_kernel(keep, up, down, chunks):
    n_chunks = chunks.shape[0]
    end = n_chunks * STRIP
    share = keep.shape[0] - end
    for i in range(n_chunks):
        at = slice(i * STRIP, (i + 1) * STRIP)
        chunks[i, :STRIP, :] = (keep[at, :] + (up[at, :].astype(F32) + down[at, :].astype(F32))).astype(BF)
    part = keep[end:, :]
    for ref in (up, down):
        part = part + (ref[end : end + share, :].astype(F32) + ref[end + share :, :].astype(F32))
    high = part.astype(BF)
    low = (part - high.astype(F32)).astype(BF)
    for i in range(n_chunks):
        chunks[i, STRIP : STRIP + share, :] = high
        chunks[i, STRIP + share :, :] = low


def far_kernel(scale, chunks, grads, weight_part):
    share = weight_part.shape[0]
    total = jnp.sum(chunks[...].astype(F32), axis=0)
    grads[...] = total[:STRIP].astype(BF)
    weight_part[...] = (total[STRIP : STRIP + share] + total[STRIP + share :]) * scale


def shift(value, axis, by):
    n = lax.axis_size(axis)
    return lax.ppermute(value, axis, [(i, (i + by) % n) for i in range(n)])


def on_device(features, weight, cotangent, tile_values, tile_rows, tile_cols, tile_count):
    own = features[0]
    per_dev, feat = own.shape
    slots = tile_values.shape[2]
    nz = lax.axis_size(Z)
    groups = 2 * nz
    n_chunks = groups // 3
    col_devs = lax.axis_size(COL)
    rows = per_dev * col_devs
    x = lax.axis_index("x")
    info = jnp.stack([x % 2, x // 2, lax.axis_index("yh"), lax.axis_index(COL), lax.axis_index("zb"), x]).astype(jnp.int32)
    params = pltpu.CompilerParams(vmem_limit_bytes=VMEM_LIMIT)
    vmem, smem = spec(pltpu.VMEM), spec(pltpu.SMEM)

    def call(kernel, name, ins, outs, scratch, *args):
        return pl.pallas_call(
            kernel,
            out_shape=tuple(jax.ShapeDtypeStruct(s, t) for s, t in outs),
            in_specs=ins,
            out_specs=(vmem,) * len(outs),
            scratch_shapes=scratch,
            compiler_params=params,
            name=name,
        )(*args)

    live = jnp.arange(slots, dtype=jnp.int32) < tile_count[0, 0]
    code = jnp.where(live, tile_rows[0, 0] + 4 * tile_cols[0, 0], -1)
    meta = jnp.pad(code.astype(F32), (0, TILE - slots))[None]

    near = jnp.concatenate([own, shift(own, "yh", 1)], axis=0)
    column = lax.all_gather(near, Z, axis=0, tiled=True)

    parcel = ((slots + 3, STRIP, TILE), BF)
    same, other = call(
        pack_kernel, "pack", [smem, vmem, vmem, vmem], [parcel] * 2, [], info, tile_values[0, 0], cotangent[0], meta
    )
    strips = [same] + [shift(same if d == 2 else other, "x", d) for d in (1, 2, 3)]
    codes = jnp.stack([code] + [s[slots + 2, 0, :slots].astype(jnp.int32) for s in strips[1:]])
    cots = jnp.stack([jnp.concatenate([s[slots], s[slots + 1]], axis=1) for s in strips])
    cot_all = lax.all_gather(cots.reshape(4 * STRIP, feat), COL, axis=0, tiled=True)
    cot_all = cot_all.reshape(col_devs, 4, STRIP, feat)

    listing = [pltpu.SMEM((3, 4 * slots + STEP), jnp.int32), pltpu.VMEM((4 * slots + 1, STRIP, TILE), BF)]
    parts = call(
        functools.partial(fwd_kernel, nz),
        "forward_tiles",
        [smem, smem] + [vmem] * 5,
        [((rows, feat), F32)] + [((rows, feat), BF)] * 3,
        listing + [pltpu.VMEM((16 * TILE, feat), F32)],
        codes, info, *strips, column,
    )

    back = [shift(parts[d], "x", -d) for d in (1, 2, 3)]
    block_sum = (parts[0] + (back[0].astype(F32) + back[1].astype(F32) + back[2].astype(F32))).astype(BF)
    pieces = lax.all_to_all(block_sum, COL, split_axis=0, concat_axis=0, tiled=True)
    agg = jnp.sum(pieces.reshape(col_devs, per_dev, feat).astype(F32), axis=0).astype(BF)
    block_agg = lax.all_gather(agg, COL, axis=0, tiled=True)
    aggs = [block_agg] + [shift(block_agg, "x", d) for d in (1, 2, 3)]

    share = feat // col_devs
    chunk_rows = n_chunks * STRIP
    output_rows, keep, up, down = call(
        functools.partial(bwd_kernel, nz),
        "backward_tiles",
        [smem, smem] + [vmem] * 10,
        [((per_dev, feat), BF), ((chunk_rows + share, feat), F32)] + [((chunk_rows + 2 * share, feat), BF)] * 2,
        listing
        + [
            pltpu.VMEM((16 * TILE, feat), BF),
            pltpu.VMEM((groups * STRIP, feat), F32),
            pltpu.VMEM((4, feat, feat), F32),
            pltpu.VMEM((rows, feat), F32),
        ],
        codes, info, *strips, *aggs, cot_all, weight,
    )
    (chunks,) = call(
        near_kernel,
        "near_sum",
        [vmem] * 3,
        [((n_chunks, STRIP + 2 * share, feat), BF)],
        [],
        keep, shift(up, Z, 1), shift(down, Z, -1),
    )
    arrived = lax.all_to_all(chunks, ("yh", "za"), split_axis=0, concat_axis=0, tiled=True)
    node_total = per_dev * lax.axis_size(ROW) * col_devs
    grads, weight_part = call(
        functools.partial(far_kernel, node_total ** (-0.5)),
        "far_sum",
        [vmem],
        [((per_dev, feat), BF), ((share, feat), F32)],
        [],
        arrived,
    )
    grad_weight = lax.all_gather(weight_part, COL, axis=0, tiled=True)
    return output_rows[None], grads[None], grad_weight


def build(mesh, split):
    grid = Mesh(mesh.devices.reshape(split), NAMES)
    return jax.shard_map(
        on_device,
        mesh=grid,
        in_specs=(
            P(COL, ROW, None),
            P(),
            P(ROW, COL, None),
            P(ROW, COL, None, None, None),
            P(ROW, COL, None),
            P(ROW, COL, None),
            P(ROW, COL),
        ),
        out_specs=(P(ROW, COL, None), P(COL, ROW, None), P()),
        check_vma=False,
    )


def solution(mesh):
    return build(mesh, SPLIT)
```

time: 234 us -> 218 us (0.932)
  the two profiles are of different devices: /device:TPU:1 before, /device:TPU:65 now
where the time goes in v3:
time: 218 us; the launch traced here: 217 us
  blocking collectives  122 us (56%)
  starting transfers between devices  38.6 us (18%)
  waiting for transfers between devices  25 us (11%)
  between operations  15 us (7%)
  Pallas kernels  11.9 us (5%)
  local copies, waits for them, and re-layouts  3.94 us (2%)
    ppermute x12, starting transfers between devices, shift(): return lax.ppermute(value, axis, [(i, (i + by) % n) for i in range(n)])  38.6 us
    all_to_all x1, blocking collectives, on_device(): lax.all_to_all(chunks, ('yh', 'za'), split_axis=0, concat_axis=0, tiled=T...  38.5 us
    all_gather x1, blocking collectives, on_device(): column = lax.all_gather(near, Z, axis=0, tiled=True)  29.9 us
    ppermute x12, waiting for transfers between devices, shift(): return lax.ppermute(value, axis, [(i, (i + by) % n) for i in range(n)])  25 us
    all_to_all x1, blocking collectives, on_device(): lax.all_to_all(block_sum, COL, split_axis=0, concat_axis=0, tiled=True)  23.3 us
    all_gather x1, blocking collectives, on_device(): grad_weight = lax.all_gather(weight_part, COL, axis=0, tiled=True)  15.4 us
    all_gather x1, blocking collectives, on_device(): block_agg = lax.all_gather(agg, COL, axis=0, tiled=True)  14.9 us
    pallas_call x5, Pallas kernels, call(): pl.pallas_call(kernel, out_shape=tuple((jax.ShapeDtypeStruct(s, t) for s,...  11.9 us
  transfers between devices with their start and end apart: 13, of which 7 were waited for; matrix products, arithmetic and copies ran while one was open for 0% of the time, Pallas kernels for 2%

profile of v3, /device:TPU:65, one launch (start us, length us, event | category | flops | bytes accessed | tf_op | source)
XLA Modules:
  0.0 217.3 jit_solution(14820171368753788923)
XLA Ops:
  11.2 4.4 %collective-permute-start.2 = (bf16[35,64,128]{2,1,0:T(8,128)(2,1)S(1)}, bf16[35,64,128]{2,1,0:T(8,128)(2,1)S(1)}, u32[]{:S(2)}, u32[]{:S(2)}) collective-permute-start(bf16[35,64,128]{2,1,0:T(8,128)(2,1)S(1)} %get-tuple-element.15), channel_id=1, source_target_pairs={{0,24},{8,0},{16,8},{24,16},{1,25},{9,1},{17,9},{25,17},{2,26},{10... | collective-permute-start | bytes 1720328 | tf_op jit(solution)/shard_map/ppermute | solution.py:180
  15.6 1.9 collective-permute-start
  17.5 7.5 %collective-permute-start.3 = (bf16[64,256]{1,0:T(8,128)(2,1)S(1)}, bf16[64,256]{1,0:T(8,128)(2,1)S(1)}, u32[]{:S(2)}, u32[]{:S(2)}) collective-permute-start(bf16[64,256]{1,0:T(8,128)(2,1)S(1)} %bitcast.67), channel_id=1, source_target_pairs={{0,384},{384,0},{1,385},{385,1},{2,386},{386,2},{3,387},{387,3},{4... | collective-permute-start | bytes 98312 | tf_op jit(solution)/shard_map/ppermute | solution.py:180
  25.0 3.6 %collective-permute-start.1 = (bf16[35,64,128]{2,1,0:T(8,128)(2,1)S(1)}, bf16[35,64,128]{2,1,0:T(8,128)(2,1)S(1)}, u32[]{:S(2)}, u32[]{:S(2)}) collective-permute-start(bf16[35,64,128]{2,1,0:T(8,128)(2,1)S(1)} %get-tuple-element.16.s0), channel_id=1, source_target_pairs={{0,16},{8,24},{16,0},{24,8},{1,17},{9,25},{17,1},{25,9},{2,18},{10... | collective-permute-start | bytes 1720328 | tf_op jit(solution)/shard_map/ppermute | solution.py:180
  28.7 29.9 %all_gather.12.feats = bf16[1536,256]{1,0:T(8,128)(2,1)S(1)} all-gather(bf16[128,256]{1,0:T(8,128)(2,1)S(1)} %pad_maximum_fusion.1), channel_id=1, replica_groups=mesh['yh'=2,'za'=4,'zb'=3,'x'=4,'yl'=4,'core'=2] {'za','zb'}, dimensions={0}, use_global_device_ids=true | all-gather | bytes 851968 | tf_op jit(solution)/shard_map/all_gather | solution.py:213
  59.4 4.4 %forward_tiles.1 = (f32[512,256]{1,0:T(8,128)S(1)}, bf16[512,256]{1,0:T(8,128)(2,1)S(1)}, bf16[512,256]{1,0:T(8,128)(2,1)S(1)}, bf16[512,256]{1,0:T(8,128)(2,1)S(1)}) custom-call(s32[4,32]{1,0:T(4,128)S(1)} %pad_add_fusion.codes, s32[6]{0:T(128)S(1)} %stack.49.info, bf16[35,64,128]{2,1,0:T(8,128)(2,1)S(1)} %get-tuple-element.16.s0, ...), custom_call_target="tpu_custom_call" | custom-call | tf_op jit(solution)/shard_map/forward_tiles/pallas_call | solution.py:198
  63.8 2.2 %collective-permute-start.4 = (bf16[512,256]{1,0:T(8,128)(2,1)S(1)}, bf16[512,256]{1,0:T(8,128)(2,1)S(1)}, u32[]{:S(2)}, u32[]{:S(2)}) collective-permute-start(bf16[512,256]{1,0:T(8,128)(2,1)S(1)} %get-tuple-element.18), channel_id=1, source_target_pairs={{0,24},{8,0},{16,8},{24,16},{1,25},{9,1},{17,9},{25,17},{2,26},{10... | collective-permute-start | bytes 786440 | tf_op jit(solution)/shard_map/ppermute | solution.py:180
  66.0 3.6 %collective-permute-start.5 = (bf16[512,256]{1,0:T(8,128)(2,1)S(1)}, bf16[512,256]{1,0:T(8,128)(2,1)S(1)}, u32[]{:S(2)}, u32[]{:S(2)}) collective-permute-start(bf16[512,256]{1,0:T(8,128)(2,1)S(1)} %get-tuple-element.19), channel_id=1, source_target_pairs={{0,16},{8,24},{16,0},{24,8},{1,17},{9,25},{17,1},{25,9},{2,18},{10... | collective-permute-start | bytes 786440 | tf_op jit(solution)/shard_map/ppermute | solution.py:180
  69.6 1.9 collective-permute-start.6
  71.6 3.0 %collective-permute-done.5 = bf16[512,256]{1,0:T(8,128)(2,1)S(1)} collective-permute-done((bf16[512,256]{1,0:T(8,128)(2,1)S(1)}, bf16[512,256]{1,0:T(8,128)(2,1)S(1)}, u32[]{:S(2)}, u32[]{:S(2)}) %collective-permute-start.5) | collective-permute-done | bytes 262176 | tf_op jit(solution)/shard_map/ppermute | solution.py:180
  74.6 3.3 %collective-permute-done.6 = bf16[512,256]{1,0:T(8,128)(2,1)S(1)} collective-permute-done((bf16[512,256]{1,0:T(8,128)(2,1)S(1)}, bf16[512,256]{1,0:T(8,128)(2,1)S(1)}, u32[]{:S(2)}, u32[]{:S(2)}) %collective-permute-start.6) | collective-permute-done | bytes 262176 | tf_op jit(solution)/shard_map/ppermute | solution.py:180
  78.1 23.3 %all_to_all.14 = bf16[8,64,256]{2,1,0:T(8,128)(2,1)S(1)} all-to-all(bf16[8,64,256]{2,1,0:T(8,128)(2,1)S(1)} %bitcast.65), channel_id=1, replica_groups=mesh['yh'=2,'za'=4,'zb'=3,'x'=4,'yl'=4,'core'=2] {'yl','core'}, dimensions={0} | all-to-all | bytes 524288 | tf_op jit(solution)/shard_map/all_to_all | solution.py:237
  101.5 14.9 %all_gather.13.a0 = bf16[512,256]{1,0:T(8,128)(2,1)S(1)} all-gather(bf16[64,256]{1,0:T(8,128)(2,1)S(1)} %reduce_sum.12), channel_id=1, replica_groups=mesh['yh'=2,'za'=4,'zb'=3,'x'=4,'yl'=4,'core'=2] {'yl','core'}, dimensions={0}, use_global_device_ids=true | all-gather | bytes 294912 | tf_op jit(solution)/shard_map/all_gather | solution.py:239
  118.3 2.4 %collective-permute-start.8 = (bf16[512,256]{1,0:T(8,128)(2,1)S(1)}, bf16[512,256]{1,0:T(8,128)(2,1)S(1)}, u32[]{:S(2)}, u32[]{:S(2)}) collective-permute-start(bf16[512,256]{1,0:T(8,128)(2,1)S(1)} %all_gather.13.a0), channel_id=1, source_target_pairs={{0,16},{8,24},{16,0},{24,8},{1,17},{9,25},{17,1},{25,9},{2,18},{10... | collective-permute-start | bytes 786440 | tf_op jit(solution)/shard_map/ppermute | solution.py:180
  120.7 2.9 %collective-permute-start.7 = (bf16[512,256]{1,0:T(8,128)(2,1)S(1)}, bf16[512,256]{1,0:T(8,128)(2,1)S(1)}, u32[]{:S(2)}, u32[]{:S(2)}) collective-permute-start(bf16[512,256]{1,0:T(8,128)(2,1)S(1)} %all_gather.13.a0), channel_id=1, source_target_pairs={{0,8},{8,16},{16,24},{24,0},{1,9},{9,17},{17,25},{25,1},{2,10},{10... | collective-permute-start | bytes 786440 | tf_op jit(solution)/shard_map/ppermute | solution.py:180
  123.6 2.4 %collective-permute-done.9.a3 = bf16[512,256]{1,0:T(8,128)(2,1)S(1)} collective-permute-done((bf16[512,256]{1,0:T(8,128)(2,1)S(1)}, bf16[512,256]{1,0:T(8,128)(2,1)S(1)}, u32[]{:S(2)}, u32[]{:S(2)}) %collective-permute-start.9) | collective-permute-done | bytes 262176 | tf_op jit(solution)/shard_map/ppermute | solution.py:180
  126.0 3.2 %collective-permute-done.8.a2 = bf16[512,256]{1,0:T(8,128)(2,1)S(1)} collective-permute-done((bf16[512,256]{1,0:T(8,128)(2,1)S(1)}, bf16[512,256]{1,0:T(8,128)(2,1)S(1)}, u32[]{:S(2)}, u32[]{:S(2)}) %collective-permute-start.8) | collective-permute-done | bytes 262176 | tf_op jit(solution)/shard_map/ppermute | solution.py:180
  129.2 6.4 %collective-permute-done.7.a1 = bf16[512,256]{1,0:T(8,128)(2,1)S(1)} collective-permute-done((bf16[512,256]{1,0:T(8,128)(2,1)S(1)}, bf16[512,256]{1,0:T(8,128)(2,1)S(1)}, u32[]{:S(2)}, u32[]{:S(2)}) %collective-permute-start.7) | collective-permute-done | bytes 262176 | tf_op jit(solution)/shard_map/ppermute | solution.py:180
  136.7 5.5 %backward_tiles.1 = (bf16[64,256]{1,0:T(8,128)(2,1)}, f32[544,256]{1,0:T(8,128)S(1)}, bf16[576,256]{1,0:T(8,128)(2,1)S(1)}, bf16[576,256]{1,0:T(8,128)(2,1)S(1)}) custom-call(s32[4,32]{1,0:T(4,128)S(1)} %pad_add_fusion.codes, s32[6]{0:T(128)S(1)} %stack.49.info, bf16[35,64,128]{2,1,0:T(8,128)(2,1)S(1)} %get-tuple-element.16.s0, ...), custom_call_target="tpu_custom_call" | custom-call | tf_op jit(solution)/shard_map/backward_tiles/pallas_call | solution.py:198
  142.2 2.8 %collective-permute-start.10 = (bf16[576,256]{1,0:T(8,128)(2,1)S(1)}, bf16[576,256]{1,0:T(8,128)(2,1)S(1)}, u32[]{:S(2)}, u32[]{:S(2)}) collective-permute-start(bf16[576,256]{1,0:T(8,128)(2,1)S(1)} %get-tuple-element.23), channel_id=1, source_target_pairs={{0,32},{32,64},{64,96},{96,128},{128,160},{160,192},{192,224},{224... | collective-permute-start | bytes 884744 | tf_op jit(solution)/shard_map/ppermute | solution.py:180
  145.1 3.4 %collective-permute-start.11 = (bf16[576,256]{1,0:T(8,128)(2,1)S(1)}, bf16[576,256]{1,0:T(8,128)(2,1)S(1)}, u32[]{:S(2)}, u32[]{:S(2)}) collective-permute-start(bf16[576,256]{1,0:T(8,128)(2,1)S(1)} %get-tuple-element.24), channel_id=1, source_target_pairs={{0,352},{32,0},{64,32},{96,64},{128,96},{160,128},{192,160},{224,1... | collective-permute-start | bytes 884744 | tf_op jit(solution)/shard_map/ppermute | solution.py:180
  148.5 4.8 %collective-permute-done.10.up = bf16[576,256]{1,0:T(8,128)(2,1)S(1)} collective-permute-done((bf16[576,256]{1,0:T(8,128)(2,1)S(1)}, bf16[576,256]{1,0:T(8,128)(2,1)S(1)}, u32[]{:S(2)}, u32[]{:S(2)}) %collective-permute-start.10) | collective-permute-done | bytes 294944 | tf_op jit(solution)/shard_map/ppermute | solution.py:180
  155.3 38.5 %all_to_all.15.chunks = bf16[8,128,256]{2,1,0:T(8,128)(2,1)S(1)} all-to-all(bf16[8,128,256]{2,1,0:T(8,128)(2,1)S(1)} %near_sum.1), channel_id=1, replica_groups=mesh['yh'=2,'za'=4,'zb'=3,'x'=4,'yl'=4,'core'=2] {'yh','za'}, dimensions={0} | all-to-all | bytes 1048576 | tf_op jit(solution)/shard_map/all_to_all | solution.py:266
  194.4 15.4 %all_gather.15 = f32[256,256]{1,0:T(8,128)S(1)} all-gather(f32[32,256]{1,0:T(8,128)S(1)} %get-tuple-element.26), channel_id=1, replica_groups=mesh['yh'=2,'za'=4,'zb'=3,'x'=4,'yl'=4,'core'=2] {'yl','core'}, dimensions={0}, use_global_device_ids=true | all-gather | bytes 294912 | tf_op jit(solution)/shard_map/all_gather | solution.py:276
  (46 shorter events, 10.7 us)
Async XLA Ops:
  7.2 128.4 %all-gather.2.cloned.1.call-start = ((), (), s32[]{:S(2)}) async-start(), calls=%async_computation.2 | async-start | bytes 1179648 | tf_op jit(solution)/shard_map/all_gather | solution.py:222
  7.2 1.5 copy-start.3
  7.9 0.7 copy-start.5
  7.9 0.7 copy-start.6
  8.7 1.2 copy-start
  9.9 7.6 %copy-start.4 = (bf16[1,64,256]{2,1,0:T(8,128)(2,1)S(1)}, bf16[1,64,256]{2,1,0:T(8,128)(2,1)}, u32[]{:S(2)}) copy-start(bf16[1,64,256]{2,1,0:T(8,128)(2,1)} %param.7) | copy-start | bytes 98308
  11.2 47.4 %collective-permute-start.2 = (bf16[35,64,128]{2,1,0:T(8,128)(2,1)S(1)}, bf16[35,64,128]{2,1,0:T(8,128)(2,1)S(1)}, u32[]{:S(2)}, u32[]{:S(2)}) collective-permute-start(bf16[35,64,128]{2,1,0:T(8,128)(2,1)S(1)} %get-tuple-element.15), channel_id=1, source_target_pairs={{0,24},{8,0},{16,8},{24,16},{1,25},{9,1},{17,9},{25,17},{2,26},{10... | collective-permute-start | bytes 1720328 | tf_op jit(solution)/shard_map/ppermute | solution.py:180
  15.6 43.0 %collective-permute-start = (bf16[35,64,128]{2,1,0:T(8,128)(2,1)S(1)}, bf16[35,64,128]{2,1,0:T(8,128)(2,1)S(1)}, u32[]{:S(2)}, u32[]{:S(2)}) collective-permute-start(bf16[35,64,128]{2,1,0:T(8,128)(2,1)S(1)} %get-tuple-element.15), channel_id=1, source_target_pairs={{0,8},{8,16},{16,24},{24,0},{1,9},{9,17},{17,25},{25,1},{2,10},{10... | collective-permute-start | bytes 1720328 | tf_op jit(solution)/shard_map/ppermute | solution.py:180
  17.5 11.1 %collective-permute-start.3 = (bf16[64,256]{1,0:T(8,128)(2,1)S(1)}, bf16[64,256]{1,0:T(8,128)(2,1)S(1)}, u32[]{:S(2)}, u32[]{:S(2)}) collective-permute-start(bf16[64,256]{1,0:T(8,128)(2,1)S(1)} %bitcast.67), channel_id=1, source_target_pairs={{0,384},{384,0},{1,385},{385,1},{2,386},{386,2},{3,387},{387,3},{4... | collective-permute-start | bytes 98312 | tf_op jit(solution)/shard_map/ppermute | solution.py:180
  25.0 33.7 %collective-permute-start.1 = (bf16[35,64,128]{2,1,0:T(8,128)(2,1)S(1)}, bf16[35,64,128]{2,1,0:T(8,128)(2,1)S(1)}, u32[]{:S(2)}, u32[]{:S(2)}) collective-permute-start(bf16[35,64,128]{2,1,0:T(8,128)(2,1)S(1)} %get-tuple-element.16.s0), channel_id=1, source_target_pairs={{0,16},{8,24},{16,0},{24,8},{1,17},{9,25},{17,1},{25,9},{2,18},{10... | collective-permute-start | bytes 1720328 | tf_op jit(solution)/shard_map/ppermute | solution.py:180
  63.8 7.8 %collective-permute-start.4 = (bf16[512,256]{1,0:T(8,128)(2,1)S(1)}, bf16[512,256]{1,0:T(8,128)(2,1)S(1)}, u32[]{:S(2)}, u32[]{:S(2)}) collective-permute-start(bf16[512,256]{1,0:T(8,128)(2,1)S(1)} %get-tuple-element.18), channel_id=1, source_target_pairs={{0,24},{8,0},{16,8},{24,16},{1,25},{9,1},{17,9},{25,17},{2,26},{10... | collective-permute-start | bytes 786440 | tf_op jit(solution)/shard_map/ppermute | solution.py:180
  66.0 8.6 %collective-permute-start.5 = (bf16[512,256]{1,0:T(8,128)(2,1)S(1)}, bf16[512,256]{1,0:T(8,128)(2,1)S(1)}, u32[]{:S(2)}, u32[]{:S(2)}) collective-permute-start(bf16[512,256]{1,0:T(8,128)(2,1)S(1)} %get-tuple-element.19), channel_id=1, source_target_pairs={{0,16},{8,24},{16,0},{24,8},{1,17},{9,25},{17,1},{25,9},{2,18},{10... | collective-permute-start | bytes 786440 | tf_op jit(solution)/shard_map/ppermute | solution.py:180
  69.6 8.3 %collective-permute-start.6 = (bf16[512,256]{1,0:T(8,128)(2,1)S(1)}, bf16[512,256]{1,0:T(8,128)(2,1)S(1)}, u32[]{:S(2)}, u32[]{:S(2)}) collective-permute-start(bf16[512,256]{1,0:T(8,128)(2,1)S(1)} %get-tuple-element.20), channel_id=1, source_target_pairs={{0,8},{8,16},{16,24},{24,0},{1,9},{9,17},{17,25},{25,1},{2,10},{10... | collective-permute-start | bytes 786440 | tf_op jit(solution)/shard_map/ppermute | solution.py:180
  101.4 34.1 %copy-start.2 = (bf16[256,256]{1,0:T(8,128)(2,1)S(1)}, bf16[256,256]{1,0:T(8,128)(2,1)}, u32[]{:S(2)}) copy-start(bf16[256,256]{1,0:T(8,128)(2,1)} %w.1) | copy-start | bytes 393220
  116.3 9.6 %collective-permute-start.9 = (bf16[512,256]{1,0:T(8,128)(2,1)S(1)}, bf16[512,256]{1,0:T(8,128)(2,1)S(1)}, u32[]{:S(2)}, u32[]{:S(2)}) collective-permute-start(bf16[512,256]{1,0:T(8,128)(2,1)S(1)} %all_gather.13.a0), channel_id=1, source_target_pairs={{0,24},{8,0},{16,8},{24,16},{1,25},{9,1},{17,9},{25,17},{2,26},{10... | collective-permute-start | bytes 786440 | tf_op jit(solution)/shard_map/ppermute | solution.py:180
  118.3 10.9 %collective-permute-start.8 = (bf16[512,256]{1,0:T(8,128)(2,1)S(1)}, bf16[512,256]{1,0:T(8,128)(2,1)S(1)}, u32[]{:S(2)}, u32[]{:S(2)}) collective-permute-start(bf16[512,256]{1,0:T(8,128)(2,1)S(1)} %all_gather.13.a0), channel_id=1, source_target_pairs={{0,16},{8,24},{16,0},{24,8},{1,17},{9,25},{17,1},{25,9},{2,18},{10... | collective-permute-start | bytes 786440 | tf_op jit(solution)/shard_map/ppermute | solution.py:180
  120.7 14.8 %collective-permute-start.7 = (bf16[512,256]{1,0:T(8,128)(2,1)S(1)}, bf16[512,256]{1,0:T(8,128)(2,1)S(1)}, u32[]{:S(2)}, u32[]{:S(2)}) collective-permute-start(bf16[512,256]{1,0:T(8,128)(2,1)S(1)} %all_gather.13.a0), channel_id=1, source_target_pairs={{0,8},{8,16},{16,24},{24,0},{1,9},{9,17},{17,25},{25,1},{2,10},{10... | collective-permute-start | bytes 786440 | tf_op jit(solution)/shard_map/ppermute | solution.py:180
  135.5 1.2 copy-start.1
  142.2 11.1 %collective-permute-start.10 = (bf16[576,256]{1,0:T(8,128)(2,1)S(1)}, bf16[576,256]{1,0:T(8,128)(2,1)S(1)}, u32[]{:S(2)}, u32[]{:S(2)}) collective-permute-start(bf16[576,256]{1,0:T(8,128)(2,1)S(1)} %get-tuple-element.23), channel_id=1, source_target_pairs={{0,32},{32,64},{64,96},{96,128},{128,160},{160,192},{192,224},{224... | collective-permute-start | bytes 884744 | tf_op jit(solution)/shard_map/ppermute | solution.py:180
  145.1 10.1 %collective-permute-start.11 = (bf16[576,256]{1,0:T(8,128)(2,1)S(1)}, bf16[576,256]{1,0:T(8,128)(2,1)S(1)}, u32[]{:S(2)}, u32[]{:S(2)}) collective-permute-start(bf16[576,256]{1,0:T(8,128)(2,1)S(1)} %get-tuple-element.24), channel_id=1, source_target_pairs={{0,352},{32,0},{64,32},{96,64},{128,96},{160,128},{192,160},{224,1... | collective-permute-start | bytes 884744 | tf_op jit(solution)/shard_map/ppermute | solution.py:180
Sparse Core Ops, SparseCore 0:
  59.5 41.2 all-gather.1

commit v4 on v3

--- a/solution.py
+++ b/solution.py
@@ -25,7 +25,7 @@
     return pl.BlockSpec(memory_space=space)
 
 
-def pack_kernel(info, tiles, cot, meta, same, other):
+def pack_kernel(info, tiles, meta, same, other):
     slots = tiles.shape[0]
     odd = info[0] == 1
 
@@ -38,12 +38,10 @@
 
     lax.fori_loop(0, slots, one, 0, unroll=4)
     for ref in (same, other):
-        ref[slots] = cot[:, :TILE]
-        ref[slots + 1] = cot[:, TILE:]
-        ref[slots + 2] = jnp.broadcast_to(meta[...], (STRIP, TILE)).astype(BF)
-
-
-def live_list(codes, mine, place_of, table, strips, pool):
+        ref[slots] = jnp.broadcast_to(meta[...], (STRIP, TILE)).astype(BF)
+
+
+def live_list(codes, mine, row_of, place_of, table, strips, pool):
     slots = codes.shape[1]
     for j, ref in enumerate(strips):
         pool[j * slots : (j + 1) * slots] = ref[:slots]
@@ -55,7 +53,7 @@
             code = codes[j, s]
             col, row = code >> 2, code & 3
             table[0, n] = j * slots + s
-            table[1, n] = j * 4 + row
+            table[1, n] = j * 4 + row_of(row)
             table[2, n] = place_of(col >> 1)
             return n + ((code >= 0) & ((col & 1) == mine)).astype(jnp.int32)
 
@@ -75,7 +73,7 @@
         far = (q >= nz).astype(jnp.int32)
         return (q - far * nz) * 2 + (far ^ my_yh)
 
-    count = live_list(codes, mine, place_of, table, (s0, s1, s2, s3), pool)
+    count = live_list(codes, mine, lambda r: r, place_of, table, (s0, s1, s2, s3), pool)
     acc[...] = jnp.zeros_like(acc)
 
     def several(t, carry):
@@ -98,27 +96,35 @@
 
 
 def bwd_kernel(
-    nz, codes, info, s0, s1, s2, s3, a0, a1, a2, a3, cot, w, out, keep, up, down, table, pool, ga, acc, gw4, act
+    nz, codes, info, s0, s1, s2, s3, a_own, a_other, c0, c1, c2, c3, w, out, keep, up, down,
+    table, pool, agg, ga, acc, gw4, act,
 ):
-    rows, feat = a0.shape
+    rows, feat = c0.shape
     mine, col_pos, my_zb, my_x = info[1], info[3], info[4], info[5]
-    share = feat // cot.shape[0]
-    count = live_list(codes, mine, lambda q: q, table, (s0, s1, s2, s3), pool)
+    my_yl, my_core = col_pos >> 1, col_pos & 1
+    share = keep.shape[0] - (acc.shape[0] // 3)
+    n_yl = rows // TILE
+    count = live_list(codes, mine, lambda r: (my_yl - r) & (n_yl - 1), lambda q: q, table, (s0, s1, s2, s3), pool)
     acc[...] = jnp.zeros_like(acc)
     per = 4 * TILE
-    for j, agg in enumerate((a0, a1, a2, a3)):
-        pre = jnp.dot(agg[...], w[...], preferred_element_type=F32)
+    for j, cot in enumerate((c0, c1, c2, c3)):
+        for d in range(n_yl):
+            src = pl.ds(pl.multiple_of((((my_yl - d) & (n_yl - 1)) * 4 + j) * STRIP, STRIP), STRIP)
+            for i, ref in enumerate((a_own, a_other)):
+                to = pl.multiple_of(j * per + d * TILE + (my_core ^ i) * STRIP, STRIP)
+                agg[pl.ds(to, STRIP), :] = ref[src, :]
+        block = agg[j * per : j * per + rows, :]
+        pre = jnp.dot(block, w[...], preferred_element_type=F32)
         sig = jax.nn.sigmoid(pre)
         if j == 0:
-            act[...] = pre * sig
+            act[...] = (pre * sig)[:TILE]
         slope = sig * (1.0 + pre * (1.0 - sig))
-        cot_j = cot[:, j].reshape(rows, feat).astype(F32)
-        gp = (cot_j * slope).astype(BF)
-        gw4[(my_x - j) & 3] = lax.dot_general(agg[...], gp, (((0,), (0,)), ((), ())), preferred_element_type=F32)
+        gp = (cot[...].astype(F32) * slope).astype(BF)
+        gw4[(my_x - j) & 3] = lax.dot_general(block, gp, (((0,), (0,)), ((), ())), preferred_element_type=F32)
         ga[j * per : j * per + rows, :] = lax.dot_general(
             gp, w[...], (((1,), (1,)), ((), ())), preferred_element_type=F32
         ).astype(BF)
-    out[...] = act[pl.ds(pl.multiple_of(col_pos * STRIP, STRIP), STRIP), :].astype(BF)
+    out[...] = act[pl.ds(pl.multiple_of(my_core * STRIP, STRIP), STRIP), :].astype(BF)
 
     def several(t, carry):
         terms = []
@@ -210,17 +216,20 @@
     meta = jnp.pad(code.astype(F32), (0, TILE - slots))[None]
 
     near = jnp.concatenate([own, shift(own, "yh", 1)], axis=0)
+
+    parcel = ((slots + 1, STRIP, TILE), BF)
+    same, other = call(pack_kernel, "pack", [smem, vmem, vmem], [parcel] * 2, [], info, tile_values[0, 0], meta)
+    strips = [same] + [shift(same if d == 2 else other, "x", d) for d in (1, 2, 3)]
+    codes = jnp.stack([code] + [s[slots, 0, :slots].astype(jnp.int32) for s in strips[1:]])
+
+    pair = lax.all_gather(cotangent[0], "core", axis=0, tiled=True)
+    n_yl = lax.axis_size("yl")
+    pairs = [pair] + [shift(pair, "yl", d) for d in range(1, n_yl)]
+    near, *pairs = lax.optimization_barrier((near, *pairs))
+    block_cot = jnp.concatenate(pairs, axis=0)
+
     column = lax.all_gather(near, Z, axis=0, tiled=True)
-
-    parcel = ((slots + 3, STRIP, TILE), BF)
-    same, other = call(
-        pack_kernel, "pack", [smem, vmem, vmem, vmem], [parcel] * 2, [], info, tile_values[0, 0], cotangent[0], meta
-    )
-    strips = [same] + [shift(same if d == 2 else other, "x", d) for d in (1, 2, 3)]
-    codes = jnp.stack([code] + [s[slots + 2, 0, :slots].astype(jnp.int32) for s in strips[1:]])
-    cots = jnp.stack([jnp.concatenate([s[slots], s[slots + 1]], axis=1) for s in strips])
-    cot_all = lax.all_gather(cots.reshape(4 * STRIP, feat), COL, axis=0, tiled=True)
-    cot_all = cot_all.reshape(col_devs, 4, STRIP, feat)
+    column, block_cot = lax.optimization_barrier((column, block_cot))
 
     listing = [pltpu.SMEM((3, 4 * slots + STEP), jnp.int32), pltpu.VMEM((4 * slots + 1, STRIP, TILE), BF)]
     parts = call(
@@ -235,25 +244,29 @@
     back = [shift(parts[d], "x", -d) for d in (1, 2, 3)]
     block_sum = (parts[0] + (back[0].astype(F32) + back[1].astype(F32) + back[2].astype(F32))).astype(BF)
     pieces = lax.all_to_all(block_sum, COL, split_axis=0, concat_axis=0, tiled=True)
+    cots = [block_cot] + [shift(block_cot, "x", d) for d in (1, 2, 3)]
+    pieces, *cots = lax.optimization_barrier((pieces, *cots))
     agg = jnp.sum(pieces.reshape(col_devs, per_dev, feat).astype(F32), axis=0).astype(BF)
-    block_agg = lax.all_gather(agg, COL, axis=0, tiled=True)
-    aggs = [block_agg] + [shift(block_agg, "x", d) for d in (1, 2, 3)]
+    group_agg = jnp.concatenate([agg] + [shift(agg, "x", d) for d in (1, 2, 3)], axis=0)
+    core_agg = lax.all_gather(group_agg, "yl", axis=0, tiled=True)
+    other_agg = shift(core_agg, "core", 1)
 
     share = feat // col_devs
     chunk_rows = n_chunks * STRIP
     output_rows, keep, up, down = call(
         functools.partial(bwd_kernel, nz),
         "backward_tiles",
-        [smem, smem] + [vmem] * 10,
+        [smem, smem] + [vmem] * 11,
         [((per_dev, feat), BF), ((chunk_rows + share, feat), F32)] + [((chunk_rows + 2 * share, feat), BF)] * 2,
         listing
         + [
             pltpu.VMEM((16 * TILE, feat), BF),
+            pltpu.VMEM((16 * TILE, feat), BF),
             pltpu.VMEM((groups * STRIP, feat), F32),
             pltpu.VMEM((4, feat, feat), F32),
-            pltpu.VMEM((rows, feat), F32),
+            pltpu.VMEM((TILE, feat), F32),
         ],
-        codes, info, *strips, *aggs, cot_all, weight,
+        codes, info, *strips, core_agg, other_agg, *cots, weight,
     )
     (chunks,) = call(
         near_kernel,

time: 218 us -> 218 us (level)
  starting transfers between devices: 38.6 us -> 75.6 us
  blocking collectives: 122 us -> 96 us
  between operations: 15 us -> 1.67 us
  waiting for transfers between devices: 25 us -> 28.4 us
    ppermute x12 -> x19, starting transfers between devices: 38.6 us -> 62.3 us  [shift(): return lax.ppermute(value, axis, [(i, (i + by) % n) for i in range(n)])]
    all_to_all x1 -> x0, blocking collectives: 23.3 us -> none  [on_device(): lax.all_to_all(block_sum, COL, split_axis=0, concat_axis=0, tiled=True)]
    all_to_all x0 -> x1, starting transfers between devices: none -> 13.2 us  [on_device(): lax.all_to_all(block_sum, COL, split_axis=0, concat_axis=0, tiled=True)]
    all_to_all x1, blocking collectives: 38.5 us -> 32.4 us  [on_device(): lax.all_to_all(chunks, ('yh', 'za'), split_axis=0, concat_axis=0, tiled=T...]
    all_gather x1, blocking collectives: 15.4 us -> 19.2 us  [on_device(): grad_weight = lax.all_gather(weight_part, COL, axis=0, tiled=True)]
    ppermute x12 -> x19, waiting for transfers between devices: 25 us -> 28.4 us  [shift(): return lax.ppermute(value, axis, [(i, (i + by) % n) for i in range(n)])]
    all_gather x1 -> x2, blocking collectives: 14.9 us -> 15 us  [the longest x1 12.6 us: on_device(): core_agg = lax.all_gather(group_agg, 'yl', axis=0, tiled=True)]
  transfers between devices with their start and end apart: 13 -> 20, of which waited for: 7 -> 10; matrix products, arithmetic and copies ran while one was open for 0% -> 0% of each run, Pallas kernels for 2% -> 1%
where the time goes in v4:
time: 218 us; the launch traced here: 217 us
  blocking collectives  96 us (44%)
  starting transfers between devices  75.6 us (35%)
  waiting for transfers between devices  28.4 us (13%)
  Pallas kernels  12.1 us (6%)
  local copies, waits for them, and re-layouts  2.69 us (1%)
    ppermute x19, starting transfers between devices, shift(): return lax.ppermute(value, axis, [(i, (i + by) % n) for i in range(n)])  62.3 us
    all_to_all x1, blocking collectives, on_device(): lax.all_to_all(chunks, ('yh', 'za'), split_axis=0, concat_axis=0, tiled=T...  32.4 us
    all_gather x1, blocking collectives, on_device(): column = lax.all_gather(near, Z, axis=0, tiled=True)  29.3 us
    ppermute x19, waiting for transfers between devices, shift(): return lax.ppermute(value, axis, [(i, (i + by) % n) for i in range(n)])  28.4 us
    all_gather x1, blocking collectives, on_device(): grad_weight = lax.all_gather(weight_part, COL, axis=0, tiled=True)  19.2 us
    all_to_all x1, starting transfers between devices, on_device(): lax.all_to_all(block_sum, COL, split_axis=0, concat_axis=0, tiled=True)  13.2 us
    all_gather x1, blocking collectives, on_device(): core_agg = lax.all_gather(group_agg, 'yl', axis=0, tiled=True)  12.6 us
    pallas_call x5, Pallas kernels, call(): pl.pallas_call(kernel, out_shape=tuple((jax.ShapeDtypeStruct(s, t) for s,...  12.1 us
  transfers between devices with their start and end apart: 20, of which 10 were waited for; matrix products, arithmetic and copies ran while one was open for 0% of the time, Pallas kernels for 1%

profile of v4, /device:TPU:65, one launch (start us, length us, event | category | flops | bytes accessed | tf_op | source)
XLA Modules:
  0.0 217.3 jit_solution(278262861359443927)
XLA Ops:
  3.0 5.2 %collective-permute-start.6 = (bf16[128,256]{1,0:T(8,128)(2,1)S(1)}, bf16[128,256]{1,0:T(8,128)(2,1)S(1)}, u32[]{:S(2)}, u32[]{:S(2)}) collective-permute-start(bf16[128,256]{1,0:T(8,128)(2,1)S(1)} %bitcast.39), channel_id=1, source_target_pairs={{0,6},{2,0},{4,2},{6,4},{1,7},{3,1},{5,3},{7,5},{8,14},{10,8},{12,... | collective-permute-start | bytes 196616 | tf_op jit(solution)/shard_map/ppermute | solution.py:186
  12.6 5.7 %collective-permute-start.3 = (bf16[64,256]{1,0:T(8,128)(2,1)S(1)}, bf16[64,256]{1,0:T(8,128)(2,1)S(1)}, u32[]{:S(2)}, u32[]{:S(2)}) collective-permute-start(bf16[64,256]{1,0:T(8,128)(2,1)S(1)} %bitcast.43), channel_id=1, source_target_pairs={{0,384},{384,0},{1,385},{385,1},{2,386},{386,2},{3,387},{387,3},{4... | collective-permute-start | bytes 98312 | tf_op jit(solution)/shard_map/ppermute | solution.py:186
  22.2 4.4 %collective-permute-start.2 = (bf16[33,64,128]{2,1,0:T(8,128)(2,1)S(1)}, bf16[33,64,128]{2,1,0:T(8,128)(2,1)S(1)}, u32[]{:S(2)}, u32[]{:S(2)}) collective-permute-start(bf16[33,64,128]{2,1,0:T(8,128)(2,1)S(1)} %get-tuple-element.27), channel_id=1, source_target_pairs={{0,24},{8,0},{16,8},{24,16},{1,25},{9,1},{17,9},{25,17},{2,26},{10... | collective-permute-start | bytes 1622024 | tf_op jit(solution)/shard_map/ppermute | solution.py:186
  28.5 3.6 %collective-permute-start.1 = (bf16[33,64,128]{2,1,0:T(8,128)(2,1)S(1)}, bf16[33,64,128]{2,1,0:T(8,128)(2,1)S(1)}, u32[]{:S(2)}, u32[]{:S(2)}) collective-permute-start(bf16[33,64,128]{2,1,0:T(8,128)(2,1)S(1)} %get-tuple-element.28.s0), channel_id=1, source_target_pairs={{0,16},{8,24},{16,0},{24,8},{1,17},{9,25},{17,1},{25,9},{2,18},{10... | collective-permute-start | bytes 1622024 | tf_op jit(solution)/shard_map/ppermute | solution.py:186
  32.2 29.3 %all_gather.13.feats = bf16[1536,256]{1,0:T(8,128)(2,1)S(1)} all-gather(bf16[128,256]{1,0:T(8,128)(2,1)S(1)} %pad_maximum_fusion.2), channel_id=1, replica_groups=mesh['yh'=2,'za'=4,'zb'=3,'x'=4,'yl'=4,'core'=2] {'za','zb'}, dimensions={0}, use_global_device_ids=true | all-gather | bytes 851968 | tf_op jit(solution)/shard_map/all_gather | solution.py:231
  61.7 4.4 %forward_tiles.1 = (f32[512,256]{1,0:T(8,128)S(1)}, bf16[512,256]{1,0:T(8,128)(2,1)S(1)}, bf16[512,256]{1,0:T(8,128)(2,1)S(1)}, bf16[512,256]{1,0:T(8,128)(2,1)S(1)}) custom-call(s32[4,32]{1,0:T(4,128)S(1)} %pad_add_fusion.codes, s32[6]{0:T(128)S(1)} %stack.34.info, bf16[33,64,128]{2,1,0:T(8,128)(2,1)S(1)} %get-tuple-element.28.s0, ...), custom_call_target="tpu_custom_call" | custom-call | tf_op jit(solution)/shard_map/forward_tiles/pallas_call | solution.py:204
  68.5 4.1 %collective-permute-start.8 = (bf16[512,256]{1,0:T(8,128)(2,1)S(1)}, bf16[512,256]{1,0:T(8,128)(2,1)S(1)}, u32[]{:S(2)}, u32[]{:S(2)}) collective-permute-start(bf16[512,256]{1,0:T(8,128)(2,1)S(1)} %get-tuple-element.37), channel_id=1, source_target_pairs={{0,16},{8,24},{16,0},{24,8},{1,17},{9,25},{17,1},{25,9},{2,18},{10... | collective-permute-start | bytes 786440 | tf_op jit(solution)/shard_map/ppermute | solution.py:186
  74.6 2.5 %collective-permute-done.8 = bf16[512,256]{1,0:T(8,128)(2,1)S(1)} collective-permute-done((bf16[512,256]{1,0:T(8,128)(2,1)S(1)}, bf16[512,256]{1,0:T(8,128)(2,1)S(1)}, u32[]{:S(2)}, u32[]{:S(2)}) %collective-permute-start.8) | collective-permute-done | bytes 262176 | tf_op jit(solution)/shard_map/ppermute | solution.py:186
  77.1 3.9 %collective-permute-done.9 = bf16[512,256]{1,0:T(8,128)(2,1)S(1)} collective-permute-done((bf16[512,256]{1,0:T(8,128)(2,1)S(1)}, bf16[512,256]{1,0:T(8,128)(2,1)S(1)}, u32[]{:S(2)}, u32[]{:S(2)}) %collective-permute-start.9) | collective-permute-done | bytes 262176 | tf_op jit(solution)/shard_map/ppermute | solution.py:186
  81.8 13.2 %all-to-all-start = ((bf16[8,64,256]{2,1,0:T(8,128)(2,1)}), bf16[8,64,256]{2,1,0:T(8,128)(2,1)S(1)}, u32[]{:S(2)}, u32[]{:S(2)}) async-start(bf16[8,64,256]{2,1,0:T(8,128)(2,1)} %bitcast.16), calls=%async_computation | async-start | bytes 524288 | tf_op jit(solution)/shard_map/all_to_all | solution.py:246
  96.9 3.1 %collective-permute-start.11 = (bf16[512,256]{1,0:T(8,128)(2,1)S(1)}, bf16[512,256]{1,0:T(8,128)(2,1)S(1)}, u32[]{:S(2)}, u32[]{:S(2)}) collective-permute-start(bf16[512,256]{1,0:T(8,128)(2,1)S(1)} %pad_maximum_fusion.c0), channel_id=1, source_target_pairs={{0,16},{8,24},{16,0},{24,8},{1,17},{9,25},{17,1},{25,9},{2,18},{10... | collective-permute-start | bytes 786440 | tf_op jit(solution)/shard_map/ppermute | solution.py:186
  100.0 2.5 %collective-permute-start.10 = (bf16[512,256]{1,0:T(8,128)(2,1)S(1)}, bf16[512,256]{1,0:T(8,128)(2,1)S(1)}, u32[]{:S(2)}, u32[]{:S(2)}) collective-permute-start(bf16[512,256]{1,0:T(8,128)(2,1)S(1)} %pad_maximum_fusion.c0), channel_id=1, source_target_pairs={{0,8},{8,16},{16,24},{24,0},{1,9},{9,17},{17,25},{25,1},{2,10},{10... | collective-permute-start | bytes 786440 | tf_op jit(solution)/shard_map/ppermute | solution.py:186
  104.8 3.5 %collective-permute-done.11.c2 = bf16[512,256]{1,0:T(8,128)(2,1)S(1)} collective-permute-done((bf16[512,256]{1,0:T(8,128)(2,1)S(1)}, bf16[512,256]{1,0:T(8,128)(2,1)S(1)}, u32[]{:S(2)}, u32[]{:S(2)}) %collective-permute-start.11) | collective-permute-done | bytes 262176 | tf_op jit(solution)/shard_map/ppermute | solution.py:186
  108.3 5.9 %collective-permute-done.10.c1 = bf16[512,256]{1,0:T(8,128)(2,1)S(1)} collective-permute-done((bf16[512,256]{1,0:T(8,128)(2,1)S(1)}, bf16[512,256]{1,0:T(8,128)(2,1)S(1)}, u32[]{:S(2)}, u32[]{:S(2)}) %collective-permute-start.10) | collective-permute-done | bytes 262176 | tf_op jit(solution)/shard_map/ppermute | solution.py:186
  116.2 3.1 %collective-permute-start.14 = (bf16[64,256]{1,0:T(8,128)(2,1)S(1)}, bf16[64,256]{1,0:T(8,128)(2,1)S(1)}, u32[]{:S(2)}, u32[]{:S(2)}) collective-permute-start(bf16[64,256]{1,0:T(8,128)(2,1)S(1)} %reduce_sum.12), channel_id=1, source_target_pairs={{0,16},{8,24},{16,0},{24,8},{1,17},{9,25},{17,1},{25,9},{2,18},{10... | collective-permute-start | bytes 98312 | tf_op jit(solution)/shard_map/ppermute | solution.py:186
  119.3 2.8 %collective-permute-start.13 = (bf16[64,256]{1,0:T(8,128)(2,1)S(1)}, bf16[64,256]{1,0:T(8,128)(2,1)S(1)}, u32[]{:S(2)}, u32[]{:S(2)}) collective-permute-start(bf16[64,256]{1,0:T(8,128)(2,1)S(1)} %reduce_sum.12), channel_id=1, source_target_pairs={{0,8},{8,16},{16,24},{24,0},{1,9},{9,17},{17,25},{25,1},{2,10},{10... | collective-permute-start | bytes 98312 | tf_op jit(solution)/shard_map/ppermute | solution.py:186
  122.3 2.8 %collective-permute-done.13 = bf16[64,256]{1,0:T(8,128)(2,1)S(1)} collective-permute-done((bf16[64,256]{1,0:T(8,128)(2,1)S(1)}, bf16[64,256]{1,0:T(8,128)(2,1)S(1)}, u32[]{:S(2)}, u32[]{:S(2)}) %collective-permute-start.13) | collective-permute-done | bytes 32800 | tf_op jit(solution)/shard_map/ppermute | solution.py:186
  125.2 12.6 %all_gather.14.a_own = bf16[1024,256]{1,0:T(8,128)(2,1)S(1)} all-gather(bf16[256,256]{1,0:T(8,128)(2,1)S(1)} %pad_maximum_fusion.1), channel_id=1, replica_groups=mesh['yh'=2,'za'=4,'zb'=3,'x'=4,'yl'=4,'core'=2] {'yl'}, dimensions={0}, use_global_device_ids=true | all-gather | bytes 655360 | tf_op jit(solution)/shard_map/all_gather | solution.py:251
  137.8 7.9 %collective-permute-start.16 = (bf16[1024,256]{1,0:T(8,128)(2,1)S(1)}, bf16[1024,256]{1,0:T(8,128)(2,1)S(1)}, u32[]{:S(2)}, u32[]{:S(2)}) collective-permute-start(bf16[1024,256]{1,0:T(8,128)(2,1)S(1)} %all_gather.14.a_own), channel_id=1, source_target_pairs={{0,1},{1,0},{2,3},{3,2},{4,5},{5,4},{6,7},{7,6},{8,9},{9,8},{10,11... | collective-permute-start | bytes 1572872 | tf_op jit(solution)/shard_map/ppermute | solution.py:186
  147.2 5.7 %backward_tiles.1 = (bf16[64,256]{1,0:T(8,128)(2,1)}, f32[544,256]{1,0:T(8,128)S(1)}, bf16[576,256]{1,0:T(8,128)(2,1)S(1)}, bf16[576,256]{1,0:T(8,128)(2,1)S(1)}) custom-call(s32[4,32]{1,0:T(4,128)S(1)} %pad_add_fusion.codes, s32[6]{0:T(128)S(1)} %stack.34.info, bf16[33,64,128]{2,1,0:T(8,128)(2,1)S(1)} %get-tuple-element.28.s0, ...), custom_call_target="tpu_custom_call" | custom-call | tf_op jit(solution)/shard_map/backward_tiles/pallas_call | solution.py:204
  155.0 3.5 %collective-permute-start.18 = (bf16[576,256]{1,0:T(8,128)(2,1)S(1)}, bf16[576,256]{1,0:T(8,128)(2,1)S(1)}, u32[]{:S(2)}, u32[]{:S(2)}) collective-permute-start(bf16[576,256]{1,0:T(8,128)(2,1)S(1)} %get-tuple-element.48), channel_id=1, source_target_pairs={{0,352},{32,0},{64,32},{96,64},{128,96},{160,128},{192,160},{224,1... | collective-permute-start | bytes 884744 | tf_op jit(solution)/shard_map/ppermute | solution.py:186
  158.5 4.7 %collective-permute-done.17.up = bf16[576,256]{1,0:T(8,128)(2,1)S(1)} collective-permute-done((bf16[576,256]{1,0:T(8,128)(2,1)S(1)}, bf16[576,256]{1,0:T(8,128)(2,1)S(1)}, u32[]{:S(2)}, u32[]{:S(2)}) %collective-permute-start.17) | collective-permute-done | bytes 294944 | tf_op jit(solution)/shard_map/ppermute | solution.py:186
  164.3 32.4 %all_to_all.17.chunks = bf16[8,128,256]{2,1,0:T(8,128)(2,1)S(1)} all-to-all(bf16[8,128,256]{2,1,0:T(8,128)(2,1)S(1)} %near_sum.1), channel_id=1, replica_groups=mesh['yh'=2,'za'=4,'zb'=3,'x'=4,'yl'=4,'core'=2] {'yh','za'}, dimensions={0} | all-to-all | bytes 1048576 | tf_op jit(solution)/shard_map/all_to_all | solution.py:279
  197.4 19.2 %all_gather.15 = f32[256,256]{1,0:T(8,128)S(1)} all-gather(f32[32,256]{1,0:T(8,128)S(1)} %get-tuple-element.50), channel_id=1, replica_groups=mesh['yh'=2,'za'=4,'zb'=3,'x'=4,'yl'=4,'core'=2] {'yl','core'}, dimensions={0}, use_global_device_ids=true | all-gather | bytes 294912 | tf_op jit(solution)/shard_map/all_gather | solution.py:289
  (50 shorter events, 29.7 us)
Async XLA Ops:
  0.6 11.9 %copy-start.2 = (bf16[1,64,256]{2,1,0:T(8,128)(2,1)S(1)}, bf16[1,64,256]{2,1,0:T(8,128)(2,1)}, u32[]{:S(2)}) copy-start(bf16[1,64,256]{2,1,0:T(8,128)(2,1)} %param.7) | copy-start | bytes 98308
  3.0 25.5 %collective-permute-start.6 = (bf16[128,256]{1,0:T(8,128)(2,1)S(1)}, bf16[128,256]{1,0:T(8,128)(2,1)S(1)}, u32[]{:S(2)}, u32[]{:S(2)}) collective-permute-start(bf16[128,256]{1,0:T(8,128)(2,1)S(1)} %bitcast.39), channel_id=1, source_target_pairs={{0,6},{2,0},{4,2},{6,4},{1,7},{3,1},{5,3},{7,5},{8,14},{10,8},{12,... | collective-permute-start | bytes 196616 | tf_op jit(solution)/shard_map/ppermute | solution.py:186
  8.3 23.9 %collective-permute-start.5 = (bf16[128,256]{1,0:T(8,128)(2,1)S(1)}, bf16[128,256]{1,0:T(8,128)(2,1)S(1)}, u32[]{:S(2)}, u32[]{:S(2)}) collective-permute-start(bf16[128,256]{1,0:T(8,128)(2,1)S(1)} %bitcast.40), channel_id=1, source_target_pairs={{0,4},{2,6},{4,0},{6,2},{1,5},{3,7},{5,1},{7,3},{8,12},{10,14},{12... | collective-permute-start | bytes 196616 | tf_op jit(solution)/shard_map/ppermute | solution.py:186
  10.2 22.0 %collective-permute-start.4 = (bf16[128,256]{1,0:T(8,128)(2,1)S(1)}, bf16[128,256]{1,0:T(8,128)(2,1)S(1)}, u32[]{:S(2)}, u32[]{:S(2)}) collective-permute-start(bf16[128,256]{1,0:T(8,128)(2,1)S(1)} %bitcast.41), channel_id=1, source_target_pairs={{0,2},{2,4},{4,6},{6,0},{1,3},{3,5},{5,7},{7,1},{8,10},{10,12},{12... | collective-permute-start | bytes 196616 | tf_op jit(solution)/shard_map/ppermute | solution.py:186
  12.6 14.0 %collective-permute-start.3 = (bf16[64,256]{1,0:T(8,128)(2,1)S(1)}, bf16[64,256]{1,0:T(8,128)(2,1)S(1)}, u32[]{:S(2)}, u32[]{:S(2)}) collective-permute-start(bf16[64,256]{1,0:T(8,128)(2,1)S(1)} %bitcast.43), channel_id=1, source_target_pairs={{0,384},{384,0},{1,385},{385,1},{2,386},{386,2},{3,387},{387,3},{4... | collective-permute-start | bytes 98312 | tf_op jit(solution)/shard_map/ppermute | solution.py:186
  18.9 0.7 copy-start.4
  19.7 1.2 copy-start
  22.2 39.4 %collective-permute-start.2 = (bf16[33,64,128]{2,1,0:T(8,128)(2,1)S(1)}, bf16[33,64,128]{2,1,0:T(8,128)(2,1)S(1)}, u32[]{:S(2)}, u32[]{:S(2)}) collective-permute-start(bf16[33,64,128]{2,1,0:T(8,128)(2,1)S(1)} %get-tuple-element.27), channel_id=1, source_target_pairs={{0,24},{8,0},{16,8},{24,16},{1,25},{9,1},{17,9},{25,17},{2,26},{10... | collective-permute-start | bytes 1622024 | tf_op jit(solution)/shard_map/ppermute | solution.py:186
  26.6 35.0 %collective-permute-start = (bf16[33,64,128]{2,1,0:T(8,128)(2,1)S(1)}, bf16[33,64,128]{2,1,0:T(8,128)(2,1)S(1)}, u32[]{:S(2)}, u32[]{:S(2)}) collective-permute-start(bf16[33,64,128]{2,1,0:T(8,128)(2,1)S(1)} %get-tuple-element.27), channel_id=1, source_target_pairs={{0,8},{8,16},{16,24},{24,0},{1,9},{9,17},{17,25},{25,1},{2,10},{10... | collective-permute-start | bytes 1622024 | tf_op jit(solution)/shard_map/ppermute | solution.py:186
  28.5 33.1 %collective-permute-start.1 = (bf16[33,64,128]{2,1,0:T(8,128)(2,1)S(1)}, bf16[33,64,128]{2,1,0:T(8,128)(2,1)S(1)}, u32[]{:S(2)}, u32[]{:S(2)}) collective-permute-start(bf16[33,64,128]{2,1,0:T(8,128)(2,1)S(1)} %get-tuple-element.28.s0), channel_id=1, source_target_pairs={{0,16},{8,24},{16,0},{24,8},{1,17},{9,25},{17,1},{25,9},{2,18},{10... | collective-permute-start | bytes 1622024 | tf_op jit(solution)/shard_map/ppermute | solution.py:186
  66.0 8.5 %collective-permute-start.7 = (bf16[512,256]{1,0:T(8,128)(2,1)S(1)}, bf16[512,256]{1,0:T(8,128)(2,1)S(1)}, u32[]{:S(2)}, u32[]{:S(2)}) collective-permute-start(bf16[512,256]{1,0:T(8,128)(2,1)S(1)} %get-tuple-element.36), channel_id=1, source_target_pairs={{0,24},{8,0},{16,8},{24,16},{1,25},{9,1},{17,9},{25,17},{2,26},{10... | collective-permute-start | bytes 786440 | tf_op jit(solution)/shard_map/ppermute | solution.py:186
  68.5 8.6 %collective-permute-start.8 = (bf16[512,256]{1,0:T(8,128)(2,1)S(1)}, bf16[512,256]{1,0:T(8,128)(2,1)S(1)}, u32[]{:S(2)}, u32[]{:S(2)}) collective-permute-start(bf16[512,256]{1,0:T(8,128)(2,1)S(1)} %get-tuple-element.37), channel_id=1, source_target_pairs={{0,16},{8,24},{16,0},{24,8},{1,17},{9,25},{17,1},{25,9},{2,18},{10... | collective-permute-start | bytes 786440 | tf_op jit(solution)/shard_map/ppermute | solution.py:186
  72.6 8.3 %collective-permute-start.9 = (bf16[512,256]{1,0:T(8,128)(2,1)S(1)}, bf16[512,256]{1,0:T(8,128)(2,1)S(1)}, u32[]{:S(2)}, u32[]{:S(2)}) collective-permute-start(bf16[512,256]{1,0:T(8,128)(2,1)S(1)} %get-tuple-element.38), channel_id=1, source_target_pairs={{0,8},{8,16},{16,24},{24,0},{1,9},{9,17},{17,25},{25,1},{2,10},{10... | collective-permute-start | bytes 786440 | tf_op jit(solution)/shard_map/ppermute | solution.py:186
  81.8 32.4 %all-to-all-start = ((bf16[8,64,256]{2,1,0:T(8,128)(2,1)}), bf16[8,64,256]{2,1,0:T(8,128)(2,1)S(1)}, u32[]{:S(2)}, u32[]{:S(2)}) async-start(bf16[8,64,256]{2,1,0:T(8,128)(2,1)} %bitcast.16), calls=%async_computation | async-start | bytes 524288 | tf_op jit(solution)/shard_map/all_to_all | solution.py:246
  95.0 9.8 %collective-permute-start.12 = (bf16[512,256]{1,0:T(8,128)(2,1)S(1)}, bf16[512,256]{1,0:T(8,128)(2,1)S(1)}, u32[]{:S(2)}, u32[]{:S(2)}) collective-permute-start(bf16[512,256]{1,0:T(8,128)(2,1)S(1)} %pad_maximum_fusion.c0), channel_id=1, source_target_pairs={{0,24},{8,0},{16,8},{24,16},{1,25},{9,1},{17,9},{25,17},{2,26},{10... | collective-permute-start | bytes 786440 | tf_op jit(solution)/shard_map/ppermute | solution.py:186
  96.9 11.4 %collective-permute-start.11 = (bf16[512,256]{1,0:T(8,128)(2,1)S(1)}, bf16[512,256]{1,0:T(8,128)(2,1)S(1)}, u32[]{:S(2)}, u32[]{:S(2)}) collective-permute-start(bf16[512,256]{1,0:T(8,128)(2,1)S(1)} %pad_maximum_fusion.c0), channel_id=1, source_target_pairs={{0,16},{8,24},{16,0},{24,8},{1,17},{9,25},{17,1},{25,9},{2,18},{10... | collective-permute-start | bytes 786440 | tf_op jit(solution)/shard_map/ppermute | solution.py:186
  100.0 14.1 %collective-permute-start.10 = (bf16[512,256]{1,0:T(8,128)(2,1)S(1)}, bf16[512,256]{1,0:T(8,128)(2,1)S(1)}, u32[]{:S(2)}, u32[]{:S(2)}) collective-permute-start(bf16[512,256]{1,0:T(8,128)(2,1)S(1)} %pad_maximum_fusion.c0), channel_id=1, source_target_pairs={{0,8},{8,16},{16,24},{24,0},{1,9},{9,17},{17,25},{25,1},{2,10},{10... | collective-permute-start | bytes 786440 | tf_op jit(solution)/shard_map/ppermute | solution.py:186
  114.2 7.8 %collective-permute-start.15 = (bf16[64,256]{1,0:T(8,128)(2,1)S(1)}, bf16[64,256]{1,0:T(8,128)(2,1)S(1)}, u32[]{:S(2)}, u32[]{:S(2)}) collective-permute-start(bf16[64,256]{1,0:T(8,128)(2,1)S(1)} %reduce_sum.12), channel_id=1, source_target_pairs={{0,24},{8,0},{16,8},{24,16},{1,25},{9,1},{17,9},{25,17},{2,26},{10... | collective-permute-start | bytes 98312 | tf_op jit(solution)/shard_map/ppermute | solution.py:186
  116.2 6.2 %collective-permute-start.14 = (bf16[64,256]{1,0:T(8,128)(2,1)S(1)}, bf16[64,256]{1,0:T(8,128)(2,1)S(1)}, u32[]{:S(2)}, u32[]{:S(2)}) collective-permute-start(bf16[64,256]{1,0:T(8,128)(2,1)S(1)} %reduce_sum.12), channel_id=1, source_target_pairs={{0,16},{8,24},{16,0},{24,8},{1,17},{9,25},{17,1},{25,9},{2,18},{10... | collective-permute-start | bytes 98312 | tf_op jit(solution)/shard_map/ppermute | solution.py:186
  119.3 5.9 %collective-permute-start.13 = (bf16[64,256]{1,0:T(8,128)(2,1)S(1)}, bf16[64,256]{1,0:T(8,128)(2,1)S(1)}, u32[]{:S(2)}, u32[]{:S(2)}) collective-permute-start(bf16[64,256]{1,0:T(8,128)(2,1)S(1)} %reduce_sum.12), channel_id=1, source_target_pairs={{0,8},{8,16},{16,24},{24,0},{1,9},{9,17},{17,25},{25,1},{2,10},{10... | collective-permute-start | bytes 98312 | tf_op jit(solution)/shard_map/ppermute | solution.py:186
  125.1 22.1 %copy-start.1 = (bf16[256,256]{1,0:T(8,128)(2,1)S(1)}, bf16[256,256]{1,0:T(8,128)(2,1)}, u32[]{:S(2)}) copy-start(bf16[256,256]{1,0:T(8,128)(2,1)} %w.1) | copy-start | bytes 393220
  137.8 9.4 %collective-permute-start.16 = (bf16[1024,256]{1,0:T(8,128)(2,1)S(1)}, bf16[1024,256]{1,0:T(8,128)(2,1)S(1)}, u32[]{:S(2)}, u32[]{:S(2)}) collective-permute-start(bf16[1024,256]{1,0:T(8,128)(2,1)S(1)} %all_gather.14.a_own), channel_id=1, source_target_pairs={{0,1},{1,0},{2,3},{3,2},{4,5},{5,4},{6,7},{7,6},{8,9},{9,8},{10,11... | collective-permute-start | bytes 1572872 | tf_op jit(solution)/shard_map/ppermute | solution.py:186
  152.9 10.3 %collective-permute-start.17 = (bf16[576,256]{1,0:T(8,128)(2,1)S(1)}, bf16[576,256]{1,0:T(8,128)(2,1)S(1)}, u32[]{:S(2)}, u32[]{:S(2)}) collective-permute-start(bf16[576,256]{1,0:T(8,128)(2,1)S(1)} %get-tuple-element.47), channel_id=1, source_target_pairs={{0,32},{32,64},{64,96},{96,128},{128,160},{160,192},{192,224},{224... | collective-permute-start | bytes 884744 | tf_op jit(solution)/shard_map/ppermute | solution.py:186
  155.0 9.2 %collective-permute-start.18 = (bf16[576,256]{1,0:T(8,128)(2,1)S(1)}, bf16[576,256]{1,0:T(8,128)(2,1)S(1)}, u32[]{:S(2)}, u32[]{:S(2)}) collective-permute-start(bf16[576,256]{1,0:T(8,128)(2,1)S(1)} %get-tuple-element.48), channel_id=1, source_target_pairs={{0,352},{32,0},{64,32},{96,64},{128,96},{160,128},{192,160},{224,1... | collective-permute-start | bytes 884744 | tf_op jit(solution)/shard_map/ppermute | solution.py:186
  (1 other events, 0.7 us)

commit v5 on v4

--- a/solution.py
+++ b/solution.py
@@ -25,7 +25,7 @@
     return pl.BlockSpec(memory_space=space)
 
 
-def pack_kernel(info, tiles, meta, same, other):
+def pack_kernel(info, tiles, meta, y0, y1, y2, y3, same, other):
     slots = tiles.shape[0]
     odd = info[0] == 1
 
@@ -39,6 +39,9 @@
     lax.fori_loop(0, slots, one, 0, unroll=4)
     for ref in (same, other):
         ref[slots] = jnp.broadcast_to(meta[...], (STRIP, TILE)).astype(BF)
+        for d, cot in enumerate((y0, y1, y2, y3)):
+            ref[slots + 1 + 2 * d] = cot[:, :TILE]
+            ref[slots + 2 + 2 * d] = cot[:, TILE:]
 
 
 def live_list(codes, mine, row_of, place_of, table, strips, pool):
@@ -65,7 +68,7 @@
     return count
 
 
-def fwd_kernel(nz, codes, info, s0, s1, s2, s3, feats, o0, o1, o2, o3, table, pool, acc):
+def fwd_kernel(nz, codes, info, s0, s1, s2, s3, feats, o0, o1, o2, o3, cots, table, pool, acc):
     rows = o0.shape[0]
     mine, my_yh = info[1], info[2]
 
@@ -93,13 +96,19 @@
     per = 4 * TILE
     for j, ref in enumerate((o0, o1, o2, o3)):
         ref[...] = acc[j * per : j * per + rows, :].astype(ref.dtype)
+    slots = codes.shape[1]
+    for j, ref in enumerate((s0, s1, s2, s3)):
+        for d in range(4):
+            at = slice((4 * j + d) * STRIP, (4 * j + d + 1) * STRIP)
+            cots[at, :TILE] = ref[slots + 1 + 2 * d]
+            cots[at, TILE:] = ref[slots + 2 + 2 * d]
 
 
 def bwd_kernel(
-    nz, codes, info, s0, s1, s2, s3, a_own, a_other, c0, c1, c2, c3, w, out, keep, up, down,
-    table, pool, agg, ga, acc, gw4, act,
+    nz, codes, info, s0, s1, s2, s3, a_own, a_other, c_own, c_other, w, out, keep, up, down,
+    table, pool, agg, cots, ga, acc, gw4, act,
 ):
-    rows, feat = c0.shape
+    rows, feat = 4 * TILE, w.shape[0]
     mine, col_pos, my_zb, my_x = info[1], info[3], info[4], info[5]
     my_yl, my_core = col_pos >> 1, col_pos & 1
     share = keep.shape[0] - (acc.shape[0] // 3)
@@ -107,19 +116,21 @@
     count = live_list(codes, mine, lambda r: (my_yl - r) & (n_yl - 1), lambda q: q, table, (s0, s1, s2, s3), pool)
     acc[...] = jnp.zeros_like(acc)
     per = 4 * TILE
-    for j, cot in enumerate((c0, c1, c2, c3)):
+    for j in range(4):
         for d in range(n_yl):
             src = pl.ds(pl.multiple_of((((my_yl - d) & (n_yl - 1)) * 4 + j) * STRIP, STRIP), STRIP)
-            for i, ref in enumerate((a_own, a_other)):
+            here = slice((4 * j + d) * STRIP, (4 * j + d + 1) * STRIP)
+            for i, (rows_in, cots_in) in enumerate(((a_own, c_own), (a_other, c_other))):
                 to = pl.multiple_of(j * per + d * TILE + (my_core ^ i) * STRIP, STRIP)
-                agg[pl.ds(to, STRIP), :] = ref[src, :]
+                agg[pl.ds(to, STRIP), :] = rows_in[src, :]
+                cots[pl.ds(to, STRIP), :] = cots_in[here, :]
         block = agg[j * per : j * per + rows, :]
         pre = jnp.dot(block, w[...], preferred_element_type=F32)
         sig = jax.nn.sigmoid(pre)
         if j == 0:
             act[...] = (pre * sig)[:TILE]
         slope = sig * (1.0 + pre * (1.0 - sig))
-        gp = (cot[...].astype(F32) * slope).astype(BF)
+        gp = (cots[j * per : j * per + rows, :].astype(F32) * slope).astype(BF)
         gw4[(my_x - j) & 3] = lax.dot_general(block, gp, (((0,), (0,)), ((), ())), preferred_element_type=F32)
         ga[j * per : j * per + rows, :] = lax.dot_general(
             gp, w[...], (((1,), (1,)), ((), ())), preferred_element_type=F32
@@ -217,35 +228,32 @@
 
     near = jnp.concatenate([own, shift(own, "yh", 1)], axis=0)
 
-    parcel = ((slots + 1, STRIP, TILE), BF)
-    same, other = call(pack_kernel, "pack", [smem, vmem, vmem], [parcel] * 2, [], info, tile_values[0, 0], meta)
+    n_yl = lax.axis_size("yl")
+    cots = [cotangent[0]] + [shift(cotangent[0], "yl", d) for d in range(1, n_yl)]
+
+    parcel = ((slots + 1 + 2 * n_yl, STRIP, TILE), BF)
+    same, other = call(
+        pack_kernel, "pack", [smem] + [vmem] * 6, [parcel] * 2, [], info, tile_values[0, 0], meta, *cots
+    )
     strips = [same] + [shift(same if d == 2 else other, "x", d) for d in (1, 2, 3)]
     codes = jnp.stack([code] + [s[slots, 0, :slots].astype(jnp.int32) for s in strips[1:]])
-
-    pair = lax.all_gather(cotangent[0], "core", axis=0, tiled=True)
-    n_yl = lax.axis_size("yl")
-    pairs = [pair] + [shift(pair, "yl", d) for d in range(1, n_yl)]
-    near, *pairs = lax.optimization_barrier((near, *pairs))
-    block_cot = jnp.concatenate(pairs, axis=0)
-
     column = lax.all_gather(near, Z, axis=0, tiled=True)
-    column, block_cot = lax.optimization_barrier((column, block_cot))
 
     listing = [pltpu.SMEM((3, 4 * slots + STEP), jnp.int32), pltpu.VMEM((4 * slots + 1, STRIP, TILE), BF)]
-    parts = call(
+    *parts, core_cots = call(
         functools.partial(fwd_kernel, nz),
         "forward_tiles",
         [smem, smem] + [vmem] * 5,
-        [((rows, feat), F32)] + [((rows, feat), BF)] * 3,
+        [((rows, feat), F32)] + [((rows, feat), BF)] * 3 + [((4 * n_yl * STRIP, feat), BF)],
         listing + [pltpu.VMEM((16 * TILE, feat), F32)],
         codes, info, *strips, column,
     )
 
     back = [shift(parts[d], "x", -d) for d in (1, 2, 3)]
     block_sum = (parts[0] + (back[0].astype(F32) + back[1].astype(F32) + back[2].astype(F32))).astype(BF)
+    other_cots = shift(core_cots, "core", 1)
+    block_sum, other_cots = lax.optimization_barrier((block_sum, other_cots))
     pieces = lax.all_to_all(block_sum, COL, split_axis=0, concat_axis=0, tiled=True)
-    cots = [block_cot] + [shift(block_cot, "x", d) for d in (1, 2, 3)]
-    pieces, *cots = lax.optimization_barrier((pieces, *cots))
     agg = jnp.sum(pieces.reshape(col_devs, per_dev, feat).astype(F32), axis=0).astype(BF)
     group_agg = jnp.concatenate([agg] + [shift(agg, "x", d) for d in (1, 2, 3)], axis=0)
     core_agg = lax.all_gather(group_agg, "yl", axis=0, tiled=True)
@@ -256,17 +264,18 @@
     output_rows, keep, up, down = call(
         functools.partial(bwd_kernel, nz),
         "backward_tiles",
-        [smem, smem] + [vmem] * 11,
+        [smem, smem] + [vmem] * 9,
         [((per_dev, feat), BF), ((chunk_rows + share, feat), F32)] + [((chunk_rows + 2 * share, feat), BF)] * 2,
         listing
         + [
+            pltpu.VMEM((16 * TILE, feat), BF),
             pltpu.VMEM((16 * TILE, feat), BF),
             pltpu.VMEM((16 * TILE, feat), BF),
             pltpu.VMEM((groups * STRIP, feat), F32),
             pltpu.VMEM((4, feat, feat), F32),
             pltpu.VMEM((TILE, feat), F32),
         ],
-        codes, info, *strips, core_agg, other_agg, *cots, weight,
+        codes, info, *strips, core_agg, other_agg, core_cots, other_cots, weight,
     )
     (chunks,) = call(
         near_kernel,

time: 218 us -> 209 us (0.959)
  blocking collectives: 96 us -> 112 us
  waiting for transfers between devices: 28.4 us -> 13.6 us
  starting transfers between devices: 75.6 us -> 64.8 us
    all_to_all x0 -> x1, blocking collectives: none -> 17.5 us  [on_device(): lax.all_to_all(block_sum, COL, split_axis=0, concat_axis=0, tiled=True)]
    ppermute x19 -> x17, waiting for transfers between devices: 28.4 us -> 13.6 us  [shift(): return lax.ppermute(value, axis, [(i, (i + by) % n) for i in range(n)])]
    all_to_all x1 -> x0, starting transfers between devices: 13.2 us -> none  [on_device(): lax.all_to_all(block_sum, COL, split_axis=0, concat_axis=0, tiled=True)]
    all_to_all x1, blocking collectives: 32.4 us -> 35.6 us  [on_device(): lax.all_to_all(chunks, ('yh', 'za'), split_axis=0, concat_axis=0, tiled=T...]
    all_gather x1, blocking collectives: 19.2 us -> 16 us  [on_device(): grad_weight = lax.all_gather(weight_part, COL, axis=0, tiled=True)]
    ppermute x19 -> x17, starting transfers between devices: 62.3 us -> 64.8 us  [shift(): return lax.ppermute(value, axis, [(i, (i + by) % n) for i in range(n)])]
    all_gather x1 -> x0, blocking collectives: 2.39 us -> none  [on_device(): pair = lax.all_gather(cotangent[0], 'core', axis=0, tiled=True)]
  transfers between devices with their start and end apart: 20 -> 17, of which waited for: 10 -> 6; matrix products, arithmetic and copies ran while one was open for 0% -> 0% of each run, Pallas kernels for 1% -> 1%
where the time goes in v5:
time: 209 us; the launch traced here: 208 us
  blocking collectives  112 us (54%)
  starting transfers between devices  64.8 us (31%)
  waiting for transfers between devices  13.6 us (7%)
  Pallas kernels  11.5 us (6%)
  local copies, waits for them, and re-layouts  4.11 us (2%)
    ppermute x17, starting transfers between devices, shift(): return lax.ppermute(value, axis, [(i, (i + by) % n) for i in range(n)])  64.8 us
    all_to_all x1, blocking collectives, on_device(): lax.all_to_all(chunks, ('yh', 'za'), split_axis=0, concat_axis=0, tiled=T...  35.6 us
    all_gather x1, blocking collectives, on_device(): column = lax.all_gather(near, Z, axis=0, tiled=True)  29.7 us
    all_to_all x1, blocking collectives, on_device(): lax.all_to_all(block_sum, COL, split_axis=0, concat_axis=0, tiled=True)  17.5 us
    all_gather x1, blocking collectives, on_device(): grad_weight = lax.all_gather(weight_part, COL, axis=0, tiled=True)  16 us
    all_gather x1, blocking collectives, on_device(): core_agg = lax.all_gather(group_agg, 'yl', axis=0, tiled=True)  13.6 us
    ppermute x17, waiting for transfers between devices, shift(): return lax.ppermute(value, axis, [(i, (i + by) % n) for i in range(n)])  13.6 us
    pallas_call x5, Pallas kernels, call(): pl.pallas_call(kernel, out_shape=tuple((jax.ShapeDtypeStruct(s, t) for s,...  11.5 us
  transfers between devices with their start and end apart: 17, of which 6 were waited for; matrix products, arithmetic and copies ran while one was open for 0% of the time, Pallas kernels for 1%

profile of v5, /device:TPU:65, one launch (start us, length us, event | category | flops | bytes accessed | tf_op | source)
XLA Modules:
  0.0 208.2 jit_solution(5963031994266617464)
XLA Ops:
  0.6 5.2 %collective-permute-start.2 = (bf16[64,256]{1,0:T(8,128)(2,1)}, bf16[64,256]{1,0:T(8,128)(2,1)S(1)}, u32[]{:S(2)}, u32[]{:S(2)}) collective-permute-start(bf16[64,256]{1,0:T(8,128)(2,1)} %bitcast.37), channel_id=1, source_target_pairs={{0,6},{2,0},{4,2},{6,4},{1,7},{3,1},{5,3},{7,5},{8,14},{10,8},{12,... | collective-permute-start | bytes 98312 | tf_op jit(solution)/shard_map/ppermute | solution.py:197
  5.9 1.9 collective-permute-start.1
  7.8 2.4 %collective-permute-start = (bf16[64,256]{1,0:T(8,128)(2,1)}, bf16[64,256]{1,0:T(8,128)(2,1)S(1)}, u32[]{:S(2)}, u32[]{:S(2)}) collective-permute-start(bf16[64,256]{1,0:T(8,128)(2,1)} %bitcast.39), channel_id=1, source_target_pairs={{0,2},{2,4},{4,6},{6,0},{1,3},{3,5},{5,7},{7,1},{8,10},{10,12},{12... | collective-permute-start | bytes 98312 | tf_op jit(solution)/shard_map/ppermute | solution.py:197
  10.2 5.7 %collective-permute-start.6 = (bf16[64,256]{1,0:T(8,128)(2,1)}, bf16[64,256]{1,0:T(8,128)(2,1)S(1)}, u32[]{:S(2)}, u32[]{:S(2)}) collective-permute-start(bf16[64,256]{1,0:T(8,128)(2,1)} %bitcast.42), channel_id=1, source_target_pairs={{0,384},{384,0},{1,385},{385,1},{2,386},{386,2},{3,387},{387,3},{4... | collective-permute-start | bytes 98312 | tf_op jit(solution)/shard_map/ppermute | solution.py:197
  20.5 4.4 %collective-permute-start.5 = (bf16[41,64,128]{2,1,0:T(8,128)(2,1)S(1)}, bf16[41,64,128]{2,1,0:T(8,128)(2,1)S(1)}, u32[]{:S(2)}, u32[]{:S(2)}) collective-permute-start(bf16[41,64,128]{2,1,0:T(8,128)(2,1)S(1)} %get-tuple-element.18), channel_id=1, source_target_pairs={{0,24},{8,0},{16,8},{24,16},{1,25},{9,1},{17,9},{25,17},{2,26},{10... | collective-permute-start | bytes 2015240 | tf_op jit(solution)/shard_map/ppermute | solution.py:197
  26.8 3.6 %collective-permute-start.4 = (bf16[41,64,128]{2,1,0:T(8,128)(2,1)S(1)}, bf16[41,64,128]{2,1,0:T(8,128)(2,1)S(1)}, u32[]{:S(2)}, u32[]{:S(2)}) collective-permute-start(bf16[41,64,128]{2,1,0:T(8,128)(2,1)S(1)} %get-tuple-element.19.s0), channel_id=1, source_target_pairs={{0,16},{8,24},{16,0},{24,8},{1,17},{9,25},{17,1},{25,9},{2,18},{10... | collective-permute-start | bytes 2015240 | tf_op jit(solution)/shard_map/ppermute | solution.py:197
  30.5 29.7 %all_gather.9.feats = bf16[1536,256]{1,0:T(8,128)(2,1)S(1)} all-gather(bf16[128,256]{1,0:T(8,128)(2,1)S(1)} %pad_maximum_fusion.1), channel_id=1, replica_groups=mesh['yh'=2,'za'=4,'zb'=3,'x'=4,'yl'=4,'core'=2] {'za','zb'}, dimensions={0}, use_global_device_ids=true | all-gather | bytes 851968 | tf_op jit(solution)/shard_map/all_gather | solution.py:240
  60.3 3.9 %forward_tiles.1 = (f32[512,256]{1,0:T(8,128)S(1)}, bf16[512,256]{1,0:T(8,128)(2,1)S(1)}, bf16[512,256]{1,0:T(8,128)(2,1)S(1)}, bf16[512,256]{1,0:T(8,128)(2,1)S(1)}, bf16[1024,256]{1,0:T(8,128)(2,1)S(1)}) custom-call(s32[4,32]{1,0:T(4,128)S(1)} %pad_add_fusion.codes, s32[6]{0:T(128)S(1)} %stack.34.info, bf16[41,64,128]{2,1,0:T(8,128)(2,1)S(1)} %get-tuple-element.19.s0, ...), custom_call_target="tpu_custom_call" | custom-call | tf_op jit(solution)/shard_map/forward_tiles/pallas_call | solution.py:215
  64.2 2.2 %collective-permute-start.7 = (bf16[512,256]{1,0:T(8,128)(2,1)S(1)}, bf16[512,256]{1,0:T(8,128)(2,1)S(1)}, u32[]{:S(2)}, u32[]{:S(2)}) collective-permute-start(bf16[512,256]{1,0:T(8,128)(2,1)S(1)} %get-tuple-element.21), channel_id=1, source_target_pairs={{0,24},{8,0},{16,8},{24,16},{1,25},{9,1},{17,9},{25,17},{2,26},{10... | collective-permute-start | bytes 786440 | tf_op jit(solution)/shard_map/ppermute | solution.py:197
  66.4 4.4 %collective-permute-start.8 = (bf16[512,256]{1,0:T(8,128)(2,1)S(1)}, bf16[512,256]{1,0:T(8,128)(2,1)S(1)}, u32[]{:S(2)}, u32[]{:S(2)}) collective-permute-start(bf16[512,256]{1,0:T(8,128)(2,1)S(1)} %get-tuple-element.22), channel_id=1, source_target_pairs={{0,16},{8,24},{16,0},{24,8},{1,17},{9,25},{17,1},{25,9},{2,18},{10... | collective-permute-start | bytes 786440 | tf_op jit(solution)/shard_map/ppermute | solution.py:197
  72.7 10.0 %collective-permute-start.10 = (bf16[1024,256]{1,0:T(8,128)(2,1)S(1)}, bf16[1024,256]{1,0:T(8,128)(2,1)S(1)}, u32[]{:S(2)}, u32[]{:S(2)}) collective-permute-start(bf16[1024,256]{1,0:T(8,128)(2,1)S(1)} %get-tuple-element.24.c_own), channel_id=1, source_target_pairs={{0,1},{1,0},{2,3},{3,2},{4,5},{5,4},{6,7},{7,6},{8,9},{9,8},{10,11... | collective-permute-start | bytes 1572872 | tf_op jit(solution)/shard_map/ppermute | solution.py:197
  85.0 17.5 %all_to_all.14 = bf16[8,64,256]{2,1,0:T(8,128)(2,1)S(1)} all-to-all(bf16[8,64,256]{2,1,0:T(8,128)(2,1)S(1)} %bitcast.41), channel_id=1, replica_groups=mesh['yh'=2,'za'=4,'zb'=3,'x'=4,'yl'=4,'core'=2] {'yl','core'}, dimensions={0} | all-to-all | bytes 524288 | tf_op jit(solution)/shard_map/all_to_all | solution.py:256
  102.5 2.1 collective-permute-start.13
  104.6 3.1 %collective-permute-start.12 = (bf16[64,256]{1,0:T(8,128)(2,1)S(1)}, bf16[64,256]{1,0:T(8,128)(2,1)S(1)}, u32[]{:S(2)}, u32[]{:S(2)}) collective-permute-start(bf16[64,256]{1,0:T(8,128)(2,1)S(1)} %reduce_sum.12), channel_id=1, source_target_pairs={{0,16},{8,24},{16,0},{24,8},{1,17},{9,25},{17,1},{25,9},{2,18},{10... | collective-permute-start | bytes 98312 | tf_op jit(solution)/shard_map/ppermute | solution.py:197
  107.7 2.5 %collective-permute-start.11 = (bf16[64,256]{1,0:T(8,128)(2,1)S(1)}, bf16[64,256]{1,0:T(8,128)(2,1)S(1)}, u32[]{:S(2)}, u32[]{:S(2)}) collective-permute-start(bf16[64,256]{1,0:T(8,128)(2,1)S(1)} %reduce_sum.12), channel_id=1, source_target_pairs={{0,8},{8,16},{16,24},{24,0},{1,9},{9,17},{17,25},{25,1},{2,10},{10... | collective-permute-start | bytes 98312 | tf_op jit(solution)/shard_map/ppermute | solution.py:197
  110.8 2.8 %collective-permute-done.11 = bf16[64,256]{1,0:T(8,128)(2,1)S(1)} collective-permute-done((bf16[64,256]{1,0:T(8,128)(2,1)S(1)}, bf16[64,256]{1,0:T(8,128)(2,1)S(1)}, u32[]{:S(2)}, u32[]{:S(2)}) %collective-permute-start.11) | collective-permute-done | bytes 32800 | tf_op jit(solution)/shard_map/ppermute | solution.py:197
  113.6 13.6 %all_gather.10.a_own = bf16[1024,256]{1,0:T(8,128)(2,1)S(1)} all-gather(bf16[256,256]{1,0:T(8,128)(2,1)S(1)} %pad_maximum_fusion), channel_id=1, replica_groups=mesh['yh'=2,'za'=4,'zb'=3,'x'=4,'yl'=4,'core'=2] {'yl'}, dimensions={0}, use_global_device_ids=true | all-gather | bytes 655360 | tf_op jit(solution)/shard_map/all_gather | solution.py:259
  127.2 6.9 %collective-permute-start.14 = (bf16[1024,256]{1,0:T(8,128)(2,1)S(1)}, bf16[1024,256]{1,0:T(8,128)(2,1)S(1)}, u32[]{:S(2)}, u32[]{:S(2)}) collective-permute-start(bf16[1024,256]{1,0:T(8,128)(2,1)S(1)} %all_gather.10.a_own), channel_id=1, source_target_pairs={{0,1},{1,0},{2,3},{3,2},{4,5},{5,4},{6,7},{7,6},{8,9},{9,8},{10,11... | collective-permute-start | bytes 1572872 | tf_op jit(solution)/shard_map/ppermute | solution.py:197
  135.6 5.5 %backward_tiles.1 = (bf16[64,256]{1,0:T(8,128)(2,1)}, f32[544,256]{1,0:T(8,128)S(1)}, bf16[576,256]{1,0:T(8,128)(2,1)S(1)}, bf16[576,256]{1,0:T(8,128)(2,1)S(1)}) custom-call(s32[4,32]{1,0:T(4,128)S(1)} %pad_add_fusion.codes, s32[6]{0:T(128)S(1)} %stack.34.info, bf16[41,64,128]{2,1,0:T(8,128)(2,1)S(1)} %get-tuple-element.19.s0, ...), custom_call_target="tpu_custom_call" | custom-call | tf_op jit(solution)/shard_map/backward_tiles/pallas_call | solution.py:215
  141.1 3.3 %collective-permute-start.15 = (bf16[576,256]{1,0:T(8,128)(2,1)S(1)}, bf16[576,256]{1,0:T(8,128)(2,1)S(1)}, u32[]{:S(2)}, u32[]{:S(2)}) collective-permute-start(bf16[576,256]{1,0:T(8,128)(2,1)S(1)} %get-tuple-element.29), channel_id=1, source_target_pairs={{0,32},{32,64},{64,96},{96,128},{128,160},{160,192},{192,224},{224... | collective-permute-start | bytes 884744 | tf_op jit(solution)/shard_map/ppermute | solution.py:197
  144.4 3.3 %collective-permute-start.16 = (bf16[576,256]{1,0:T(8,128)(2,1)S(1)}, bf16[576,256]{1,0:T(8,128)(2,1)S(1)}, u32[]{:S(2)}, u32[]{:S(2)}) collective-permute-start(bf16[576,256]{1,0:T(8,128)(2,1)S(1)} %get-tuple-element.30), channel_id=1, source_target_pairs={{0,352},{32,0},{64,32},{96,64},{128,96},{160,128},{192,160},{224,1... | collective-permute-start | bytes 884744 | tf_op jit(solution)/shard_map/ppermute | solution.py:197
  147.7 5.4 %collective-permute-done.15.up = bf16[576,256]{1,0:T(8,128)(2,1)S(1)} collective-permute-done((bf16[576,256]{1,0:T(8,128)(2,1)S(1)}, bf16[576,256]{1,0:T(8,128)(2,1)S(1)}, u32[]{:S(2)}, u32[]{:S(2)}) %collective-permute-start.15) | collective-permute-done | bytes 294944 | tf_op jit(solution)/shard_map/ppermute | solution.py:197
  155.2 35.6 %all_to_all.15.chunks = bf16[8,128,256]{2,1,0:T(8,128)(2,1)S(1)} all-to-all(bf16[8,128,256]{2,1,0:T(8,128)(2,1)S(1)} %near_sum.1), channel_id=1, replica_groups=mesh['yh'=2,'za'=4,'zb'=3,'x'=4,'yl'=4,'core'=2] {'yh','za'}, dimensions={0} | all-to-all | bytes 1048576 | tf_op jit(solution)/shard_map/all_to_all | solution.py:288
  191.4 16.0 %all_gather.11 = f32[256,256]{1,0:T(8,128)S(1)} all-gather(f32[32,256]{1,0:T(8,128)S(1)} %get-tuple-element.32), channel_id=1, replica_groups=mesh['yh'=2,'za'=4,'zb'=3,'x'=4,'yl'=4,'core'=2] {'yl','core'}, dimensions={0}, use_global_device_ids=true | all-gather | bytes 294912 | tf_op jit(solution)/shard_map/all_gather | solution.py:298
  (49 shorter events, 15.6 us)
Async XLA Ops:
  0.6 16.7 %collective-permute-start.2 = (bf16[64,256]{1,0:T(8,128)(2,1)}, bf16[64,256]{1,0:T(8,128)(2,1)S(1)}, u32[]{:S(2)}, u32[]{:S(2)}) collective-permute-start(bf16[64,256]{1,0:T(8,128)(2,1)} %bitcast.37), channel_id=1, source_target_pairs={{0,6},{2,0},{4,2},{6,4},{1,7},{3,1},{5,3},{7,5},{8,14},{10,8},{12,... | collective-permute-start | bytes 98312 | tf_op jit(solution)/shard_map/ppermute | solution.py:197
  5.9 11.4 %collective-permute-start.1 = (bf16[64,256]{1,0:T(8,128)(2,1)}, bf16[64,256]{1,0:T(8,128)(2,1)S(1)}, u32[]{:S(2)}, u32[]{:S(2)}) collective-permute-start(bf16[64,256]{1,0:T(8,128)(2,1)} %bitcast.38), channel_id=1, source_target_pairs={{0,4},{2,6},{4,0},{6,2},{1,5},{3,7},{5,1},{7,3},{8,12},{10,14},{12... | collective-permute-start | bytes 98312 | tf_op jit(solution)/shard_map/ppermute | solution.py:197
  7.8 9.5 %collective-permute-start = (bf16[64,256]{1,0:T(8,128)(2,1)}, bf16[64,256]{1,0:T(8,128)(2,1)S(1)}, u32[]{:S(2)}, u32[]{:S(2)}) collective-permute-start(bf16[64,256]{1,0:T(8,128)(2,1)} %bitcast.39), channel_id=1, source_target_pairs={{0,2},{2,4},{4,6},{6,0},{1,3},{3,5},{5,7},{7,1},{8,10},{10,12},{12... | collective-permute-start | bytes 98312 | tf_op jit(solution)/shard_map/ppermute | solution.py:197
  10.2 20.3 %collective-permute-start.6 = (bf16[64,256]{1,0:T(8,128)(2,1)}, bf16[64,256]{1,0:T(8,128)(2,1)S(1)}, u32[]{:S(2)}, u32[]{:S(2)}) collective-permute-start(bf16[64,256]{1,0:T(8,128)(2,1)} %bitcast.42), channel_id=1, source_target_pairs={{0,384},{384,0},{1,385},{385,1},{2,386},{386,2},{3,387},{387,3},{4... | collective-permute-start | bytes 98312 | tf_op jit(solution)/shard_map/ppermute | solution.py:197
  16.5 0.7 copy-start.7
  17.2 0.8 copy-start.4
  17.9 1.2 copy-start
  19.1 11.3 %copy-start.5 = (bf16[1,64,256]{2,1,0:T(8,128)(2,1)S(1)}, bf16[1,64,256]{2,1,0:T(8,128)(2,1)}, u32[]{:S(2)}) copy-start(bf16[1,64,256]{2,1,0:T(8,128)(2,1)} %param.7) | copy-start | bytes 98308
  20.5 39.7 %collective-permute-start.5 = (bf16[41,64,128]{2,1,0:T(8,128)(2,1)S(1)}, bf16[41,64,128]{2,1,0:T(8,128)(2,1)S(1)}, u32[]{:S(2)}, u32[]{:S(2)}) collective-permute-start(bf16[41,64,128]{2,1,0:T(8,128)(2,1)S(1)} %get-tuple-element.18), channel_id=1, source_target_pairs={{0,24},{8,0},{16,8},{24,16},{1,25},{9,1},{17,9},{25,17},{2,26},{10... | collective-permute-start | bytes 2015240 | tf_op jit(solution)/shard_map/ppermute | solution.py:197
  24.9 35.3 %collective-permute-start.3 = (bf16[41,64,128]{2,1,0:T(8,128)(2,1)S(1)}, bf16[41,64,128]{2,1,0:T(8,128)(2,1)S(1)}, u32[]{:S(2)}, u32[]{:S(2)}) collective-permute-start(bf16[41,64,128]{2,1,0:T(8,128)(2,1)S(1)} %get-tuple-element.18), channel_id=1, source_target_pairs={{0,8},{8,16},{16,24},{24,0},{1,9},{9,17},{17,25},{25,1},{2,10},{10... | collective-permute-start | bytes 2015240 | tf_op jit(solution)/shard_map/ppermute | solution.py:197
  26.8 33.4 %collective-permute-start.4 = (bf16[41,64,128]{2,1,0:T(8,128)(2,1)S(1)}, bf16[41,64,128]{2,1,0:T(8,128)(2,1)S(1)}, u32[]{:S(2)}, u32[]{:S(2)}) collective-permute-start(bf16[41,64,128]{2,1,0:T(8,128)(2,1)S(1)} %get-tuple-element.19.s0), channel_id=1, source_target_pairs={{0,16},{8,24},{16,0},{24,8},{1,17},{9,25},{17,1},{25,9},{2,18},{10... | collective-permute-start | bytes 2015240 | tf_op jit(solution)/shard_map/ppermute | solution.py:197
  64.2 18.5 %collective-permute-start.7 = (bf16[512,256]{1,0:T(8,128)(2,1)S(1)}, bf16[512,256]{1,0:T(8,128)(2,1)S(1)}, u32[]{:S(2)}, u32[]{:S(2)}) collective-permute-start(bf16[512,256]{1,0:T(8,128)(2,1)S(1)} %get-tuple-element.21), channel_id=1, source_target_pairs={{0,24},{8,0},{16,8},{24,16},{1,25},{9,1},{17,9},{25,17},{2,26},{10... | collective-permute-start | bytes 786440 | tf_op jit(solution)/shard_map/ppermute | solution.py:197
  66.4 16.3 %collective-permute-start.8 = (bf16[512,256]{1,0:T(8,128)(2,1)S(1)}, bf16[512,256]{1,0:T(8,128)(2,1)S(1)}, u32[]{:S(2)}, u32[]{:S(2)}) collective-permute-start(bf16[512,256]{1,0:T(8,128)(2,1)S(1)} %get-tuple-element.22), channel_id=1, source_target_pairs={{0,16},{8,24},{16,0},{24,8},{1,17},{9,25},{17,1},{25,9},{2,18},{10... | collective-permute-start | bytes 786440 | tf_op jit(solution)/shard_map/ppermute | solution.py:197
  70.8 11.9 %collective-permute-start.9 = (bf16[512,256]{1,0:T(8,128)(2,1)S(1)}, bf16[512,256]{1,0:T(8,128)(2,1)S(1)}, u32[]{:S(2)}, u32[]{:S(2)}) collective-permute-start(bf16[512,256]{1,0:T(8,128)(2,1)S(1)} %get-tuple-element.23), channel_id=1, source_target_pairs={{0,8},{8,16},{16,24},{24,0},{1,9},{9,17},{17,25},{25,1},{2,10},{10... | collective-permute-start | bytes 786440 | tf_op jit(solution)/shard_map/ppermute | solution.py:197
  72.7 11.5 %collective-permute-start.10 = (bf16[1024,256]{1,0:T(8,128)(2,1)S(1)}, bf16[1024,256]{1,0:T(8,128)(2,1)S(1)}, u32[]{:S(2)}, u32[]{:S(2)}) collective-permute-start(bf16[1024,256]{1,0:T(8,128)(2,1)S(1)} %get-tuple-element.24.c_own), channel_id=1, source_target_pairs={{0,1},{1,0},{2,3},{3,2},{4,5},{5,4},{6,7},{7,6},{8,9},{9,8},{10,11... | collective-permute-start | bytes 1572872 | tf_op jit(solution)/shard_map/ppermute | solution.py:197
  84.2 0.8 copy-start.1
  102.5 33.1 %copy-start.2 = (bf16[1024,256]{1,0:T(8,128)(2,1)S(1)}, bf16[1024,256]{1,0:T(8,128)(2,1)}, u32[]{:S(2)}) copy-start(bf16[1024,256]{1,0:T(8,128)(2,1)} %copy-done.1) | copy-start | bytes 1572868
  102.5 7.7 %collective-permute-start.13 = (bf16[64,256]{1,0:T(8,128)(2,1)S(1)}, bf16[64,256]{1,0:T(8,128)(2,1)S(1)}, u32[]{:S(2)}, u32[]{:S(2)}) collective-permute-start(bf16[64,256]{1,0:T(8,128)(2,1)S(1)} %reduce_sum.12), channel_id=1, source_target_pairs={{0,24},{8,0},{16,8},{24,16},{1,25},{9,1},{17,9},{25,17},{2,26},{10... | collective-permute-start | bytes 98312 | tf_op jit(solution)/shard_map/ppermute | solution.py:197
  104.6 6.2 %collective-permute-start.12 = (bf16[64,256]{1,0:T(8,128)(2,1)S(1)}, bf16[64,256]{1,0:T(8,128)(2,1)S(1)}, u32[]{:S(2)}, u32[]{:S(2)}) collective-permute-start(bf16[64,256]{1,0:T(8,128)(2,1)S(1)} %reduce_sum.12), channel_id=1, source_target_pairs={{0,16},{8,24},{16,0},{24,8},{1,17},{9,25},{17,1},{25,9},{2,18},{10... | collective-permute-start | bytes 98312 | tf_op jit(solution)/shard_map/ppermute | solution.py:197
  107.7 5.9 %collective-permute-start.11 = (bf16[64,256]{1,0:T(8,128)(2,1)S(1)}, bf16[64,256]{1,0:T(8,128)(2,1)S(1)}, u32[]{:S(2)}, u32[]{:S(2)}) collective-permute-start(bf16[64,256]{1,0:T(8,128)(2,1)S(1)} %reduce_sum.12), channel_id=1, source_target_pairs={{0,8},{8,16},{16,24},{24,0},{1,9},{9,17},{17,25},{25,1},{2,10},{10... | collective-permute-start | bytes 98312 | tf_op jit(solution)/shard_map/ppermute | solution.py:197
  113.6 22.1 %copy-start.3 = (bf16[256,256]{1,0:T(8,128)(2,1)S(1)}, bf16[256,256]{1,0:T(8,128)(2,1)}, u32[]{:S(2)}) copy-start(bf16[256,256]{1,0:T(8,128)(2,1)} %w.1) | copy-start | bytes 393220
  127.2 8.4 %collective-permute-start.14 = (bf16[1024,256]{1,0:T(8,128)(2,1)S(1)}, bf16[1024,256]{1,0:T(8,128)(2,1)S(1)}, u32[]{:S(2)}, u32[]{:S(2)}) collective-permute-start(bf16[1024,256]{1,0:T(8,128)(2,1)S(1)} %all_gather.10.a_own), channel_id=1, source_target_pairs={{0,1},{1,0},{2,3},{3,2},{4,5},{5,4},{6,7},{7,6},{8,9},{9,8},{10,11... | collective-permute-start | bytes 1572872 | tf_op jit(solution)/shard_map/ppermute | solution.py:197
  141.1 12.1 %collective-permute-start.15 = (bf16[576,256]{1,0:T(8,128)(2,1)S(1)}, bf16[576,256]{1,0:T(8,128)(2,1)S(1)}, u32[]{:S(2)}, u32[]{:S(2)}) collective-permute-start(bf16[576,256]{1,0:T(8,128)(2,1)S(1)} %get-tuple-element.29), channel_id=1, source_target_pairs={{0,32},{32,64},{64,96},{96,128},{128,160},{160,192},{192,224},{224... | collective-permute-start | bytes 884744 | tf_op jit(solution)/shard_map/ppermute | solution.py:197
  144.4 10.6 %collective-permute-start.16 = (bf16[576,256]{1,0:T(8,128)(2,1)S(1)}, bf16[576,256]{1,0:T(8,128)(2,1)S(1)}, u32[]{:S(2)}, u32[]{:S(2)}) collective-permute-start(bf16[576,256]{1,0:T(8,128)(2,1)S(1)} %get-tuple-element.30), channel_id=1, source_target_pairs={{0,352},{32,0},{64,32},{96,64},{128,96},{160,128},{192,160},{224,1... | collective-permute-start | bytes 884744 | tf_op jit(solution)/shard_map/ppermute | solution.py:197
  (1 other events, 0.7 us)

commit v6 on v5

--- a/solution.py
+++ b/solution.py
@@ -25,7 +25,7 @@
     return pl.BlockSpec(memory_space=space)
 
 
-def pack_kernel(info, tiles, meta, y0, y1, y2, y3, same, other):
+def pack_kernel(info, tiles, meta, cot, same, other):
     slots = tiles.shape[0]
     odd = info[0] == 1
 
@@ -39,9 +39,8 @@
     lax.fori_loop(0, slots, one, 0, unroll=4)
     for ref in (same, other):
         ref[slots] = jnp.broadcast_to(meta[...], (STRIP, TILE)).astype(BF)
-        for d, cot in enumerate((y0, y1, y2, y3)):
-            ref[slots + 1 + 2 * d] = cot[:, :TILE]
-            ref[slots + 2 + 2 * d] = cot[:, TILE:]
+        ref[slots + 1] = cot[:, :TILE]
+        ref[slots + 2] = cot[:, TILE:]
 
 
 def live_list(codes, mine, row_of, place_of, table, strips, pool):
@@ -68,7 +67,7 @@
     return count
 
 
-def fwd_kernel(nz, codes, info, s0, s1, s2, s3, feats, o0, o1, o2, o3, cots, table, pool, acc):
+def fwd_kernel(nz, codes, info, s0, s1, s2, s3, feats, o0, o1, o2, o3, table, pool, acc):
     rows = o0.shape[0]
     mine, my_yh = info[1], info[2]
 
@@ -96,12 +95,6 @@
     per = 4 * TILE
     for j, ref in enumerate((o0, o1, o2, o3)):
         ref[...] = acc[j * per : j * per + rows, :].astype(ref.dtype)
-    slots = codes.shape[1]
-    for j, ref in enumerate((s0, s1, s2, s3)):
-        for d in range(4):
-            at = slice((4 * j + d) * STRIP, (4 * j + d + 1) * STRIP)
-            cots[at, :TILE] = ref[slots + 1 + 2 * d]
-            cots[at, TILE:] = ref[slots + 2 + 2 * d]
 
 
 def bwd_kernel(
@@ -119,11 +112,10 @@
     for j in range(4):
         for d in range(n_yl):
             src = pl.ds(pl.multiple_of((((my_yl - d) & (n_yl - 1)) * 4 + j) * STRIP, STRIP), STRIP)
-            here = slice((4 * j + d) * STRIP, (4 * j + d + 1) * STRIP)
             for i, (rows_in, cots_in) in enumerate(((a_own, c_own), (a_other, c_other))):
                 to = pl.multiple_of(j * per + d * TILE + (my_core ^ i) * STRIP, STRIP)
                 agg[pl.ds(to, STRIP), :] = rows_in[src, :]
-                cots[pl.ds(to, STRIP), :] = cots_in[here, :]
+                cots[pl.ds(to, STRIP), :] = cots_in[src, :]
         block = agg[j * per : j * per + rows, :]
         pre = jnp.dot(block, w[...], preferred_element_type=F32)
         sig = jax.nn.sigmoid(pre)
@@ -228,34 +220,34 @@
 
     near = jnp.concatenate([own, shift(own, "yh", 1)], axis=0)
 
-    n_yl = lax.axis_size("yl")
-    cots = [cotangent[0]] + [shift(cotangent[0], "yl", d) for d in range(1, n_yl)]
-
-    parcel = ((slots + 1 + 2 * n_yl, STRIP, TILE), BF)
+    parcel = ((slots + 3, STRIP, TILE), BF)
     same, other = call(
-        pack_kernel, "pack", [smem] + [vmem] * 6, [parcel] * 2, [], info, tile_values[0, 0], meta, *cots
+        pack_kernel, "pack", [smem] + [vmem] * 3, [parcel] * 2, [], info, tile_values[0, 0], meta, cotangent[0]
     )
     strips = [same] + [shift(same if d == 2 else other, "x", d) for d in (1, 2, 3)]
     codes = jnp.stack([code] + [s[slots, 0, :slots].astype(jnp.int32) for s in strips[1:]])
+    cots = [jnp.concatenate([s[slots + 1], s[slots + 2]], axis=1) for s in strips]
     column = lax.all_gather(near, Z, axis=0, tiled=True)
 
     listing = [pltpu.SMEM((3, 4 * slots + STEP), jnp.int32), pltpu.VMEM((4 * slots + 1, STRIP, TILE), BF)]
-    *parts, core_cots = call(
+    parts = call(
         functools.partial(fwd_kernel, nz),
         "forward_tiles",
         [smem, smem] + [vmem] * 5,
-        [((rows, feat), F32)] + [((rows, feat), BF)] * 3 + [((4 * n_yl * STRIP, feat), BF)],
+        [((rows, feat), F32)] + [((rows, feat), BF)] * 3,
         listing + [pltpu.VMEM((16 * TILE, feat), F32)],
         codes, info, *strips, column,
     )
 
     back = [shift(parts[d], "x", -d) for d in (1, 2, 3)]
     block_sum = (parts[0] + (back[0].astype(F32) + back[1].astype(F32) + back[2].astype(F32))).astype(BF)
-    other_cots = shift(core_cots, "core", 1)
-    block_sum, other_cots = lax.optimization_barrier((block_sum, other_cots))
+    core_cots = lax.all_gather(jnp.concatenate(cots, axis=0), "yl", axis=0, tiled=True)
+    block_sum, core_cots = lax.optimization_barrier((block_sum, core_cots))
     pieces = lax.all_to_all(block_sum, COL, split_axis=0, concat_axis=0, tiled=True)
     agg = jnp.sum(pieces.reshape(col_devs, per_dev, feat).astype(F32), axis=0).astype(BF)
     group_agg = jnp.concatenate([agg] + [shift(agg, "x", d) for d in (1, 2, 3)], axis=0)
+    other_cots = shift(core_cots, "core", 1)
+    group_agg, other_cots = lax.optimization_barrier((group_agg, other_cots))
     core_agg = lax.all_gather(group_agg, "yl", axis=0, tiled=True)
     other_agg = shift(core_agg, "core", 1)
 

time: 209 us -> 212 us (1.014)
  waiting for transfers between devices: 13.6 us -> 20.4 us
  blocking collectives: 112 us -> 109 us
    all_to_all x1 -> x0, blocking collectives: 17.5 us -> none  [on_device(): lax.all_to_all(block_sum, COL, split_axis=0, concat_axis=0, tiled=True)]
    ppermute x17 -> x14, starting transfers between devices: 64.8 us -> 48.7 us  [shift(): return lax.ppermute(value, axis, [(i, (i + by) % n) for i in range(n)])]
    all_to_all x0 -> x1, starting transfers between devices: none -> 14.9 us  [on_device(): lax.all_to_all(block_sum, COL, split_axis=0, concat_axis=0, tiled=True)]
    all_gather x0 -> x1, blocking collectives: none -> 12.2 us  [on_device(): lax.all_gather(jnp.concatenate(cots, axis=0), 'yl', axis=0, tiled=True)]
    all_to_all x0 -> x1, waiting for transfers between devices: none -> 6.78 us  [on_device(): lax.all_to_all(block_sum, COL, split_axis=0, concat_axis=0, tiled=True)]
    all_to_all x1, blocking collectives: 35.6 us -> 38.3 us  [on_device(): lax.all_to_all(chunks, ('yh', 'za'), split_axis=0, concat_axis=0, tiled=T...]
    ppermute x17 -> x14, waiting for transfers between devices: 13.6 us -> 13.6 us  [shift(): return lax.ppermute(value, axis, [(i, (i + by) % n) for i in range(n)])]
  transfers between devices with their start and end apart: 17 -> 15, of which waited for: 6 -> 6; matrix products, arithmetic and copies ran while one was open for 0% -> 1% of each run, Pallas kernels for 1% -> 0%
where the time goes in v6:
time: 212 us; the launch traced here: 211 us
  blocking collectives  109 us (51%)
  starting transfers between devices  63.6 us (30%)
  waiting for transfers between devices  20.4 us (10%)
  Pallas kernels  11.3 us (5%)
  local copies, waits for them, and re-layouts  2.71 us (1%)
    ppermute x14, starting transfers between devices, shift(): return lax.ppermute(value, axis, [(i, (i + by) % n) for i in range(n)])  48.7 us
    all_to_all x1, blocking collectives, on_device(): lax.all_to_all(chunks, ('yh', 'za'), split_axis=0, concat_axis=0, tiled=T...  38.3 us
    all_gather x1, blocking collectives, on_device(): column = lax.all_gather(near, Z, axis=0, tiled=True)  29.9 us
    all_gather x1, blocking collectives, on_device(): grad_weight = lax.all_gather(weight_part, COL, axis=0, tiled=True)  15.5 us
    all_to_all x1, starting transfers between devices, on_device(): lax.all_to_all(block_sum, COL, split_axis=0, concat_axis=0, tiled=True)  14.9 us
    ppermute x14, waiting for transfers between devices, shift(): return lax.ppermute(value, axis, [(i, (i + by) % n) for i in range(n)])  13.6 us
    all_gather x1, blocking collectives, on_device(): core_agg = lax.all_gather(group_agg, 'yl', axis=0, tiled=True)  13.3 us
    all_gather x1, blocking collectives, on_device(): lax.all_gather(jnp.concatenate(cots, axis=0), 'yl', axis=0, tiled=True)  12.2 us
  transfers between devices with their start and end apart: 15, of which 6 were waited for; matrix products, arithmetic and copies ran while one was open for 1% of the time, Pallas kernels for 0%

profile of v6, /device:TPU:65, one launch (start us, length us, event | category | flops | bytes accessed | tf_op | source)
XLA Modules:
  0.0 210.8 jit_solution(14328895299253796821)
XLA Ops:
  4.6 4.4 %collective-permute-start.2 = (bf16[35,64,128]{2,1,0:T(8,128)(2,1)S(1)}, bf16[35,64,128]{2,1,0:T(8,128)(2,1)S(1)}, u32[]{:S(2)}, u32[]{:S(2)}) collective-permute-start(bf16[35,64,128]{2,1,0:T(8,128)(2,1)S(1)} %get-tuple-element.19), channel_id=1, source_target_pairs={{0,24},{8,0},{16,8},{24,16},{1,25},{9,1},{17,9},{25,17},{2,26},{10... | collective-permute-start | bytes 1720328 | tf_op jit(solution)/shard_map/ppermute | solution.py:189
  9.0 1.9 collective-permute-start
  10.9 7.5 %collective-permute-start.3 = (bf16[64,256]{1,0:T(8,128)(2,1)S(1)}, bf16[64,256]{1,0:T(8,128)(2,1)S(1)}, u32[]{:S(2)}, u32[]{:S(2)}) collective-permute-start(bf16[64,256]{1,0:T(8,128)(2,1)S(1)} %bitcast.54), channel_id=1, source_target_pairs={{0,384},{384,0},{1,385},{385,1},{2,386},{386,2},{3,387},{387,3},{4... | collective-permute-start | bytes 98312 | tf_op jit(solution)/shard_map/ppermute | solution.py:189
  18.4 3.6 %collective-permute-start.1 = (bf16[35,64,128]{2,1,0:T(8,128)(2,1)S(1)}, bf16[35,64,128]{2,1,0:T(8,128)(2,1)S(1)}, u32[]{:S(2)}, u32[]{:S(2)}) collective-permute-start(bf16[35,64,128]{2,1,0:T(8,128)(2,1)S(1)} %get-tuple-element.20.s0), channel_id=1, source_target_pairs={{0,16},{8,24},{16,0},{24,8},{1,17},{9,25},{17,1},{25,9},{2,18},{10... | collective-permute-start | bytes 1720328 | tf_op jit(solution)/shard_map/ppermute | solution.py:189
  22.1 29.9 %all_gather.12.feats = bf16[1536,256]{1,0:T(8,128)(2,1)S(1)} all-gather(bf16[128,256]{1,0:T(8,128)(2,1)S(1)} %pad_maximum_fusion.1), channel_id=1, replica_groups=mesh['yh'=2,'za'=4,'zb'=3,'x'=4,'yl'=4,'core'=2] {'za','zb'}, dimensions={0}, use_global_device_ids=true | all-gather | bytes 851968 | tf_op jit(solution)/shard_map/all_gather | solution.py:230
  52.1 3.8 %forward_tiles.1 = (f32[512,256]{1,0:T(8,128)S(1)}, bf16[512,256]{1,0:T(8,128)(2,1)S(1)}, bf16[512,256]{1,0:T(8,128)(2,1)S(1)}, bf16[512,256]{1,0:T(8,128)(2,1)S(1)}) custom-call(s32[4,32]{1,0:T(4,128)S(1)} %pad_add_fusion.codes, s32[6]{0:T(128)S(1)} %stack.34.info, bf16[35,64,128]{2,1,0:T(8,128)(2,1)S(1)} %get-tuple-element.20.s0, ...), custom_call_target="tpu_custom_call" | custom-call | tf_op jit(solution)/shard_map/forward_tiles/pallas_call | solution.py:207
  55.9 3.5 %collective-permute-start.4 = (bf16[512,256]{1,0:T(8,128)(2,1)S(1)}, bf16[512,256]{1,0:T(8,128)(2,1)S(1)}, u32[]{:S(2)}, u32[]{:S(2)}) collective-permute-start(bf16[512,256]{1,0:T(8,128)(2,1)S(1)} %get-tuple-element.22), channel_id=1, source_target_pairs={{0,24},{8,0},{16,8},{24,16},{1,25},{9,1},{17,9},{25,17},{2,26},{10... | collective-permute-start | bytes 786440 | tf_op jit(solution)/shard_map/ppermute | solution.py:189
  59.4 2.3 %collective-permute-start.5 = (bf16[512,256]{1,0:T(8,128)(2,1)S(1)}, bf16[512,256]{1,0:T(8,128)(2,1)S(1)}, u32[]{:S(2)}, u32[]{:S(2)}) collective-permute-start(bf16[512,256]{1,0:T(8,128)(2,1)S(1)} %get-tuple-element.23), channel_id=1, source_target_pairs={{0,16},{8,24},{16,0},{24,8},{1,17},{9,25},{17,1},{25,9},{2,18},{10... | collective-permute-start | bytes 786440 | tf_op jit(solution)/shard_map/ppermute | solution.py:189
  61.8 2.2 %collective-permute-start.6 = (bf16[512,256]{1,0:T(8,128)(2,1)S(1)}, bf16[512,256]{1,0:T(8,128)(2,1)S(1)}, u32[]{:S(2)}, u32[]{:S(2)}) collective-permute-start(bf16[512,256]{1,0:T(8,128)(2,1)S(1)} %get-tuple-element.24), channel_id=1, source_target_pairs={{0,8},{8,16},{16,24},{24,0},{1,9},{9,17},{17,25},{25,1},{2,10},{10... | collective-permute-start | bytes 786440 | tf_op jit(solution)/shard_map/ppermute | solution.py:189
  64.0 12.2 %all_gather.13.c_own = bf16[1024,256]{1,0:T(8,128)(2,1)S(1)} all-gather(bf16[256,256]{1,0:T(8,128)(2,1)S(1)} %maximum_maximum_fusion), channel_id=1, replica_groups=mesh['yh'=2,'za'=4,'zb'=3,'x'=4,'yl'=4,'core'=2] {'yl'}, dimensions={0}, use_global_device_ids=true | all-gather | bytes 655360 | tf_op jit(solution)/shard_map/all_gather | solution.py:244
  77.0 14.9 %all-to-all-start = ((bf16[8,64,256]{2,1,0:T(8,128)(2,1)}), bf16[8,64,256]{2,1,0:T(8,128)(2,1)}, u32[]{:S(2)}, u32[]{:S(2)}) async-start(bf16[8,64,256]{2,1,0:T(8,128)(2,1)} %bitcast.24), calls=%async_computation | async-start | bytes 524288 | tf_op jit(solution)/shard_map/all_to_all | solution.py:246
  92.0 2.0 collective-permute-start.10
  94.0 6.8 %all-to-all-done = bf16[8,64,256]{2,1,0:T(8,128)(2,1)} async-done(((bf16[8,64,256]{2,1,0:T(8,128)(2,1)}), bf16[8,64,256]{2,1,0:T(8,128)(2,1)}, u32[]{:S(2)}, u32[]{:S(2)}) %all-to-all-start) | async-done | bytes 262176 | tf_op jit(solution)/shard_map/all_to_all | solution.py:246
  101.8 4.9 %collective-permute-start.9 = (bf16[64,256]{1,0:T(8,128)(2,1)S(1)}, bf16[64,256]{1,0:T(8,128)(2,1)S(1)}, u32[]{:S(2)}, u32[]{:S(2)}) collective-permute-start(bf16[64,256]{1,0:T(8,128)(2,1)S(1)} %reduce_sum.12), channel_id=1, source_target_pairs={{0,24},{8,0},{16,8},{24,16},{1,25},{9,1},{17,9},{25,17},{2,26},{10... | collective-permute-start | bytes 98312 | tf_op jit(solution)/shard_map/ppermute | solution.py:189
  108.6 2.5 %collective-permute-start.7 = (bf16[64,256]{1,0:T(8,128)(2,1)S(1)}, bf16[64,256]{1,0:T(8,128)(2,1)S(1)}, u32[]{:S(2)}, u32[]{:S(2)}) collective-permute-start(bf16[64,256]{1,0:T(8,128)(2,1)S(1)} %reduce_sum.12), channel_id=1, source_target_pairs={{0,8},{8,16},{16,24},{24,0},{1,9},{9,17},{17,25},{25,1},{2,10},{10... | collective-permute-start | bytes 98312 | tf_op jit(solution)/shard_map/ppermute | solution.py:189
  112.8 2.3 %collective-permute-done.7 = bf16[64,256]{1,0:T(8,128)(2,1)S(1)} collective-permute-done((bf16[64,256]{1,0:T(8,128)(2,1)S(1)}, bf16[64,256]{1,0:T(8,128)(2,1)S(1)}, u32[]{:S(2)}, u32[]{:S(2)}) %collective-permute-start.7) | collective-permute-done | bytes 32800 | tf_op jit(solution)/shard_map/ppermute | solution.py:189
  115.1 13.3 %all_gather.14.a_own = bf16[1024,256]{1,0:T(8,128)(2,1)S(1)} all-gather(bf16[256,256]{1,0:T(8,128)(2,1)S(1)} %pad_maximum_fusion), channel_id=1, replica_groups=mesh['yh'=2,'za'=4,'zb'=3,'x'=4,'yl'=4,'core'=2] {'yl'}, dimensions={0}, use_global_device_ids=true | all-gather | bytes 655360 | tf_op jit(solution)/shard_map/all_gather | solution.py:251
  128.4 6.5 %collective-permute-start.11 = (bf16[1024,256]{1,0:T(8,128)(2,1)S(1)}, bf16[1024,256]{1,0:T(8,128)(2,1)S(1)}, u32[]{:S(2)}, u32[]{:S(2)}) collective-permute-start(bf16[1024,256]{1,0:T(8,128)(2,1)S(1)} %all_gather.14.a_own), channel_id=1, source_target_pairs={{0,1},{1,0},{2,3},{3,2},{4,5},{5,4},{6,7},{7,6},{8,9},{9,8},{10,11... | collective-permute-start | bytes 1572872 | tf_op jit(solution)/shard_map/ppermute | solution.py:189
  136.4 5.4 %backward_tiles.1 = (bf16[64,256]{1,0:T(8,128)(2,1)}, f32[544,256]{1,0:T(8,128)S(1)}, bf16[576,256]{1,0:T(8,128)(2,1)S(1)}, bf16[576,256]{1,0:T(8,128)(2,1)S(1)}) custom-call(s32[4,32]{1,0:T(4,128)S(1)} %pad_add_fusion.codes, s32[6]{0:T(128)S(1)} %stack.34.info, bf16[35,64,128]{2,1,0:T(8,128)(2,1)S(1)} %get-tuple-element.20.s0, ...), custom_call_target="tpu_custom_call" | custom-call | tf_op jit(solution)/shard_map/backward_tiles/pallas_call | solution.py:207
  141.9 3.6 %collective-permute-start.12 = (bf16[576,256]{1,0:T(8,128)(2,1)S(1)}, bf16[576,256]{1,0:T(8,128)(2,1)S(1)}, u32[]{:S(2)}, u32[]{:S(2)}) collective-permute-start(bf16[576,256]{1,0:T(8,128)(2,1)S(1)} %get-tuple-element.31), channel_id=1, source_target_pairs={{0,32},{32,64},{64,96},{96,128},{128,160},{160,192},{192,224},{224... | collective-permute-start | bytes 884744 | tf_op jit(solution)/shard_map/ppermute | solution.py:189
  147.4 4.3 %collective-permute-done.12.up = bf16[576,256]{1,0:T(8,128)(2,1)S(1)} collective-permute-done((bf16[576,256]{1,0:T(8,128)(2,1)S(1)}, bf16[576,256]{1,0:T(8,128)(2,1)S(1)}, u32[]{:S(2)}, u32[]{:S(2)}) %collective-permute-start.12) | collective-permute-done | bytes 294944 | tf_op jit(solution)/shard_map/ppermute | solution.py:189
  151.7 3.8 %collective-permute-done.13.down = bf16[576,256]{1,0:T(8,128)(2,1)S(1)} collective-permute-done((bf16[576,256]{1,0:T(8,128)(2,1)S(1)}, bf16[576,256]{1,0:T(8,128)(2,1)S(1)}, u32[]{:S(2)}, u32[]{:S(2)}) %collective-permute-start.13) | collective-permute-done | bytes 294944 | tf_op jit(solution)/shard_map/ppermute | solution.py:189
  155.6 38.3 %all_to_all.14.chunks = bf16[8,128,256]{2,1,0:T(8,128)(2,1)S(1)} all-to-all(bf16[8,128,256]{2,1,0:T(8,128)(2,1)S(1)} %near_sum.1), channel_id=1, replica_groups=mesh['yh'=2,'za'=4,'zb'=3,'x'=4,'yl'=4,'core'=2] {'yh','za'}, dimensions={0} | all-to-all | bytes 1048576 | tf_op jit(solution)/shard_map/all_to_all | solution.py:280
  194.6 15.5 %all_gather.15 = f32[256,256]{1,0:T(8,128)S(1)} all-gather(f32[32,256]{1,0:T(8,128)S(1)} %get-tuple-element.34), channel_id=1, replica_groups=mesh['yh'=2,'za'=4,'zb'=3,'x'=4,'yl'=4,'core'=2] {'yl','core'}, dimensions={0}, use_global_device_ids=true | all-gather | bytes 294912 | tf_op jit(solution)/shard_map/all_gather | solution.py:290
  (46 shorter events, 13.8 us)
Async XLA Ops:
  0.6 1.5 copy-start.2
  1.3 0.7 copy-start.4
  1.3 0.7 copy-start.5
  2.1 1.2 copy-start
  3.3 7.6 %copy-start.3 = (bf16[1,64,256]{2,1,0:T(8,128)(2,1)S(1)}, bf16[1,64,256]{2,1,0:T(8,128)(2,1)}, u32[]{:S(2)}) copy-start(bf16[1,64,256]{2,1,0:T(8,128)(2,1)} %param.7) | copy-start | bytes 98308
  4.6 47.4 %collective-permute-start.2 = (bf16[35,64,128]{2,1,0:T(8,128)(2,1)S(1)}, bf16[35,64,128]{2,1,0:T(8,128)(2,1)S(1)}, u32[]{:S(2)}, u32[]{:S(2)}) collective-permute-start(bf16[35,64,128]{2,1,0:T(8,128)(2,1)S(1)} %get-tuple-element.19), channel_id=1, source_target_pairs={{0,24},{8,0},{16,8},{24,16},{1,25},{9,1},{17,9},{25,17},{2,26},{10... | collective-permute-start | bytes 1720328 | tf_op jit(solution)/shard_map/ppermute | solution.py:189
  9.0 43.0 %collective-permute-start = (bf16[35,64,128]{2,1,0:T(8,128)(2,1)S(1)}, bf16[35,64,128]{2,1,0:T(8,128)(2,1)S(1)}, u32[]{:S(2)}, u32[]{:S(2)}) collective-permute-start(bf16[35,64,128]{2,1,0:T(8,128)(2,1)S(1)} %get-tuple-element.19), channel_id=1, source_target_pairs={{0,8},{8,16},{16,24},{24,0},{1,9},{9,17},{17,25},{25,1},{2,10},{10... | collective-permute-start | bytes 1720328 | tf_op jit(solution)/shard_map/ppermute | solution.py:189
  10.9 11.1 %collective-permute-start.3 = (bf16[64,256]{1,0:T(8,128)(2,1)S(1)}, bf16[64,256]{1,0:T(8,128)(2,1)S(1)}, u32[]{:S(2)}, u32[]{:S(2)}) collective-permute-start(bf16[64,256]{1,0:T(8,128)(2,1)S(1)} %bitcast.54), channel_id=1, source_target_pairs={{0,384},{384,0},{1,385},{385,1},{2,386},{386,2},{3,387},{387,3},{4... | collective-permute-start | bytes 98312 | tf_op jit(solution)/shard_map/ppermute | solution.py:189
  18.4 33.6 %collective-permute-start.1 = (bf16[35,64,128]{2,1,0:T(8,128)(2,1)S(1)}, bf16[35,64,128]{2,1,0:T(8,128)(2,1)S(1)}, u32[]{:S(2)}, u32[]{:S(2)}) collective-permute-start(bf16[35,64,128]{2,1,0:T(8,128)(2,1)S(1)} %get-tuple-element.20.s0), channel_id=1, source_target_pairs={{0,16},{8,24},{16,0},{24,8},{1,17},{9,25},{17,1},{25,9},{2,18},{10... | collective-permute-start | bytes 1720328 | tf_op jit(solution)/shard_map/ppermute | solution.py:189
  55.9 20.2 %collective-permute-start.4 = (bf16[512,256]{1,0:T(8,128)(2,1)S(1)}, bf16[512,256]{1,0:T(8,128)(2,1)S(1)}, u32[]{:S(2)}, u32[]{:S(2)}) collective-permute-start(bf16[512,256]{1,0:T(8,128)(2,1)S(1)} %get-tuple-element.22), channel_id=1, source_target_pairs={{0,24},{8,0},{16,8},{24,16},{1,25},{9,1},{17,9},{25,17},{2,26},{10... | collective-permute-start | bytes 786440 | tf_op jit(solution)/shard_map/ppermute | solution.py:189
  59.4 16.7 %collective-permute-start.5 = (bf16[512,256]{1,0:T(8,128)(2,1)S(1)}, bf16[512,256]{1,0:T(8,128)(2,1)S(1)}, u32[]{:S(2)}, u32[]{:S(2)}) collective-permute-start(bf16[512,256]{1,0:T(8,128)(2,1)S(1)} %get-tuple-element.23), channel_id=1, source_target_pairs={{0,16},{8,24},{16,0},{24,8},{1,17},{9,25},{17,1},{25,9},{2,18},{10... | collective-permute-start | bytes 786440 | tf_op jit(solution)/shard_map/ppermute | solution.py:189
  61.8 14.4 %collective-permute-start.6 = (bf16[512,256]{1,0:T(8,128)(2,1)S(1)}, bf16[512,256]{1,0:T(8,128)(2,1)S(1)}, u32[]{:S(2)}, u32[]{:S(2)}) collective-permute-start(bf16[512,256]{1,0:T(8,128)(2,1)S(1)} %get-tuple-element.24), channel_id=1, source_target_pairs={{0,8},{8,16},{16,24},{24,0},{1,9},{9,17},{17,25},{25,1},{2,10},{10... | collective-permute-start | bytes 786440 | tf_op jit(solution)/shard_map/ppermute | solution.py:189
  77.0 23.8 %all-to-all-start = ((bf16[8,64,256]{2,1,0:T(8,128)(2,1)}), bf16[8,64,256]{2,1,0:T(8,128)(2,1)}, u32[]{:S(2)}, u32[]{:S(2)}) async-start(bf16[8,64,256]{2,1,0:T(8,128)(2,1)} %bitcast.24), calls=%async_computation | async-start | bytes 524288 | tf_op jit(solution)/shard_map/all_to_all | solution.py:246
  92.0 23.2 %collective-permute-start.10 = (bf16[1024,256]{1,0:T(8,128)(2,1)S(1)}, bf16[1024,256]{1,0:T(8,128)(2,1)S(1)}, u32[]{:S(2)}, u32[]{:S(2)}) collective-permute-start(bf16[1024,256]{1,0:T(8,128)(2,1)S(1)} %all_gather.13.c_own), channel_id=1, source_target_pairs={{0,1},{1,0},{2,3},{3,2},{4,5},{5,4},{6,7},{7,6},{8,9},{9,8},{10,11... | collective-permute-start | bytes 1572872 | tf_op jit(solution)/shard_map/ppermute | solution.py:189
  101.8 9.3 %collective-permute-start.9 = (bf16[64,256]{1,0:T(8,128)(2,1)S(1)}, bf16[64,256]{1,0:T(8,128)(2,1)S(1)}, u32[]{:S(2)}, u32[]{:S(2)}) collective-permute-start(bf16[64,256]{1,0:T(8,128)(2,1)S(1)} %reduce_sum.12), channel_id=1, source_target_pairs={{0,24},{8,0},{16,8},{24,16},{1,25},{9,1},{17,9},{25,17},{2,26},{10... | collective-permute-start | bytes 98312 | tf_op jit(solution)/shard_map/ppermute | solution.py:189
  106.7 6.2 %collective-permute-start.8 = (bf16[64,256]{1,0:T(8,128)(2,1)S(1)}, bf16[64,256]{1,0:T(8,128)(2,1)S(1)}, u32[]{:S(2)}, u32[]{:S(2)}) collective-permute-start(bf16[64,256]{1,0:T(8,128)(2,1)S(1)} %reduce_sum.12), channel_id=1, source_target_pairs={{0,16},{8,24},{16,0},{24,8},{1,17},{9,25},{17,1},{25,9},{2,18},{10... | collective-permute-start | bytes 98312 | tf_op jit(solution)/shard_map/ppermute | solution.py:189
  108.6 6.5 %collective-permute-start.7 = (bf16[64,256]{1,0:T(8,128)(2,1)S(1)}, bf16[64,256]{1,0:T(8,128)(2,1)S(1)}, u32[]{:S(2)}, u32[]{:S(2)}) collective-permute-start(bf16[64,256]{1,0:T(8,128)(2,1)S(1)} %reduce_sum.12), channel_id=1, source_target_pairs={{0,8},{8,16},{16,24},{24,0},{1,9},{9,17},{17,25},{25,1},{2,10},{10... | collective-permute-start | bytes 98312 | tf_op jit(solution)/shard_map/ppermute | solution.py:189
  115.1 21.3 %copy-start.1 = (bf16[256,256]{1,0:T(8,128)(2,1)S(1)}, bf16[256,256]{1,0:T(8,128)(2,1)}, u32[]{:S(2)}) copy-start(bf16[256,256]{1,0:T(8,128)(2,1)} %w.1) | copy-start | bytes 393220
  128.4 8.0 %collective-permute-start.11 = (bf16[1024,256]{1,0:T(8,128)(2,1)S(1)}, bf16[1024,256]{1,0:T(8,128)(2,1)S(1)}, u32[]{:S(2)}, u32[]{:S(2)}) collective-permute-start(bf16[1024,256]{1,0:T(8,128)(2,1)S(1)} %all_gather.14.a_own), channel_id=1, source_target_pairs={{0,1},{1,0},{2,3},{3,2},{4,5},{5,4},{6,7},{7,6},{8,9},{9,8},{10,11... | collective-permute-start | bytes 1572872 | tf_op jit(solution)/shard_map/ppermute | solution.py:189
  141.9 9.8 %collective-permute-start.12 = (bf16[576,256]{1,0:T(8,128)(2,1)S(1)}, bf16[576,256]{1,0:T(8,128)(2,1)S(1)}, u32[]{:S(2)}, u32[]{:S(2)}) collective-permute-start(bf16[576,256]{1,0:T(8,128)(2,1)S(1)} %get-tuple-element.31), channel_id=1, source_target_pairs={{0,32},{32,64},{64,96},{96,128},{128,160},{160,192},{192,224},{224... | collective-permute-start | bytes 884744 | tf_op jit(solution)/shard_map/ppermute | solution.py:189
  145.5 10.0 %collective-permute-start.13 = (bf16[576,256]{1,0:T(8,128)(2,1)S(1)}, bf16[576,256]{1,0:T(8,128)(2,1)S(1)}, u32[]{:S(2)}, u32[]{:S(2)}) collective-permute-start(bf16[576,256]{1,0:T(8,128)(2,1)S(1)} %get-tuple-element.32), channel_id=1, source_target_pairs={{0,352},{32,0},{64,32},{96,64},{128,96},{160,128},{192,160},{224,1... | collective-permute-start | bytes 884744 | tf_op jit(solution)/shard_map/ppermute | solution.py:189

commit v7 on v6

--- a/solution.py
+++ b/solution.py
@@ -12,7 +12,7 @@
 F32 = jnp.float32
 TILE = 128
 STRIP = 64
-SPLIT = (2, 4, 3, 4, 4, 2)
+SPLIT = (2, 3, 4, 4, 4, 2)
 NAMES = ("yh", "za", "zb", "x", "yl", "core")
 ROW = ("yh", "za", "zb", "x")
 Z = ("za", "zb")
@@ -98,13 +98,13 @@
 
 
 def bwd_kernel(
-    nz, codes, info, s0, s1, s2, s3, a_own, a_other, c_own, c_other, w, out, keep, up, down,
+    nz, codes, info, s0, s1, s2, s3, a_own, a_other, c_own, c_other, w, out, keep, up, down, back,
     table, pool, agg, cots, ga, acc, gw4, act,
 ):
     rows, feat = 4 * TILE, w.shape[0]
     mine, col_pos, my_zb, my_x = info[1], info[3], info[4], info[5]
     my_yl, my_core = col_pos >> 1, col_pos & 1
-    share = keep.shape[0] - (acc.shape[0] // 3)
+    share = keep.shape[0] - (acc.shape[0] // 4)
     n_yl = rows // TILE
     count = live_list(codes, mine, lambda r: (my_yl - r) & (n_yl - 1), lambda q: q, table, (s0, s1, s2, s3), pool)
     acc[...] = jnp.zeros_like(acc)
@@ -145,30 +145,32 @@
     part = (gw4[0, mine_rows, :] + gw4[1, mine_rows, :]) + (gw4[2, mine_rows, :] + gw4[3, mine_rows, :])
     high = part.astype(BF)
     low = (part - high.astype(F32)).astype(BF)
-    n_chunks = acc.shape[0] // (3 * STRIP)
-    n_za = nz // 3
-    for base, ref in ((0, keep), (1, up), (2, down)):
-        which = lax.rem(my_zb + base, 3)
+    n_chunks = acc.shape[0] // (4 * STRIP)
+    n_za = nz // 4
+    for base, ref in ((0, keep), (1, up), (3, down), (2, back)):
+        which = (my_zb + base) & 3
         for i in range(n_chunks):
-            q = (i // n_za) * nz + 3 * (i % n_za) + which
+            q = (i // n_za) * nz + 4 * (i % n_za) + which
             block = acc[pl.ds(pl.multiple_of(q * STRIP, STRIP), STRIP), :]
             ref[i * STRIP : (i + 1) * STRIP, :] = block.astype(ref.dtype)
     end = n_chunks * STRIP
     keep[end:, :] = part
-    for ref in (up, down):
+    for ref in (up, down, back):
         ref[end : end + share, :] = high
         ref[end + share :, :] = low
 
 
-def near_kernel(keep, up, down, chunks):
+def near_kernel(keep, up, down, back, chunks):
     n_chunks = chunks.shape[0]
     end = n_chunks * STRIP
     share = keep.shape[0] - end
     for i in range(n_chunks):
         at = slice(i * STRIP, (i + 1) * STRIP)
-        chunks[i, :STRIP, :] = (keep[at, :] + (up[at, :].astype(F32) + down[at, :].astype(F32))).astype(BF)
+        chunks[i, :STRIP, :] = (
+            (keep[at, :] + up[at, :].astype(F32)) + (down[at, :].astype(F32) + back[at, :].astype(F32))
+        ).astype(BF)
     part = keep[end:, :]
-    for ref in (up, down):
+    for ref in (up, down, back):
         part = part + (ref[end : end + share, :].astype(F32) + ref[end + share :, :].astype(F32))
     high = part.astype(BF)
     low = (part - high.astype(F32)).astype(BF)
@@ -195,7 +197,7 @@
     slots = tile_values.shape[2]
     nz = lax.axis_size(Z)
     groups = 2 * nz
-    n_chunks = groups // 3
+    n_chunks = groups // 4
     col_devs = lax.axis_size(COL)
     rows = per_dev * col_devs
     x = lax.axis_index("x")
@@ -247,17 +249,16 @@
     agg = jnp.sum(pieces.reshape(col_devs, per_dev, feat).astype(F32), axis=0).astype(BF)
     group_agg = jnp.concatenate([agg] + [shift(agg, "x", d) for d in (1, 2, 3)], axis=0)
     other_cots = shift(core_cots, "core", 1)
-    group_agg, other_cots = lax.optimization_barrier((group_agg, other_cots))
     core_agg = lax.all_gather(group_agg, "yl", axis=0, tiled=True)
     other_agg = shift(core_agg, "core", 1)
 
     share = feat // col_devs
     chunk_rows = n_chunks * STRIP
-    output_rows, keep, up, down = call(
+    output_rows, keep, up, down, back = call(
         functools.partial(bwd_kernel, nz),
         "backward_tiles",
         [smem, smem] + [vmem] * 9,
-        [((per_dev, feat), BF), ((chunk_rows + share, feat), F32)] + [((chunk_rows + 2 * share, feat), BF)] * 2,
+        [((per_dev, feat), BF), ((chunk_rows + share, feat), F32)] + [((chunk_rows + 2 * share, feat), BF)] * 3,
         listing
         + [
             pltpu.VMEM((16 * TILE, feat), BF),
@@ -272,10 +273,10 @@
     (chunks,) = call(
         near_kernel,
         "near_sum",
-        [vmem] * 3,
+        [vmem] * 4,
         [((n_chunks, STRIP + 2 * share, feat), BF)],
         [],
-        keep, shift(up, Z, 1), shift(down, Z, -1),
+        keep, shift(up, Z, 1), shift(down, Z, -1), shift(back, Z, -2),
     )
     arrived = lax.all_to_all(chunks, ("yh", "za"), split_axis=0, concat_axis=0, tiled=True)
     node_total = per_dev * lax.axis_size(ROW) * col_devs

time: 212 us -> 208 us (0.981)
  the two profiles are of different devices: /device:TPU:65 before, /device:TPU:1 now
where the time goes in v7:
time: 208 us; the launch traced here: 207 us
  blocking collectives  121 us (58%)
  starting transfers between devices  55.6 us (27%)
  waiting for transfers between devices  14.8 us (7%)
  Pallas kernels  11.3 us (5%)
  local copies, waits for them, and re-layouts  2.71 us (1%)
    ppermute x15, starting transfers between devices, shift(): return lax.ppermute(value, axis, [(i, (i + by) % n) for i in range(n)])  55.6 us
    all_gather x1, blocking collectives, on_device(): column = lax.all_gather(near, Z, axis=0, tiled=True)  32.3 us
    all_to_all x1, blocking collectives, on_device(): lax.all_to_all(chunks, ('yh', 'za'), split_axis=0, concat_axis=0, tiled=T...  25.8 us
    all_to_all x1, blocking collectives, on_device(): lax.all_to_all(block_sum, COL, split_axis=0, concat_axis=0, tiled=True)  21.6 us
    all_gather x1, blocking collectives, on_device(): grad_weight = lax.all_gather(weight_part, COL, axis=0, tiled=True)  15.5 us
    ppermute x15, waiting for transfers between devices, shift(): return lax.ppermute(value, axis, [(i, (i + by) % n) for i in range(n)])  14.8 us
    all_gather x1, blocking collectives, on_device(): core_agg = lax.all_gather(group_agg, 'yl', axis=0, tiled=True)  13.6 us
    all_gather x1, blocking collectives, on_device(): lax.all_gather(jnp.concatenate(cots, axis=0), 'yl', axis=0, tiled=True)  12.1 us
  transfers between devices with their start and end apart: 15, of which 5 were waited for; matrix products, arithmetic and copies ran while one was open for 0% of the time, Pallas kernels for 0%

profile of v7, /device:TPU:1, one launch (start us, length us, event | category | flops | bytes accessed | tf_op | source)
XLA Modules:
  0.0 207.3 jit_solution(12689531456345076266)
XLA Ops:
  4.6 5.2 %collective-permute-start.2 = (bf16[35,64,128]{2,1,0:T(8,128)(2,1)S(1)}, bf16[35,64,128]{2,1,0:T(8,128)(2,1)S(1)}, u32[]{:S(2)}, u32[]{:S(2)}) collective-permute-start(bf16[35,64,128]{2,1,0:T(8,128)(2,1)S(1)} %get-tuple-element.18), channel_id=1, source_target_pairs={{0,24},{8,0},{16,8},{24,16},{1,25},{9,1},{17,9},{25,17},{2,26},{10... | collective-permute-start | bytes 1720328 | tf_op jit(solution)/shard_map/ppermute | solution.py:191
  9.8 1.9 collective-permute-start
  11.8 7.5 %collective-permute-start.3 = (bf16[64,256]{1,0:T(8,128)(2,1)S(1)}, bf16[64,256]{1,0:T(8,128)(2,1)S(1)}, u32[]{:S(2)}, u32[]{:S(2)}) collective-permute-start(bf16[64,256]{1,0:T(8,128)(2,1)S(1)} %bitcast.55), channel_id=1, source_target_pairs={{0,384},{384,0},{1,385},{385,1},{2,386},{386,2},{3,387},{387,3},{4... | collective-permute-start | bytes 98312 | tf_op jit(solution)/shard_map/ppermute | solution.py:191
  19.2 3.6 %collective-permute-start.1 = (bf16[35,64,128]{2,1,0:T(8,128)(2,1)S(1)}, bf16[35,64,128]{2,1,0:T(8,128)(2,1)S(1)}, u32[]{:S(2)}, u32[]{:S(2)}) collective-permute-start(bf16[35,64,128]{2,1,0:T(8,128)(2,1)S(1)} %get-tuple-element.19.s0), channel_id=1, source_target_pairs={{0,16},{8,24},{16,0},{24,8},{1,17},{9,25},{17,1},{25,9},{2,18},{10... | collective-permute-start | bytes 1720328 | tf_op jit(solution)/shard_map/ppermute | solution.py:191
  22.9 32.3 %all_gather.12.feats = bf16[1536,256]{1,0:T(8,128)(2,1)S(1)} all-gather(bf16[128,256]{1,0:T(8,128)(2,1)S(1)} %pad_maximum_fusion.1), channel_id=1, replica_groups=mesh['yh'=2,'za'=3,'zb'=4,'x'=4,'yl'=4,'core'=2] {'za','zb'}, dimensions={0}, use_global_device_ids=true | all-gather | bytes 851968 | tf_op jit(solution)/shard_map/all_gather | solution.py:232
  55.3 3.8 %forward_tiles.1 = (f32[512,256]{1,0:T(8,128)S(1)}, bf16[512,256]{1,0:T(8,128)(2,1)S(1)}, bf16[512,256]{1,0:T(8,128)(2,1)S(1)}, bf16[512,256]{1,0:T(8,128)(2,1)S(1)}) custom-call(s32[4,32]{1,0:T(4,128)S(1)} %pad_add_fusion.codes, s32[6]{0:T(128)S(1)} %stack.34.info, bf16[35,64,128]{2,1,0:T(8,128)(2,1)S(1)} %get-tuple-element.19.s0, ...), custom_call_target="tpu_custom_call" | custom-call | tf_op jit(solution)/shard_map/forward_tiles/pallas_call | solution.py:209
  59.2 2.9 %collective-permute-start.4 = (bf16[512,256]{1,0:T(8,128)(2,1)S(1)}, bf16[512,256]{1,0:T(8,128)(2,1)S(1)}, u32[]{:S(2)}, u32[]{:S(2)}) collective-permute-start(bf16[512,256]{1,0:T(8,128)(2,1)S(1)} %get-tuple-element.21), channel_id=1, source_target_pairs={{0,24},{8,0},{16,8},{24,16},{1,25},{9,1},{17,9},{25,17},{2,26},{10... | collective-permute-start | bytes 786440 | tf_op jit(solution)/shard_map/ppermute | solution.py:191
  62.1 4.1 %collective-permute-start.5 = (bf16[512,256]{1,0:T(8,128)(2,1)S(1)}, bf16[512,256]{1,0:T(8,128)(2,1)S(1)}, u32[]{:S(2)}, u32[]{:S(2)}) collective-permute-start(bf16[512,256]{1,0:T(8,128)(2,1)S(1)} %get-tuple-element.22), channel_id=1, source_target_pairs={{0,16},{8,24},{16,0},{24,8},{1,17},{9,25},{17,1},{25,9},{2,18},{10... | collective-permute-start | bytes 786440 | tf_op jit(solution)/shard_map/ppermute | solution.py:191
  66.1 1.9 collective-permute-start.6
  68.1 12.1 %all_gather.13.c_own = bf16[1024,256]{1,0:T(8,128)(2,1)S(1)} all-gather(bf16[256,256]{1,0:T(8,128)(2,1)S(1)} %maximum_maximum_fusion), channel_id=1, replica_groups=mesh['yh'=2,'za'=3,'zb'=4,'x'=4,'yl'=4,'core'=2] {'yl'}, dimensions={0}, use_global_device_ids=true | all-gather | bytes 655360 | tf_op jit(solution)/shard_map/all_gather | solution.py:246
  80.4 21.6 %all_to_all.14 = bf16[8,64,256]{2,1,0:T(8,128)(2,1)S(1)} all-to-all(bf16[8,64,256]{2,1,0:T(8,128)(2,1)S(1)} %bitcast.54), channel_id=1, replica_groups=mesh['yh'=2,'za'=3,'zb'=4,'x'=4,'yl'=4,'core'=2] {'yl','core'}, dimensions={0} | all-to-all | bytes 524288 | tf_op jit(solution)/shard_map/all_to_all | solution.py:248
  102.0 4.9 %collective-permute-start.9 = (bf16[64,256]{1,0:T(8,128)(2,1)S(1)}, bf16[64,256]{1,0:T(8,128)(2,1)S(1)}, u32[]{:S(2)}, u32[]{:S(2)}) collective-permute-start(bf16[64,256]{1,0:T(8,128)(2,1)S(1)} %reduce_sum.12), channel_id=1, source_target_pairs={{0,24},{8,0},{16,8},{24,16},{1,25},{9,1},{17,9},{25,17},{2,26},{10... | collective-permute-start | bytes 98312 | tf_op jit(solution)/shard_map/ppermute | solution.py:191
  106.9 2.9 %collective-permute-start.8 = (bf16[64,256]{1,0:T(8,128)(2,1)S(1)}, bf16[64,256]{1,0:T(8,128)(2,1)S(1)}, u32[]{:S(2)}, u32[]{:S(2)}) collective-permute-start(bf16[64,256]{1,0:T(8,128)(2,1)S(1)} %reduce_sum.12), channel_id=1, source_target_pairs={{0,16},{8,24},{16,0},{24,8},{1,17},{9,25},{17,1},{25,9},{2,18},{10... | collective-permute-start | bytes 98312 | tf_op jit(solution)/shard_map/ppermute | solution.py:191
  109.8 1.9 collective-permute-start.7
  111.7 3.5 %collective-permute-start.11 = (bf16[1024,256]{1,0:T(8,128)(2,1)S(1)}, bf16[1024,256]{1,0:T(8,128)(2,1)S(1)}, u32[]{:S(2)}, u32[]{:S(2)}) collective-permute-start(bf16[1024,256]{1,0:T(8,128)(2,1)S(1)} %all_gather.13.c_own), channel_id=1, source_target_pairs={{0,1},{1,0},{2,3},{3,2},{4,5},{5,4},{6,7},{7,6},{8,9},{9,8},{10,11... | collective-permute-start | bytes 1572872 | tf_op jit(solution)/shard_map/ppermute | solution.py:191
  115.7 13.6 %all_gather.14.a_own = bf16[1024,256]{1,0:T(8,128)(2,1)S(1)} all-gather(bf16[256,256]{1,0:T(8,128)(2,1)S(1)} %pad_maximum_fusion), channel_id=1, replica_groups=mesh['yh'=2,'za'=3,'zb'=4,'x'=4,'yl'=4,'core'=2] {'yl'}, dimensions={0}, use_global_device_ids=true | all-gather | bytes 655360 | tf_op jit(solution)/shard_map/all_gather | solution.py:252
  129.2 6.9 %collective-permute-start.10 = (bf16[1024,256]{1,0:T(8,128)(2,1)S(1)}, bf16[1024,256]{1,0:T(8,128)(2,1)S(1)}, u32[]{:S(2)}, u32[]{:S(2)}) collective-permute-start(bf16[1024,256]{1,0:T(8,128)(2,1)S(1)} %all_gather.14.a_own), channel_id=1, source_target_pairs={{0,1},{1,0},{2,3},{3,2},{4,5},{5,4},{6,7},{7,6},{8,9},{9,8},{10,11... | collective-permute-start | bytes 1572872 | tf_op jit(solution)/shard_map/ppermute | solution.py:191
  137.7 5.4 %backward_tiles.1 = (bf16[64,256]{1,0:T(8,128)(2,1)}, f32[416,256]{1,0:T(8,128)S(1)}, bf16[448,256]{1,0:T(8,128)(2,1)S(1)}, bf16[448,256]{1,0:T(8,128)(2,1)S(1)}, bf16[448,256]{1,0:T(8,128)(2,1)S(1)}) custom-call(s32[4,32]{1,0:T(4,128)S(1)} %pad_add_fusion.codes, s32[6]{0:T(128)S(1)} %stack.34.info, bf16[35,64,128]{2,1,0:T(8,128)(2,1)S(1)} %get-tuple-element.19.s0, ...), custom_call_target="tpu_custom_call" | custom-call | tf_op jit(solution)/shard_map/backward_tiles/pallas_call | solution.py:209
  143.1 1.9 collective-permute-start.12
  145.1 4.6 %collective-permute-start.13 = (bf16[448,256]{1,0:T(8,128)(2,1)S(1)}, bf16[448,256]{1,0:T(8,128)(2,1)S(1)}, u32[]{:S(2)}, u32[]{:S(2)}) collective-permute-start(bf16[448,256]{1,0:T(8,128)(2,1)S(1)} %get-tuple-element.29), channel_id=1, source_target_pairs={{0,352},{32,0},{64,32},{96,64},{128,96},{160,128},{192,160},{224,1... | collective-permute-start | bytes 688136 | tf_op jit(solution)/shard_map/ppermute | solution.py:191
  149.6 1.9 collective-permute-start.14
  153.2 11.2 %collective-permute-done.14.back = bf16[448,256]{1,0:T(8,128)(2,1)S(1)} collective-permute-done((bf16[448,256]{1,0:T(8,128)(2,1)S(1)}, bf16[448,256]{1,0:T(8,128)(2,1)S(1)}, u32[]{:S(2)}, u32[]{:S(2)}) %collective-permute-start.14) | collective-permute-done | bytes 229408 | tf_op jit(solution)/shard_map/ppermute | solution.py:191
  164.6 25.8 %all_to_all.15.chunks = bf16[6,128,256]{2,1,0:T(8,128)(2,1)S(1)} all-to-all(bf16[6,128,256]{2,1,0:T(8,128)(2,1)S(1)} %near_sum.1), channel_id=1, replica_groups=mesh['yh'=2,'za'=3,'zb'=4,'x'=4,'yl'=4,'core'=2] {'yh','za'}, dimensions={0} | all-to-all | bytes 786432 | tf_op jit(solution)/shard_map/all_to_all | solution.py:281
  191.1 15.5 %all_gather.15 = f32[256,256]{1,0:T(8,128)S(1)} all-gather(f32[32,256]{1,0:T(8,128)S(1)} %get-tuple-element.32), channel_id=1, replica_groups=mesh['yh'=2,'za'=3,'zb'=4,'x'=4,'yl'=4,'core'=2] {'yl','core'}, dimensions={0}, use_global_device_ids=true | all-gather | bytes 294912 | tf_op jit(solution)/shard_map/all_gather | solution.py:291
  (47 shorter events, 8.6 us)
Async XLA Ops:
  0.6 1.5 copy-start.2
  1.3 0.7 copy-start.4
  1.3 0.7 copy-start.5
  2.1 1.2 copy-start
  3.3 8.4 %copy-start.3 = (bf16[1,64,256]{2,1,0:T(8,128)(2,1)S(1)}, bf16[1,64,256]{2,1,0:T(8,128)(2,1)}, u32[]{:S(2)}) copy-start(bf16[1,64,256]{2,1,0:T(8,128)(2,1)} %param.7) | copy-start | bytes 98308
  4.6 50.7 %collective-permute-start.2 = (bf16[35,64,128]{2,1,0:T(8,128)(2,1)S(1)}, bf16[35,64,128]{2,1,0:T(8,128)(2,1)S(1)}, u32[]{:S(2)}, u32[]{:S(2)}) collective-permute-start(bf16[35,64,128]{2,1,0:T(8,128)(2,1)S(1)} %get-tuple-element.18), channel_id=1, source_target_pairs={{0,24},{8,0},{16,8},{24,16},{1,25},{9,1},{17,9},{25,17},{2,26},{10... | collective-permute-start | bytes 1720328 | tf_op jit(solution)/shard_map/ppermute | solution.py:191
  9.8 45.4 %collective-permute-start = (bf16[35,64,128]{2,1,0:T(8,128)(2,1)S(1)}, bf16[35,64,128]{2,1,0:T(8,128)(2,1)S(1)}, u32[]{:S(2)}, u32[]{:S(2)}) collective-permute-start(bf16[35,64,128]{2,1,0:T(8,128)(2,1)S(1)} %get-tuple-element.18), channel_id=1, source_target_pairs={{0,8},{8,16},{16,24},{24,0},{1,9},{9,17},{17,25},{25,1},{2,10},{10... | collective-permute-start | bytes 1720328 | tf_op jit(solution)/shard_map/ppermute | solution.py:191
  11.8 11.1 %collective-permute-start.3 = (bf16[64,256]{1,0:T(8,128)(2,1)S(1)}, bf16[64,256]{1,0:T(8,128)(2,1)S(1)}, u32[]{:S(2)}, u32[]{:S(2)}) collective-permute-start(bf16[64,256]{1,0:T(8,128)(2,1)S(1)} %bitcast.55), channel_id=1, source_target_pairs={{0,384},{384,0},{1,385},{385,1},{2,386},{386,2},{3,387},{387,3},{4... | collective-permute-start | bytes 98312 | tf_op jit(solution)/shard_map/ppermute | solution.py:191
  19.2 36.1 %collective-permute-start.1 = (bf16[35,64,128]{2,1,0:T(8,128)(2,1)S(1)}, bf16[35,64,128]{2,1,0:T(8,128)(2,1)S(1)}, u32[]{:S(2)}, u32[]{:S(2)}) collective-permute-start(bf16[35,64,128]{2,1,0:T(8,128)(2,1)S(1)} %get-tuple-element.19.s0), channel_id=1, source_target_pairs={{0,16},{8,24},{16,0},{24,8},{1,17},{9,25},{17,1},{25,9},{2,18},{10... | collective-permute-start | bytes 1720328 | tf_op jit(solution)/shard_map/ppermute | solution.py:191
  59.2 21.0 %collective-permute-start.4 = (bf16[512,256]{1,0:T(8,128)(2,1)S(1)}, bf16[512,256]{1,0:T(8,128)(2,1)S(1)}, u32[]{:S(2)}, u32[]{:S(2)}) collective-permute-start(bf16[512,256]{1,0:T(8,128)(2,1)S(1)} %get-tuple-element.21), channel_id=1, source_target_pairs={{0,24},{8,0},{16,8},{24,16},{1,25},{9,1},{17,9},{25,17},{2,26},{10... | collective-permute-start | bytes 786440 | tf_op jit(solution)/shard_map/ppermute | solution.py:191
  62.1 18.1 %collective-permute-start.5 = (bf16[512,256]{1,0:T(8,128)(2,1)S(1)}, bf16[512,256]{1,0:T(8,128)(2,1)S(1)}, u32[]{:S(2)}, u32[]{:S(2)}) collective-permute-start(bf16[512,256]{1,0:T(8,128)(2,1)S(1)} %get-tuple-element.22), channel_id=1, source_target_pairs={{0,16},{8,24},{16,0},{24,8},{1,17},{9,25},{17,1},{25,9},{2,18},{10... | collective-permute-start | bytes 786440 | tf_op jit(solution)/shard_map/ppermute | solution.py:191
  66.1 14.1 %collective-permute-start.6 = (bf16[512,256]{1,0:T(8,128)(2,1)S(1)}, bf16[512,256]{1,0:T(8,128)(2,1)S(1)}, u32[]{:S(2)}, u32[]{:S(2)}) collective-permute-start(bf16[512,256]{1,0:T(8,128)(2,1)S(1)} %get-tuple-element.23), channel_id=1, source_target_pairs={{0,8},{8,16},{16,24},{24,0},{1,9},{9,17},{17,25},{25,1},{2,10},{10... | collective-permute-start | bytes 786440 | tf_op jit(solution)/shard_map/ppermute | solution.py:191
  102.0 13.2 %collective-permute-start.9 = (bf16[64,256]{1,0:T(8,128)(2,1)S(1)}, bf16[64,256]{1,0:T(8,128)(2,1)S(1)}, u32[]{:S(2)}, u32[]{:S(2)}) collective-permute-start(bf16[64,256]{1,0:T(8,128)(2,1)S(1)} %reduce_sum.12), channel_id=1, source_target_pairs={{0,24},{8,0},{16,8},{24,16},{1,25},{9,1},{17,9},{25,17},{2,26},{10... | collective-permute-start | bytes 98312 | tf_op jit(solution)/shard_map/ppermute | solution.py:191
  106.9 8.3 %collective-permute-start.8 = (bf16[64,256]{1,0:T(8,128)(2,1)S(1)}, bf16[64,256]{1,0:T(8,128)(2,1)S(1)}, u32[]{:S(2)}, u32[]{:S(2)}) collective-permute-start(bf16[64,256]{1,0:T(8,128)(2,1)S(1)} %reduce_sum.12), channel_id=1, source_target_pairs={{0,16},{8,24},{16,0},{24,8},{1,17},{9,25},{17,1},{25,9},{2,18},{10... | collective-permute-start | bytes 98312 | tf_op jit(solution)/shard_map/ppermute | solution.py:191
  109.8 5.9 %collective-permute-start.7 = (bf16[64,256]{1,0:T(8,128)(2,1)S(1)}, bf16[64,256]{1,0:T(8,128)(2,1)S(1)}, u32[]{:S(2)}, u32[]{:S(2)}) collective-permute-start(bf16[64,256]{1,0:T(8,128)(2,1)S(1)} %reduce_sum.12), channel_id=1, source_target_pairs={{0,8},{8,16},{16,24},{24,0},{1,9},{9,17},{17,25},{25,1},{2,10},{10... | collective-permute-start | bytes 98312 | tf_op jit(solution)/shard_map/ppermute | solution.py:191
  111.7 24.5 %collective-permute-start.11 = (bf16[1024,256]{1,0:T(8,128)(2,1)S(1)}, bf16[1024,256]{1,0:T(8,128)(2,1)S(1)}, u32[]{:S(2)}, u32[]{:S(2)}) collective-permute-start(bf16[1024,256]{1,0:T(8,128)(2,1)S(1)} %all_gather.13.c_own), channel_id=1, source_target_pairs={{0,1},{1,0},{2,3},{3,2},{4,5},{5,4},{6,7},{7,6},{8,9},{9,8},{10,11... | collective-permute-start | bytes 1572872 | tf_op jit(solution)/shard_map/ppermute | solution.py:191
  115.6 22.1 %copy-start.1 = (bf16[256,256]{1,0:T(8,128)(2,1)S(1)}, bf16[256,256]{1,0:T(8,128)(2,1)}, u32[]{:S(2)}) copy-start(bf16[256,256]{1,0:T(8,128)(2,1)} %w.1) | copy-start | bytes 393220
  129.2 8.4 %collective-permute-start.10 = (bf16[1024,256]{1,0:T(8,128)(2,1)S(1)}, bf16[1024,256]{1,0:T(8,128)(2,1)S(1)}, u32[]{:S(2)}, u32[]{:S(2)}) collective-permute-start(bf16[1024,256]{1,0:T(8,128)(2,1)S(1)} %all_gather.14.a_own), channel_id=1, source_target_pairs={{0,1},{1,0},{2,3},{3,2},{4,5},{5,4},{6,7},{7,6},{8,9},{9,8},{10,11... | collective-permute-start | bytes 1572872 | tf_op jit(solution)/shard_map/ppermute | solution.py:191
  143.1 9.3 %collective-permute-start.12 = (bf16[448,256]{1,0:T(8,128)(2,1)S(1)}, bf16[448,256]{1,0:T(8,128)(2,1)S(1)}, u32[]{:S(2)}, u32[]{:S(2)}) collective-permute-start(bf16[448,256]{1,0:T(8,128)(2,1)S(1)} %get-tuple-element.28), channel_id=1, source_target_pairs={{0,32},{32,64},{64,96},{96,128},{128,160},{160,192},{192,224},{224... | collective-permute-start | bytes 688136 | tf_op jit(solution)/shard_map/ppermute | solution.py:191
  145.1 8.2 %collective-permute-start.13 = (bf16[448,256]{1,0:T(8,128)(2,1)S(1)}, bf16[448,256]{1,0:T(8,128)(2,1)S(1)}, u32[]{:S(2)}, u32[]{:S(2)}) collective-permute-start(bf16[448,256]{1,0:T(8,128)(2,1)S(1)} %get-tuple-element.29), channel_id=1, source_target_pairs={{0,352},{32,0},{64,32},{96,64},{128,96},{160,128},{192,160},{224,1... | collective-permute-start | bytes 688136 | tf_op jit(solution)/shard_map/ppermute | solution.py:191
  149.6 14.8 %collective-permute-start.14 = (bf16[448,256]{1,0:T(8,128)(2,1)S(1)}, bf16[448,256]{1,0:T(8,128)(2,1)S(1)}, u32[]{:S(2)}, u32[]{:S(2)}) collective-permute-start(bf16[448,256]{1,0:T(8,128)(2,1)S(1)} %get-tuple-element.30), channel_id=1, source_target_pairs={{0,320},{32,352},{64,0},{96,32},{128,64},{160,96},{192,128},{224,1... | collective-permute-start | bytes 688136 | tf_op jit(solution)/shard_map/ppermute | solution.py:191

commit v8 on v7

--- a/solution.py
+++ b/solution.py
@@ -17,6 +17,7 @@
 ROW = ("yh", "za", "zb", "x")
 Z = ("za", "zb")
 STEP = 4
+LEFT = 16
 COL = ("yl", "core")
 VMEM_LIMIT = 40 * 1024 * 1024
 
@@ -98,7 +99,7 @@
 
 
 def bwd_kernel(
-    nz, codes, info, s0, s1, s2, s3, a_own, a_other, c_own, c_other, w, out, keep, up, down, back,
+    nz, codes, info, s0, s1, s2, s3, r_own, r_other, lefts, w, out, keep, up, down, back,
     table, pool, agg, cots, ga, acc, gw4, act,
 ):
     rows, feat = 4 * TILE, w.shape[0]
@@ -111,11 +112,15 @@
     per = 4 * TILE
     for j in range(4):
         for d in range(n_yl):
-            src = pl.ds(pl.multiple_of((((my_yl - d) & (n_yl - 1)) * 4 + j) * STRIP, STRIP), STRIP)
-            for i, (rows_in, cots_in) in enumerate(((a_own, c_own), (a_other, c_other))):
+            yl = (my_yl - d) & (n_yl - 1)
+            base = yl * (r_own.shape[0] // n_yl) + j * STRIP
+            n = STRIP if j < 3 else STRIP - LEFT
+            for i, ref in enumerate((r_own, r_other)):
                 to = pl.multiple_of(j * per + d * TILE + (my_core ^ i) * STRIP, STRIP)
-                agg[pl.ds(to, STRIP), :] = rows_in[src, :]
-                cots[pl.ds(to, STRIP), :] = cots_in[src, :]
+                agg[pl.ds(to, STRIP), :] = ref[pl.ds(pl.multiple_of(base, LEFT), STRIP), :]
+                cots[pl.ds(to, n), :] = ref[pl.ds(pl.multiple_of(base + 4 * STRIP, LEFT), n), :]
+                if n < STRIP:
+                    cots[pl.ds(pl.multiple_of(to + n, LEFT), LEFT), :] = lefts[yl * 2 + (my_core ^ i)]
         block = agg[j * per : j * per + rows, :]
         pre = jnp.dot(block, w[...], preferred_element_type=F32)
         sig = jax.nn.sigmoid(pre)
@@ -243,21 +248,23 @@
 
     back = [shift(parts[d], "x", -d) for d in (1, 2, 3)]
     block_sum = (parts[0] + (back[0].astype(F32) + back[1].astype(F32) + back[2].astype(F32))).astype(BF)
-    core_cots = lax.all_gather(jnp.concatenate(cots, axis=0), "yl", axis=0, tiled=True)
-    block_sum, core_cots = lax.optimization_barrier((block_sum, core_cots))
-    pieces = lax.all_to_all(block_sum, COL, split_axis=0, concat_axis=0, tiled=True)
-    agg = jnp.sum(pieces.reshape(col_devs, per_dev, feat).astype(F32), axis=0).astype(BF)
-    group_agg = jnp.concatenate([agg] + [shift(agg, "x", d) for d in (1, 2, 3)], axis=0)
-    other_cots = shift(core_cots, "core", 1)
-    core_agg = lax.all_gather(group_agg, "yl", axis=0, tiled=True)
-    other_agg = shift(core_agg, "core", 1)
+    cot_rows = jnp.concatenate(cots, axis=0)
+    left = jnp.broadcast_to(cot_rows[4 * STRIP - LEFT :][None], (col_devs, LEFT, feat))
+    sent = jnp.concatenate([block_sum.reshape(col_devs, per_dev, feat), left], axis=1)
+    pieces = lax.all_to_all(sent, COL, split_axis=0, concat_axis=0, tiled=True)
+    agg = jnp.sum(pieces[:, :per_dev].astype(F32), axis=0).astype(BF)
+    lefts = pieces[:, per_dev:]
+    group_agg = [agg] + [shift(agg, "x", d) for d in (1, 2, 3)]
+    group_rows = jnp.concatenate(group_agg + [cot_rows[: 4 * STRIP - LEFT]], axis=0)
+    core_rows = lax.all_gather(group_rows, "yl", axis=0, tiled=True)
+    other_rows = shift(core_rows, "core", 1)
 
     share = feat // col_devs
     chunk_rows = n_chunks * STRIP
     output_rows, keep, up, down, back = call(
         functools.partial(bwd_kernel, nz),
         "backward_tiles",
-        [smem, smem] + [vmem] * 9,
+        [smem, smem] + [vmem] * 8,
         [((per_dev, feat), BF), ((chunk_rows + share, feat), F32)] + [((chunk_rows + 2 * share, feat), BF)] * 3,
         listing
         + [
@@ -268,7 +275,7 @@
             pltpu.VMEM((4, feat, feat), F32),
             pltpu.VMEM((TILE, feat), F32),
         ],
-        codes, info, *strips, core_agg, other_agg, core_cots, other_cots, weight,
+        codes, info, *strips, core_rows, other_rows, lefts, weight,
     )
     (chunks,) = call(
         near_kernel,

time: 208 us -> 205 us (0.986)
  blocking collectives: 121 us -> 91.8 us
  waiting for transfers between devices: 14.8 us -> 33.5 us
  starting transfers between devices: 55.6 us -> 61.2 us
    all_to_all x1 -> x0, blocking collectives: 21.6 us -> none  [on_device(): lax.all_to_all(block_sum, COL, split_axis=0, concat_axis=0, tiled=True)]
    all_to_all x0 -> x1, starting transfers between devices: none -> 12.1 us  [on_device(): pieces = lax.all_to_all(sent, COL, split_axis=0, concat_axis=0, tiled=True)]
    all_to_all x0 -> x1, waiting for transfers between devices: none -> 10 us  [on_device(): pieces = lax.all_to_all(sent, COL, split_axis=0, concat_axis=0, tiled=True)]
    ppermute x15 -> x14, waiting for transfers between devices: 14.8 us -> 23.4 us  [shift(): return lax.ppermute(value, axis, [(i, (i + by) % n) for i in range(n)])]
    all_gather x2 -> x1, blocking collectives: 25.7 us -> 18.6 us  [on_device(): core_rows = lax.all_gather(group_rows, 'yl', axis=0, tiled=True)]
    ppermute x15 -> x14, starting transfers between devices: 55.6 us -> 49.2 us  [shift(): return lax.ppermute(value, axis, [(i, (i + by) % n) for i in range(n)])]
    all_to_all x1, blocking collectives: 25.8 us -> 22 us  [on_device(): lax.all_to_all(chunks, ('yh', 'za'), split_axis=0, concat_axis=0, tiled=T...]
    all_gather x1, blocking collectives: 15.5 us -> 18.9 us  [on_device(): grad_weight = lax.all_gather(weight_part, COL, axis=0, tiled=True)]
  transfers between devices with their start and end apart: 15 -> 15, of which waited for: 5 -> 8; matrix products, arithmetic and copies ran while one was open for 0% -> 0% of each run, Pallas kernels for 0% -> 0%
where the time goes in v8:
time: 205 us; the launch traced here: 204 us
  blocking collectives  91.8 us (45%)
  starting transfers between devices  61.2 us (30%)
  waiting for transfers between devices  33.5 us (16%)
  Pallas kernels  12.2 us (6%)
  local copies, waits for them, and re-layouts  2.73 us (1%)
    ppermute x14, starting transfers between devices, shift(): return lax.ppermute(value, axis, [(i, (i + by) % n) for i in range(n)])  49.2 us
    all_gather x1, blocking collectives, on_device(): column = lax.all_gather(near, Z, axis=0, tiled=True)  32.3 us
    ppermute x14, waiting for transfers between devices, shift(): return lax.ppermute(value, axis, [(i, (i + by) % n) for i in range(n)])  23.4 us
    all_to_all x1, blocking collectives, on_device(): lax.all_to_all(chunks, ('yh', 'za'), split_axis=0, concat_axis=0, tiled=T...  22 us
    all_gather x1, blocking collectives, on_device(): grad_weight = lax.all_gather(weight_part, COL, axis=0, tiled=True)  18.9 us
    all_gather x1, blocking collectives, on_device(): core_rows = lax.all_gather(group_rows, 'yl', axis=0, tiled=True)  18.6 us
    pallas_call x5, Pallas kernels, call(): pl.pallas_call(kernel, out_shape=tuple((jax.ShapeDtypeStruct(s, t) for s,...  12.2 us
    all_to_all x1, starting transfers between devices, on_device(): pieces = lax.all_to_all(sent, COL, split_axis=0, concat_axis=0, tiled=True)  12.1 us
  transfers between devices with their start and end apart: 15, of which 8 were waited for; matrix products, arithmetic and copies ran while one was open for 0% of the time, Pallas kernels for 0%

profile of v8, /device:TPU:1, one launch (start us, length us, event | category | flops | bytes accessed | tf_op | source)
XLA Modules:
  0.0 204.1 jit_solution(16780482442515457039)
XLA Ops:
  4.6 5.2 %collective-permute-start.2 = (bf16[35,64,128]{2,1,0:T(8,128)(2,1)S(1)}, bf16[35,64,128]{2,1,0:T(8,128)(2,1)S(1)}, u32[]{:S(2)}, u32[]{:S(2)}) collective-permute-start(bf16[35,64,128]{2,1,0:T(8,128)(2,1)S(1)} %get-tuple-element.16), channel_id=1, source_target_pairs={{0,24},{8,0},{16,8},{24,16},{1,25},{9,1},{17,9},{25,17},{2,26},{10... | collective-permute-start | bytes 1720328 | tf_op jit(solution)/shard_map/ppermute | solution.py:196
  11.8 7.5 %collective-permute-start.3 = (bf16[64,256]{1,0:T(8,128)(2,1)S(1)}, bf16[64,256]{1,0:T(8,128)(2,1)S(1)}, u32[]{:S(2)}, u32[]{:S(2)}) collective-permute-start(bf16[64,256]{1,0:T(8,128)(2,1)S(1)} %bitcast.55), channel_id=1, source_target_pairs={{0,384},{384,0},{1,385},{385,1},{2,386},{386,2},{3,387},{387,3},{4... | collective-permute-start | bytes 98312 | tf_op jit(solution)/shard_map/ppermute | solution.py:196
  19.2 3.6 %collective-permute-start.1 = (bf16[35,64,128]{2,1,0:T(8,128)(2,1)S(1)}, bf16[35,64,128]{2,1,0:T(8,128)(2,1)S(1)}, u32[]{:S(2)}, u32[]{:S(2)}) collective-permute-start(bf16[35,64,128]{2,1,0:T(8,128)(2,1)S(1)} %get-tuple-element.17.s0), channel_id=1, source_target_pairs={{0,16},{8,24},{16,0},{24,8},{1,17},{9,25},{17,1},{25,9},{2,18},{10... | collective-permute-start | bytes 1720328 | tf_op jit(solution)/shard_map/ppermute | solution.py:196
  22.9 32.3 %all_gather.9.feats = bf16[1536,256]{1,0:T(8,128)(2,1)S(1)} all-gather(bf16[128,256]{1,0:T(8,128)(2,1)S(1)} %pad_maximum_fusion.5), channel_id=1, replica_groups=mesh['yh'=2,'za'=3,'zb'=4,'x'=4,'yl'=4,'core'=2] {'za','zb'}, dimensions={0}, use_global_device_ids=true | all-gather | bytes 851968 | tf_op jit(solution)/shard_map/all_gather | solution.py:237
  55.3 4.4 %forward_tiles.1 = (f32[512,256]{1,0:T(8,128)S(1)}, bf16[512,256]{1,0:T(8,128)(2,1)S(1)}, bf16[512,256]{1,0:T(8,128)(2,1)S(1)}, bf16[512,256]{1,0:T(8,128)(2,1)S(1)}) custom-call(s32[4,32]{1,0:T(4,128)S(1)} %pad_add_fusion.codes, s32[6]{0:T(128)S(1)} %stack.34.info, bf16[35,64,128]{2,1,0:T(8,128)(2,1)S(1)} %get-tuple-element.17.s0, ...), custom_call_target="tpu_custom_call" | custom-call | tf_op jit(solution)/shard_map/forward_tiles/pallas_call | solution.py:214
  59.7 2.6 %collective-permute-start.4 = (bf16[512,256]{1,0:T(8,128)(2,1)S(1)}, bf16[512,256]{1,0:T(8,128)(2,1)S(1)}, u32[]{:S(2)}, u32[]{:S(2)}) collective-permute-start(bf16[512,256]{1,0:T(8,128)(2,1)S(1)} %get-tuple-element.19), channel_id=1, source_target_pairs={{0,24},{8,0},{16,8},{24,16},{1,25},{9,1},{17,9},{25,17},{2,26},{10... | collective-permute-start | bytes 786440 | tf_op jit(solution)/shard_map/ppermute | solution.py:196
  62.3 4.3 %collective-permute-start.5 = (bf16[512,256]{1,0:T(8,128)(2,1)S(1)}, bf16[512,256]{1,0:T(8,128)(2,1)S(1)}, u32[]{:S(2)}, u32[]{:S(2)}) collective-permute-start(bf16[512,256]{1,0:T(8,128)(2,1)S(1)} %get-tuple-element.20), channel_id=1, source_target_pairs={{0,16},{8,24},{16,0},{24,8},{1,17},{9,25},{17,1},{25,9},{2,18},{10... | collective-permute-start | bytes 786440 | tf_op jit(solution)/shard_map/ppermute | solution.py:196
  66.6 1.9 collective-permute-start.6
  68.6 2.3 %collective-permute-done.5 = bf16[512,256]{1,0:T(8,128)(2,1)S(1)} collective-permute-done((bf16[512,256]{1,0:T(8,128)(2,1)S(1)}, bf16[512,256]{1,0:T(8,128)(2,1)S(1)}, u32[]{:S(2)}, u32[]{:S(2)}) %collective-permute-start.5) | collective-permute-done | bytes 262176 | tf_op jit(solution)/shard_map/ppermute | solution.py:196
  70.9 4.0 %collective-permute-done.6 = bf16[512,256]{1,0:T(8,128)(2,1)S(1)} collective-permute-done((bf16[512,256]{1,0:T(8,128)(2,1)S(1)}, bf16[512,256]{1,0:T(8,128)(2,1)S(1)}, u32[]{:S(2)}, u32[]{:S(2)}) %collective-permute-start.6) | collective-permute-done | bytes 262176 | tf_op jit(solution)/shard_map/ppermute | solution.py:196
  75.9 12.1 %all-to-all-start = ((bf16[8,80,256]{2,1,0:T(8,128)(2,1)}), bf16[8,80,256]{2,1,0:T(8,128)(2,1)S(1)}, u32[]{:S(2)}, u32[]{:S(2)}) async-start(bf16[8,80,256]{2,1,0:T(8,128)(2,1)} %pad_maximum_fusion), calls=%async_computation | async-start | bytes 655360 | tf_op jit(solution)/shard_map/all_to_all | solution.py:254
  88.0 10.0 %all-to-all-done = bf16[8,80,256]{2,1,0:T(8,128)(2,1)S(1)} async-done(((bf16[8,80,256]{2,1,0:T(8,128)(2,1)}), bf16[8,80,256]{2,1,0:T(8,128)(2,1)S(1)}, u32[]{:S(2)}, u32[]{:S(2)}) %all-to-all-start) | async-done | bytes 327712 | tf_op jit(solution)/shard_map/all_to_all | solution.py:254
  100.0 3.1 %collective-permute-start.8 = (bf16[64,256]{1,0:T(8,128)(2,1)S(1)}, bf16[64,256]{1,0:T(8,128)(2,1)S(1)}, u32[]{:S(2)}, u32[]{:S(2)}) collective-permute-start(bf16[64,256]{1,0:T(8,128)(2,1)S(1)} %slice_reduce_fusion), channel_id=1, source_target_pairs={{0,16},{8,24},{16,0},{24,8},{1,17},{9,25},{17,1},{25,9},{2,18},{10... | collective-permute-start | bytes 98312 | tf_op jit(solution)/shard_map/ppermute | solution.py:196
  103.1 2.4 %collective-permute-start.7 = (bf16[64,256]{1,0:T(8,128)(2,1)S(1)}, bf16[64,256]{1,0:T(8,128)(2,1)S(1)}, u32[]{:S(2)}, u32[]{:S(2)}) collective-permute-start(bf16[64,256]{1,0:T(8,128)(2,1)S(1)} %slice_reduce_fusion), channel_id=1, source_target_pairs={{0,8},{8,16},{16,24},{24,0},{1,9},{9,17},{17,25},{25,1},{2,10},{10... | collective-permute-start | bytes 98312 | tf_op jit(solution)/shard_map/ppermute | solution.py:196
  105.6 3.4 %collective-permute-done.7 = bf16[64,256]{1,0:T(8,128)(2,1)S(1)} collective-permute-done((bf16[64,256]{1,0:T(8,128)(2,1)S(1)}, bf16[64,256]{1,0:T(8,128)(2,1)S(1)}, u32[]{:S(2)}, u32[]{:S(2)}) %collective-permute-start.7) | collective-permute-done | bytes 32800 | tf_op jit(solution)/shard_map/ppermute | solution.py:196
  109.0 18.6 %all_gather.10.r_own = bf16[1984,256]{1,0:T(8,128)(2,1)S(1)} all-gather(bf16[496,256]{1,0:T(8,128)(2,1)S(1)} %fusion.1), channel_id=1, replica_groups=mesh['yh'=2,'za'=3,'zb'=4,'x'=4,'yl'=4,'core'=2] {'yl'}, dimensions={0}, use_global_device_ids=true | all-gather | bytes 1269760 | tf_op jit(solution)/shard_map/all_gather | solution.py:259
  127.6 6.2 %collective-permute-start.10 = (bf16[1984,256]{1,0:T(8,128)(2,1)S(1)}, bf16[1984,256]{1,0:T(8,128)(2,1)S(1)}, u32[]{:S(2)}, u32[]{:S(2)}) collective-permute-start(bf16[1984,256]{1,0:T(8,128)(2,1)S(1)} %all_gather.10.r_own), channel_id=1, source_target_pairs={{0,1},{1,0},{2,3},{3,2},{4,5},{5,4},{6,7},{7,6},{8,9},{9,8},{10,11... | collective-permute-start | bytes 3047432 | tf_op jit(solution)/shard_map/ppermute | solution.py:196
  133.8 2.2 %collective-permute-done.10.r_other = bf16[1984,256]{1,0:T(8,128)(2,1)S(1)} collective-permute-done((bf16[1984,256]{1,0:T(8,128)(2,1)S(1)}, bf16[1984,256]{1,0:T(8,128)(2,1)S(1)}, u32[]{:S(2)}, u32[]{:S(2)}) %collective-permute-start.10) | collective-permute-done | bytes 1015840 | tf_op jit(solution)/shard_map/ppermute | solution.py:196
  136.0 5.8 %backward_tiles.1 = (bf16[64,256]{1,0:T(8,128)(2,1)}, f32[416,256]{1,0:T(8,128)S(1)}, bf16[448,256]{1,0:T(8,128)(2,1)S(1)}, bf16[448,256]{1,0:T(8,128)(2,1)S(1)}, bf16[448,256]{1,0:T(8,128)(2,1)S(1)}) custom-call(s32[4,32]{1,0:T(4,128)S(1)} %pad_add_fusion.codes, s32[6]{0:T(128)S(1)} %stack.34.info, bf16[35,64,128]{2,1,0:T(8,128)(2,1)S(1)} %get-tuple-element.17.s0, ...), custom_call_target="tpu_custom_call" | custom-call | tf_op jit(solution)/shard_map/backward_tiles/pallas_call | solution.py:214
  143.8 4.6 %collective-permute-start.12 = (bf16[448,256]{1,0:T(8,128)(2,1)S(1)}, bf16[448,256]{1,0:T(8,128)(2,1)S(1)}, u32[]{:S(2)}, u32[]{:S(2)}) collective-permute-start(bf16[448,256]{1,0:T(8,128)(2,1)S(1)} %get-tuple-element.25), channel_id=1, source_target_pairs={{0,352},{32,0},{64,32},{96,64},{128,96},{160,128},{192,160},{224,1... | collective-permute-start | bytes 688136 | tf_op jit(solution)/shard_map/ppermute | solution.py:196
  148.4 1.9 collective-permute-start.13
  152.2 9.5 %collective-permute-done.13.back = bf16[448,256]{1,0:T(8,128)(2,1)S(1)} collective-permute-done((bf16[448,256]{1,0:T(8,128)(2,1)S(1)}, bf16[448,256]{1,0:T(8,128)(2,1)S(1)}, u32[]{:S(2)}, u32[]{:S(2)}) %collective-permute-start.13) | collective-permute-done | bytes 229408 | tf_op jit(solution)/shard_map/ppermute | solution.py:196
  161.9 22.0 %all_to_all.10.chunks = bf16[6,128,256]{2,1,0:T(8,128)(2,1)S(1)} all-to-all(bf16[6,128,256]{2,1,0:T(8,128)(2,1)S(1)} %near_sum.1), channel_id=1, replica_groups=mesh['yh'=2,'za'=3,'zb'=4,'x'=4,'yl'=4,'core'=2] {'yh','za'}, dimensions={0} | all-to-all | bytes 786432 | tf_op jit(solution)/shard_map/all_to_all | solution.py:288
  184.5 18.9 %all_gather.11 = f32[256,256]{1,0:T(8,128)S(1)} all-gather(f32[32,256]{1,0:T(8,128)S(1)} %get-tuple-element.28), channel_id=1, replica_groups=mesh['yh'=2,'za'=3,'zb'=4,'x'=4,'yl'=4,'core'=2] {'yl','core'}, dimensions={0}, use_global_device_ids=true | all-gather | bytes 294912 | tf_op jit(solution)/shard_map/all_gather | solution.py:298
  (52 shorter events, 13.5 us)
Async XLA Ops:
  0.6 1.5 copy-start.2
  1.3 0.7 copy-start.4
  1.3 0.7 copy-start.5
  2.1 1.2 copy-start
  3.3 8.4 %copy-start.3 = (bf16[1,64,256]{2,1,0:T(8,128)(2,1)S(1)}, bf16[1,64,256]{2,1,0:T(8,128)(2,1)}, u32[]{:S(2)}) copy-start(bf16[1,64,256]{2,1,0:T(8,128)(2,1)} %param.7) | copy-start | bytes 98308
  4.6 50.6 %collective-permute-start.2 = (bf16[35,64,128]{2,1,0:T(8,128)(2,1)S(1)}, bf16[35,64,128]{2,1,0:T(8,128)(2,1)S(1)}, u32[]{:S(2)}, u32[]{:S(2)}) collective-permute-start(bf16[35,64,128]{2,1,0:T(8,128)(2,1)S(1)} %get-tuple-element.16), channel_id=1, source_target_pairs={{0,24},{8,0},{16,8},{24,16},{1,25},{9,1},{17,9},{25,17},{2,26},{10... | collective-permute-start | bytes 1720328 | tf_op jit(solution)/shard_map/ppermute | solution.py:196
  9.8 45.4 %collective-permute-start = (bf16[35,64,128]{2,1,0:T(8,128)(2,1)S(1)}, bf16[35,64,128]{2,1,0:T(8,128)(2,1)S(1)}, u32[]{:S(2)}, u32[]{:S(2)}) collective-permute-start(bf16[35,64,128]{2,1,0:T(8,128)(2,1)S(1)} %get-tuple-element.16), channel_id=1, source_target_pairs={{0,8},{8,16},{16,24},{24,0},{1,9},{9,17},{17,25},{25,1},{2,10},{10... | collective-permute-start | bytes 1720328 | tf_op jit(solution)/shard_map/ppermute | solution.py:196
  11.8 11.1 %collective-permute-start.3 = (bf16[64,256]{1,0:T(8,128)(2,1)S(1)}, bf16[64,256]{1,0:T(8,128)(2,1)S(1)}, u32[]{:S(2)}, u32[]{:S(2)}) collective-permute-start(bf16[64,256]{1,0:T(8,128)(2,1)S(1)} %bitcast.55), channel_id=1, source_target_pairs={{0,384},{384,0},{1,385},{385,1},{2,386},{386,2},{3,387},{387,3},{4... | collective-permute-start | bytes 98312 | tf_op jit(solution)/shard_map/ppermute | solution.py:196
  19.2 36.0 %collective-permute-start.1 = (bf16[35,64,128]{2,1,0:T(8,128)(2,1)S(1)}, bf16[35,64,128]{2,1,0:T(8,128)(2,1)S(1)}, u32[]{:S(2)}, u32[]{:S(2)}) collective-permute-start(bf16[35,64,128]{2,1,0:T(8,128)(2,1)S(1)} %get-tuple-element.17.s0), channel_id=1, source_target_pairs={{0,16},{8,24},{16,0},{24,8},{1,17},{9,25},{17,1},{25,9},{2,18},{10... | collective-permute-start | bytes 1720328 | tf_op jit(solution)/shard_map/ppermute | solution.py:196
  59.7 8.9 %collective-permute-start.4 = (bf16[512,256]{1,0:T(8,128)(2,1)S(1)}, bf16[512,256]{1,0:T(8,128)(2,1)S(1)}, u32[]{:S(2)}, u32[]{:S(2)}) collective-permute-start(bf16[512,256]{1,0:T(8,128)(2,1)S(1)} %get-tuple-element.19), channel_id=1, source_target_pairs={{0,24},{8,0},{16,8},{24,16},{1,25},{9,1},{17,9},{25,17},{2,26},{10... | collective-permute-start | bytes 786440 | tf_op jit(solution)/shard_map/ppermute | solution.py:196
  62.3 8.6 %collective-permute-start.5 = (bf16[512,256]{1,0:T(8,128)(2,1)S(1)}, bf16[512,256]{1,0:T(8,128)(2,1)S(1)}, u32[]{:S(2)}, u32[]{:S(2)}) collective-permute-start(bf16[512,256]{1,0:T(8,128)(2,1)S(1)} %get-tuple-element.20), channel_id=1, source_target_pairs={{0,16},{8,24},{16,0},{24,8},{1,17},{9,25},{17,1},{25,9},{2,18},{10... | collective-permute-start | bytes 786440 | tf_op jit(solution)/shard_map/ppermute | solution.py:196
  66.6 8.3 %collective-permute-start.6 = (bf16[512,256]{1,0:T(8,128)(2,1)S(1)}, bf16[512,256]{1,0:T(8,128)(2,1)S(1)}, u32[]{:S(2)}, u32[]{:S(2)}) collective-permute-start(bf16[512,256]{1,0:T(8,128)(2,1)S(1)} %get-tuple-element.21), channel_id=1, source_target_pairs={{0,8},{8,16},{16,24},{24,0},{1,9},{9,17},{17,25},{25,1},{2,10},{10... | collective-permute-start | bytes 786440 | tf_op jit(solution)/shard_map/ppermute | solution.py:196
  75.9 22.1 %all-to-all-start = ((bf16[8,80,256]{2,1,0:T(8,128)(2,1)}), bf16[8,80,256]{2,1,0:T(8,128)(2,1)S(1)}, u32[]{:S(2)}, u32[]{:S(2)}) async-start(bf16[8,80,256]{2,1,0:T(8,128)(2,1)} %pad_maximum_fusion), calls=%async_computation | async-start | bytes 655360 | tf_op jit(solution)/shard_map/all_to_all | solution.py:254
  98.0 11.0 %collective-permute-start.9 = (bf16[64,256]{1,0:T(8,128)(2,1)S(1)}, bf16[64,256]{1,0:T(8,128)(2,1)S(1)}, u32[]{:S(2)}, u32[]{:S(2)}) collective-permute-start(bf16[64,256]{1,0:T(8,128)(2,1)S(1)} %slice_reduce_fusion), channel_id=1, source_target_pairs={{0,24},{8,0},{16,8},{24,16},{1,25},{9,1},{17,9},{25,17},{2,26},{10... | collective-permute-start | bytes 98312 | tf_op jit(solution)/shard_map/ppermute | solution.py:196
  100.0 9.0 %collective-permute-start.8 = (bf16[64,256]{1,0:T(8,128)(2,1)S(1)}, bf16[64,256]{1,0:T(8,128)(2,1)S(1)}, u32[]{:S(2)}, u32[]{:S(2)}) collective-permute-start(bf16[64,256]{1,0:T(8,128)(2,1)S(1)} %slice_reduce_fusion), channel_id=1, source_target_pairs={{0,16},{8,24},{16,0},{24,8},{1,17},{9,25},{17,1},{25,9},{2,18},{10... | collective-permute-start | bytes 98312 | tf_op jit(solution)/shard_map/ppermute | solution.py:196
  103.1 5.9 %collective-permute-start.7 = (bf16[64,256]{1,0:T(8,128)(2,1)S(1)}, bf16[64,256]{1,0:T(8,128)(2,1)S(1)}, u32[]{:S(2)}, u32[]{:S(2)}) collective-permute-start(bf16[64,256]{1,0:T(8,128)(2,1)S(1)} %slice_reduce_fusion), channel_id=1, source_target_pairs={{0,8},{8,16},{16,24},{24,0},{1,9},{9,17},{17,25},{25,1},{2,10},{10... | collective-permute-start | bytes 98312 | tf_op jit(solution)/shard_map/ppermute | solution.py:196
  127.6 8.4 %copy-start.1 = (bf16[256,256]{1,0:T(8,128)(2,1)S(1)}, bf16[256,256]{1,0:T(8,128)(2,1)}, u32[]{:S(2)}) copy-start(bf16[256,256]{1,0:T(8,128)(2,1)} %w.1) | copy-start | bytes 393220
  127.6 8.4 %collective-permute-start.10 = (bf16[1984,256]{1,0:T(8,128)(2,1)S(1)}, bf16[1984,256]{1,0:T(8,128)(2,1)S(1)}, u32[]{:S(2)}, u32[]{:S(2)}) collective-permute-start(bf16[1984,256]{1,0:T(8,128)(2,1)S(1)} %all_gather.10.r_own), channel_id=1, source_target_pairs={{0,1},{1,0},{2,3},{3,2},{4,5},{5,4},{6,7},{7,6},{8,9},{9,8},{10,11... | collective-permute-start | bytes 3047432 | tf_op jit(solution)/shard_map/ppermute | solution.py:196
  141.9 9.5 %collective-permute-start.11 = (bf16[448,256]{1,0:T(8,128)(2,1)S(1)}, bf16[448,256]{1,0:T(8,128)(2,1)S(1)}, u32[]{:S(2)}, u32[]{:S(2)}) collective-permute-start(bf16[448,256]{1,0:T(8,128)(2,1)S(1)} %get-tuple-element.24), channel_id=1, source_target_pairs={{0,32},{32,64},{64,96},{96,128},{128,160},{160,192},{192,224},{224... | collective-permute-start | bytes 688136 | tf_op jit(solution)/shard_map/ppermute | solution.py:196
  143.8 8.4 %collective-permute-start.12 = (bf16[448,256]{1,0:T(8,128)(2,1)S(1)}, bf16[448,256]{1,0:T(8,128)(2,1)S(1)}, u32[]{:S(2)}, u32[]{:S(2)}) collective-permute-start(bf16[448,256]{1,0:T(8,128)(2,1)S(1)} %get-tuple-element.25), channel_id=1, source_target_pairs={{0,352},{32,0},{64,32},{96,64},{128,96},{160,128},{192,160},{224,1... | collective-permute-start | bytes 688136 | tf_op jit(solution)/shard_map/ppermute | solution.py:196
  148.4 13.4 %collective-permute-start.13 = (bf16[448,256]{1,0:T(8,128)(2,1)S(1)}, bf16[448,256]{1,0:T(8,128)(2,1)S(1)}, u32[]{:S(2)}, u32[]{:S(2)}) collective-permute-start(bf16[448,256]{1,0:T(8,128)(2,1)S(1)} %get-tuple-element.26), channel_id=1, source_target_pairs={{0,320},{32,352},{64,0},{96,32},{128,64},{160,96},{192,128},{224,1... | collective-permute-start | bytes 688136 | tf_op jit(solution)/shard_map/ppermute | solution.py:196

commit v9 on v8

--- a/solution.py
+++ b/solution.py
@@ -99,7 +99,7 @@
 
 
 def bwd_kernel(
-    nz, codes, info, s0, s1, s2, s3, r_own, r_other, lefts, w, out, keep, up, down, back,
+    nz, codes, info, s0, s1, s2, s3, r_own, r_other, lefts, w, out, keep, up, down, fore, back,
     table, pool, agg, cots, ga, acc, gw4, act,
 ):
     rows, feat = 4 * TILE, w.shape[0]
@@ -152,31 +152,35 @@
     low = (part - high.astype(F32)).astype(BF)
     n_chunks = acc.shape[0] // (4 * STRIP)
     n_za = nz // 4
-    for base, ref in ((0, keep), (1, up), (3, down), (2, back)):
+    half = n_chunks // 2
+    whole = range(n_chunks)
+    for base, ref, these in ((0, keep, whole), (1, up, whole), (3, down, whole), (2, back, whole[:half]), (2, fore, whole[half:])):
         which = (my_zb + base) & 3
-        for i in range(n_chunks):
+        for place, i in enumerate(these):
             q = (i // n_za) * nz + 4 * (i % n_za) + which
             block = acc[pl.ds(pl.multiple_of(q * STRIP, STRIP), STRIP), :]
-            ref[i * STRIP : (i + 1) * STRIP, :] = block.astype(ref.dtype)
+            ref[place * STRIP : (place + 1) * STRIP, :] = block.astype(ref.dtype)
     end = n_chunks * STRIP
     keep[end:, :] = part
-    for ref in (up, down, back):
+    for ref, end in ((up, end), (down, end), (back, half * STRIP)):
         ref[end : end + share, :] = high
         ref[end + share :, :] = low
 
 
-def near_kernel(keep, up, down, back, chunks):
+def near_kernel(keep, up, down, fore, back, chunks):
     n_chunks = chunks.shape[0]
+    half = n_chunks // 2
     end = n_chunks * STRIP
     share = keep.shape[0] - end
     for i in range(n_chunks):
         at = slice(i * STRIP, (i + 1) * STRIP)
-        chunks[i, :STRIP, :] = (
-            (keep[at, :] + up[at, :].astype(F32)) + (down[at, :].astype(F32) + back[at, :].astype(F32))
-        ).astype(BF)
+        far, j = (back, i) if i < half else (fore, i - half)
+        away = far[j * STRIP : (j + 1) * STRIP, :].astype(F32)
+        total = (keep[at, :] + up[at, :].astype(F32)) + (down[at, :].astype(F32) + away)
+        chunks[i, :STRIP, :] = total.astype(BF)
     part = keep[end:, :]
-    for ref in (up, down, back):
-        part = part + (ref[end : end + share, :].astype(F32) + ref[end + share :, :].astype(F32))
+    for ref, at in ((up, end), (down, end), (back, half * STRIP)):
+        part = part + (ref[at : at + share, :].astype(F32) + ref[at + share :, :].astype(F32))
     high = part.astype(BF)
     low = (part - high.astype(F32)).astype(BF)
     for i in range(n_chunks):
@@ -246,7 +250,7 @@
         codes, info, *strips, column,
     )
 
-    back = [shift(parts[d], "x", -d) for d in (1, 2, 3)]
+    back = [shift(parts[d], "x", -d) for d in (2, 1, 3)]
     block_sum = (parts[0] + (back[0].astype(F32) + back[1].astype(F32) + back[2].astype(F32))).astype(BF)
     cot_rows = jnp.concatenate(cots, axis=0)
     left = jnp.broadcast_to(cot_rows[4 * STRIP - LEFT :][None], (col_devs, LEFT, feat))
@@ -261,11 +265,12 @@
 
     share = feat // col_devs
     chunk_rows = n_chunks * STRIP
-    output_rows, keep, up, down, back = call(
+    output_rows, keep, up, down, fore, back = call(
         functools.partial(bwd_kernel, nz),
         "backward_tiles",
         [smem, smem] + [vmem] * 8,
-        [((per_dev, feat), BF), ((chunk_rows + share, feat), F32)] + [((chunk_rows + 2 * share, feat), BF)] * 3,
+        [((per_dev, feat), BF), ((chunk_rows + share, feat), F32)] + [((chunk_rows + 2 * share, feat), BF)] * 2
+        + [((chunk_rows // 2, feat), BF), ((chunk_rows // 2 + 2 * share, feat), BF)],
         listing
         + [
             pltpu.VMEM((16 * TILE, feat), BF),
@@ -277,13 +282,14 @@
         ],
         codes, info, *strips, core_rows, other_rows, lefts, weight,
     )
+    back, fore = shift(back, Z, -2), shift(fore, Z, 2)
     (chunks,) = call(
         near_kernel,
         "near_sum",
-        [vmem] * 4,
+        [vmem] * 5,
         [((n_chunks, STRIP + 2 * share, feat), BF)],
         [],
-        keep, shift(up, Z, 1), shift(down, Z, -1), shift(back, Z, -2),
+        keep, shift(up, Z, 1), shift(down, Z, -1), fore, back,
     )
     arrived = lax.all_to_all(chunks, ("yh", "za"), split_axis=0, concat_axis=0, tiled=True)
     node_total = per_dev * lax.axis_size(ROW) * col_devs

time: 205 us -> 205 us (level)
  waiting for transfers between devices: 33.5 us -> 28.8 us
  blocking collectives: 91.8 us -> 95.6 us
    all_to_all x1, blocking collectives: 22 us -> 30.4 us  [on_device(): lax.all_to_all(chunks, ('yh', 'za'), split_axis=0, concat_axis=0, tiled=T...]
    ppermute x14 -> x15, starting transfers between devices: 49.2 us -> 53.9 us  [shift(): return lax.ppermute(value, axis, [(i, (i + by) % n) for i in range(n)])]
    ppermute x14 -> x15, waiting for transfers between devices: 23.4 us -> 18.8 us  [shift(): return lax.ppermute(value, axis, [(i, (i + by) % n) for i in range(n)])]
    all_gather x1, blocking collectives: 18.9 us -> 14.5 us  [on_device(): grad_weight = lax.all_gather(weight_part, COL, axis=0, tiled=True)]
    all_to_all x1, starting transfers between devices: 12.1 us -> 8.65 us  [on_device(): pieces = lax.all_to_all(sent, COL, split_axis=0, concat_axis=0, tiled=True)]
  transfers between devices with their start and end apart: 15 -> 16, of which waited for: 8 -> 7; matrix products, arithmetic and copies ran while one was open for 0% -> 0% of each run, Pallas kernels for 0% -> 0%
where the time goes in v9:
time: 205 us
  blocking collectives  95.6 us (47%)
  starting transfers between devices  62.5 us (30%)
  waiting for transfers between devices  28.8 us (14%)
  Pallas kernels  12.2 us (6%)
  local copies, waits for them, and re-layouts  2.73 us (1%)
    ppermute x15, starting transfers between devices, shift(): return lax.ppermute(value, axis, [(i, (i + by) % n) for i in range(n)])  53.9 us
    all_gather x1, blocking collectives, on_device(): column = lax.all_gather(near, Z, axis=0, tiled=True)  32.3 us
    all_to_all x1, blocking collectives, on_device(): lax.all_to_all(chunks, ('yh', 'za'), split_axis=0, concat_axis=0, tiled=T...  30.4 us
    ppermute x15, waiting for transfers between devices, shift(): return lax.ppermute(value, axis, [(i, (i + by) % n) for i in range(n)])  18.8 us
    all_gather x1, blocking collectives, on_device(): core_rows = lax.all_gather(group_rows, 'yl', axis=0, tiled=True)  18.3 us
    all_gather x1, blocking collectives, on_device(): grad_weight = lax.all_gather(weight_part, COL, axis=0, tiled=True)  14.5 us
    pallas_call x5, Pallas kernels, call(): pl.pallas_call(kernel, out_shape=tuple((jax.ShapeDtypeStruct(s, t) for s,...  12.2 us
    all_to_all x1, waiting for transfers between devices, on_device(): pieces = lax.all_to_all(sent, COL, split_axis=0, concat_axis=0, tiled=True)  10 us
  transfers between devices with their start and end apart: 16, of which 7 were waited for; matrix products, arithmetic and copies ran while one was open for 0% of the time, Pallas kernels for 0%

profile of v9, /device:TPU:1, one launch (start us, length us, event | category | flops | bytes accessed | tf_op | source)
XLA Modules:
  0.0 204.5 jit_solution(12498620752335371598)
XLA Ops:
  4.6 5.2 %collective-permute-start.2 = (bf16[35,64,128]{2,1,0:T(8,128)(2,1)S(1)}, bf16[35,64,128]{2,1,0:T(8,128)(2,1)S(1)}, u32[]{:S(2)}, u32[]{:S(2)}) collective-permute-start(bf16[35,64,128]{2,1,0:T(8,128)(2,1)S(1)} %get-tuple-element.17), channel_id=1, source_target_pairs={{0,24},{8,0},{16,8},{24,16},{1,25},{9,1},{17,9},{25,17},{2,26},{10... | collective-permute-start | bytes 1720328 | tf_op jit(solution)/shard_map/ppermute | solution.py:200
  11.8 7.5 %collective-permute-start.3 = (bf16[64,256]{1,0:T(8,128)(2,1)S(1)}, bf16[64,256]{1,0:T(8,128)(2,1)S(1)}, u32[]{:S(2)}, u32[]{:S(2)}) collective-permute-start(bf16[64,256]{1,0:T(8,128)(2,1)S(1)} %bitcast.55), channel_id=1, source_target_pairs={{0,384},{384,0},{1,385},{385,1},{2,386},{386,2},{3,387},{387,3},{4... | collective-permute-start | bytes 98312 | tf_op jit(solution)/shard_map/ppermute | solution.py:200
  19.2 3.6 %collective-permute-start.1 = (bf16[35,64,128]{2,1,0:T(8,128)(2,1)S(1)}, bf16[35,64,128]{2,1,0:T(8,128)(2,1)S(1)}, u32[]{:S(2)}, u32[]{:S(2)}) collective-permute-start(bf16[35,64,128]{2,1,0:T(8,128)(2,1)S(1)} %get-tuple-element.18.s0), channel_id=1, source_target_pairs={{0,16},{8,24},{16,0},{24,8},{1,17},{9,25},{17,1},{25,9},{2,18},{10... | collective-permute-start | bytes 1720328 | tf_op jit(solution)/shard_map/ppermute | solution.py:200
  22.9 32.3 %all_gather.9.feats = bf16[1536,256]{1,0:T(8,128)(2,1)S(1)} all-gather(bf16[128,256]{1,0:T(8,128)(2,1)S(1)} %pad_maximum_fusion.5), channel_id=1, replica_groups=mesh['yh'=2,'za'=3,'zb'=4,'x'=4,'yl'=4,'core'=2] {'za','zb'}, dimensions={0}, use_global_device_ids=true | all-gather | bytes 851968 | tf_op jit(solution)/shard_map/all_gather | solution.py:241
  55.3 4.4 %forward_tiles.1 = (f32[512,256]{1,0:T(8,128)S(1)}, bf16[512,256]{1,0:T(8,128)(2,1)S(1)}, bf16[512,256]{1,0:T(8,128)(2,1)S(1)}, bf16[512,256]{1,0:T(8,128)(2,1)S(1)}) custom-call(s32[4,32]{1,0:T(4,128)S(1)} %pad_add_fusion.codes, s32[6]{0:T(128)S(1)} %stack.34.info, bf16[35,64,128]{2,1,0:T(8,128)(2,1)S(1)} %get-tuple-element.18.s0, ...), custom_call_target="tpu_custom_call" | custom-call | tf_op jit(solution)/shard_map/forward_tiles/pallas_call | solution.py:218
  59.7 2.0 %collective-permute-start.4 = (bf16[512,256]{1,0:T(8,128)(2,1)S(1)}, bf16[512,256]{1,0:T(8,128)(2,1)S(1)}, u32[]{:S(2)}, u32[]{:S(2)}) collective-permute-start(bf16[512,256]{1,0:T(8,128)(2,1)S(1)} %get-tuple-element.20), channel_id=1, source_target_pairs={{0,16},{8,24},{16,0},{24,8},{1,17},{9,25},{17,1},{25,9},{2,18},{10... | collective-permute-start | bytes 786440 | tf_op jit(solution)/shard_map/ppermute | solution.py:200
  61.8 5.5 %collective-permute-start.5 = (bf16[512,256]{1,0:T(8,128)(2,1)S(1)}, bf16[512,256]{1,0:T(8,128)(2,1)S(1)}, u32[]{:S(2)}, u32[]{:S(2)}) collective-permute-start(bf16[512,256]{1,0:T(8,128)(2,1)S(1)} %get-tuple-element.21), channel_id=1, source_target_pairs={{0,24},{8,0},{16,8},{24,16},{1,25},{9,1},{17,9},{25,17},{2,26},{10... | collective-permute-start | bytes 786440 | tf_op jit(solution)/shard_map/ppermute | solution.py:200
  69.2 4.1 %collective-permute-done.5 = bf16[512,256]{1,0:T(8,128)(2,1)S(1)} collective-permute-done((bf16[512,256]{1,0:T(8,128)(2,1)S(1)}, bf16[512,256]{1,0:T(8,128)(2,1)S(1)}, u32[]{:S(2)}, u32[]{:S(2)}) %collective-permute-start.5) | collective-permute-done | bytes 262176 | tf_op jit(solution)/shard_map/ppermute | solution.py:200
  73.3 4.8 %collective-permute-done.6 = bf16[512,256]{1,0:T(8,128)(2,1)S(1)} collective-permute-done((bf16[512,256]{1,0:T(8,128)(2,1)S(1)}, bf16[512,256]{1,0:T(8,128)(2,1)S(1)}, u32[]{:S(2)}, u32[]{:S(2)}) %collective-permute-start.6) | collective-permute-done | bytes 262176 | tf_op jit(solution)/shard_map/ppermute | solution.py:200
  79.1 8.6 %all-to-all-start = ((bf16[8,80,256]{2,1,0:T(8,128)(2,1)}), bf16[8,80,256]{2,1,0:T(8,128)(2,1)S(1)}, u32[]{:S(2)}, u32[]{:S(2)}) async-start(bf16[8,80,256]{2,1,0:T(8,128)(2,1)} %pad_maximum_fusion), calls=%async_computation | async-start | bytes 655360 | tf_op jit(solution)/shard_map/all_to_all | solution.py:258
  87.8 10.0 %all-to-all-done = bf16[8,80,256]{2,1,0:T(8,128)(2,1)S(1)} async-done(((bf16[8,80,256]{2,1,0:T(8,128)(2,1)}), bf16[8,80,256]{2,1,0:T(8,128)(2,1)S(1)}, u32[]{:S(2)}, u32[]{:S(2)}) %all-to-all-start) | async-done | bytes 327712 | tf_op jit(solution)/shard_map/all_to_all | solution.py:258
  97.8 1.9 collective-permute-start.9
  99.8 2.2 %collective-permute-start.8 = (bf16[64,256]{1,0:T(8,128)(2,1)S(1)}, bf16[64,256]{1,0:T(8,128)(2,1)S(1)}, u32[]{:S(2)}, u32[]{:S(2)}) collective-permute-start(bf16[64,256]{1,0:T(8,128)(2,1)S(1)} %slice_reduce_fusion), channel_id=1, source_target_pairs={{0,16},{8,24},{16,0},{24,8},{1,17},{9,25},{17,1},{25,9},{2,18},{10... | collective-permute-start | bytes 98312 | tf_op jit(solution)/shard_map/ppermute | solution.py:200
  102.0 3.1 %collective-permute-start.7 = (bf16[64,256]{1,0:T(8,128)(2,1)S(1)}, bf16[64,256]{1,0:T(8,128)(2,1)S(1)}, u32[]{:S(2)}, u32[]{:S(2)}) collective-permute-start(bf16[64,256]{1,0:T(8,128)(2,1)S(1)} %slice_reduce_fusion), channel_id=1, source_target_pairs={{0,8},{8,16},{16,24},{24,0},{1,9},{9,17},{17,25},{25,1},{2,10},{10... | collective-permute-start | bytes 98312 | tf_op jit(solution)/shard_map/ppermute | solution.py:200
  105.1 3.7 %collective-permute-done.7 = bf16[64,256]{1,0:T(8,128)(2,1)S(1)} collective-permute-done((bf16[64,256]{1,0:T(8,128)(2,1)S(1)}, bf16[64,256]{1,0:T(8,128)(2,1)S(1)}, u32[]{:S(2)}, u32[]{:S(2)}) %collective-permute-start.7) | collective-permute-done | bytes 32800 | tf_op jit(solution)/shard_map/ppermute | solution.py:200
  108.8 18.3 %all_gather.10.r_own = bf16[1984,256]{1,0:T(8,128)(2,1)S(1)} all-gather(bf16[496,256]{1,0:T(8,128)(2,1)S(1)} %fusion.1), channel_id=1, replica_groups=mesh['yh'=2,'za'=3,'zb'=4,'x'=4,'yl'=4,'core'=2] {'yl'}, dimensions={0}, use_global_device_ids=true | all-gather | bytes 1269760 | tf_op jit(solution)/shard_map/all_gather | solution.py:263
  127.2 6.3 %collective-permute-start.10 = (bf16[1984,256]{1,0:T(8,128)(2,1)S(1)}, bf16[1984,256]{1,0:T(8,128)(2,1)S(1)}, u32[]{:S(2)}, u32[]{:S(2)}) collective-permute-start(bf16[1984,256]{1,0:T(8,128)(2,1)S(1)} %all_gather.10.r_own), channel_id=1, source_target_pairs={{0,1},{1,0},{2,3},{3,2},{4,5},{5,4},{6,7},{7,6},{8,9},{9,8},{10,11... | collective-permute-start | bytes 3047432 | tf_op jit(solution)/shard_map/ppermute | solution.py:200
  133.5 2.2 %collective-permute-done.10.r_other = bf16[1984,256]{1,0:T(8,128)(2,1)S(1)} collective-permute-done((bf16[1984,256]{1,0:T(8,128)(2,1)S(1)}, bf16[1984,256]{1,0:T(8,128)(2,1)S(1)}, u32[]{:S(2)}, u32[]{:S(2)}) %collective-permute-start.10) | collective-permute-done | bytes 1015840 | tf_op jit(solution)/shard_map/ppermute | solution.py:200
  135.7 5.8 %backward_tiles.1 = (bf16[64,256]{1,0:T(8,128)(2,1)}, f32[416,256]{1,0:T(8,128)S(1)}, bf16[448,256]{1,0:T(8,128)(2,1)S(1)}, bf16[448,256]{1,0:T(8,128)(2,1)S(1)}...) custom-call(s32[4,32]{1,0:T(4,128)S(1)} %pad_add_fusion.codes, s32[6]{0:T(128)S(1)} %stack.34.info, ...), custom_call_target="tpu_custom_call" | custom-call | tf_op jit(solution)/shard_map/backward_tiles/pallas_call | solution.py:218
  143.4 4.6 %collective-permute-start.12 = (bf16[448,256]{1,0:T(8,128)(2,1)S(1)}, bf16[448,256]{1,0:T(8,128)(2,1)S(1)}, u32[]{:S(2)}, u32[]{:S(2)}) collective-permute-start(bf16[448,256]{1,0:T(8,128)(2,1)S(1)} %get-tuple-element.26), channel_id=1, source_target_pairs={{0,352},{32,0},{64,32},{96,64},{128,96},{160,128},{192,160},{224,1... | collective-permute-start | bytes 688136 | tf_op jit(solution)/shard_map/ppermute | solution.py:200
  149.9 4.3 %collective-permute-start.13 = (bf16[192,256]{1,0:T(8,128)(2,1)S(1)}, bf16[192,256]{1,0:T(8,128)(2,1)S(1)}, u32[]{:S(2)}, u32[]{:S(2)}) collective-permute-start(bf16[192,256]{1,0:T(8,128)(2,1)S(1)} %get-tuple-element.27), channel_id=1, source_target_pairs={{0,64},{32,96},{64,128},{96,160},{128,192},{160,224},{192,256},{22... | collective-permute-start | bytes 294920 | tf_op jit(solution)/shard_map/ppermute | solution.py:200
  154.2 3.5 %collective-permute-done.13.fore = bf16[192,256]{1,0:T(8,128)(2,1)S(1)} collective-permute-done((bf16[192,256]{1,0:T(8,128)(2,1)S(1)}, bf16[192,256]{1,0:T(8,128)(2,1)S(1)}, u32[]{:S(2)}, u32[]{:S(2)}) %collective-permute-start.13) | collective-permute-done | bytes 98336 | tf_op jit(solution)/shard_map/ppermute | solution.py:200
  158.2 30.4 %all_to_all.10.chunks = bf16[6,128,256]{2,1,0:T(8,128)(2,1)S(1)} all-to-all(bf16[6,128,256]{2,1,0:T(8,128)(2,1)S(1)} %near_sum.1), channel_id=1, replica_groups=mesh['yh'=2,'za'=3,'zb'=4,'x'=4,'yl'=4,'core'=2] {'yh','za'}, dimensions={0} | all-to-all | bytes 786432 | tf_op jit(solution)/shard_map/all_to_all | solution.py:294
  189.3 14.5 %all_gather.11 = f32[256,256]{1,0:T(8,128)S(1)} all-gather(f32[32,256]{1,0:T(8,128)S(1)} %get-tuple-element.30), channel_id=1, replica_groups=mesh['yh'=2,'za'=3,'zb'=4,'x'=4,'yl'=4,'core'=2] {'yl','core'}, dimensions={0}, use_global_device_ids=true | all-gather | bytes 294912 | tf_op jit(solution)/shard_map/all_gather | solution.py:304
  (54 shorter events, 13.8 us)
Async XLA Ops:
  0.6 1.5 copy-start.2
  1.3 0.7 copy-start.4
  1.3 0.7 copy-start.5
  2.1 1.2 copy-start
  3.3 8.4 %copy-start.3 = (bf16[1,64,256]{2,1,0:T(8,128)(2,1)S(1)}, bf16[1,64,256]{2,1,0:T(8,128)(2,1)}, u32[]{:S(2)}) copy-start(bf16[1,64,256]{2,1,0:T(8,128)(2,1)} %param.7) | copy-start | bytes 98308
  4.6 50.6 %collective-permute-start.2 = (bf16[35,64,128]{2,1,0:T(8,128)(2,1)S(1)}, bf16[35,64,128]{2,1,0:T(8,128)(2,1)S(1)}, u32[]{:S(2)}, u32[]{:S(2)}) collective-permute-start(bf16[35,64,128]{2,1,0:T(8,128)(2,1)S(1)} %get-tuple-element.17), channel_id=1, source_target_pairs={{0,24},{8,0},{16,8},{24,16},{1,25},{9,1},{17,9},{25,17},{2,26},{10... | collective-permute-start | bytes 1720328 | tf_op jit(solution)/shard_map/ppermute | solution.py:200
  9.8 45.4 %collective-permute-start = (bf16[35,64,128]{2,1,0:T(8,128)(2,1)S(1)}, bf16[35,64,128]{2,1,0:T(8,128)(2,1)S(1)}, u32[]{:S(2)}, u32[]{:S(2)}) collective-permute-start(bf16[35,64,128]{2,1,0:T(8,128)(2,1)S(1)} %get-tuple-element.17), channel_id=1, source_target_pairs={{0,8},{8,16},{16,24},{24,0},{1,9},{9,17},{17,25},{25,1},{2,10},{10... | collective-permute-start | bytes 1720328 | tf_op jit(solution)/shard_map/ppermute | solution.py:200
  11.8 11.1 %collective-permute-start.3 = (bf16[64,256]{1,0:T(8,128)(2,1)S(1)}, bf16[64,256]{1,0:T(8,128)(2,1)S(1)}, u32[]{:S(2)}, u32[]{:S(2)}) collective-permute-start(bf16[64,256]{1,0:T(8,128)(2,1)S(1)} %bitcast.55), channel_id=1, source_target_pairs={{0,384},{384,0},{1,385},{385,1},{2,386},{386,2},{3,387},{387,3},{4... | collective-permute-start | bytes 98312 | tf_op jit(solution)/shard_map/ppermute | solution.py:200
  19.2 36.0 %collective-permute-start.1 = (bf16[35,64,128]{2,1,0:T(8,128)(2,1)S(1)}, bf16[35,64,128]{2,1,0:T(8,128)(2,1)S(1)}, u32[]{:S(2)}, u32[]{:S(2)}) collective-permute-start(bf16[35,64,128]{2,1,0:T(8,128)(2,1)S(1)} %get-tuple-element.18.s0), channel_id=1, source_target_pairs={{0,16},{8,24},{16,0},{24,8},{1,17},{9,25},{17,1},{25,9},{2,18},{10... | collective-permute-start | bytes 1720328 | tf_op jit(solution)/shard_map/ppermute | solution.py:200
  59.7 9.5 %collective-permute-start.4 = (bf16[512,256]{1,0:T(8,128)(2,1)S(1)}, bf16[512,256]{1,0:T(8,128)(2,1)S(1)}, u32[]{:S(2)}, u32[]{:S(2)}) collective-permute-start(bf16[512,256]{1,0:T(8,128)(2,1)S(1)} %get-tuple-element.20), channel_id=1, source_target_pairs={{0,16},{8,24},{16,0},{24,8},{1,17},{9,25},{17,1},{25,9},{2,18},{10... | collective-permute-start | bytes 786440 | tf_op jit(solution)/shard_map/ppermute | solution.py:200
  61.8 11.6 %collective-permute-start.5 = (bf16[512,256]{1,0:T(8,128)(2,1)S(1)}, bf16[512,256]{1,0:T(8,128)(2,1)S(1)}, u32[]{:S(2)}, u32[]{:S(2)}) collective-permute-start(bf16[512,256]{1,0:T(8,128)(2,1)S(1)} %get-tuple-element.21), channel_id=1, source_target_pairs={{0,24},{8,0},{16,8},{24,16},{1,25},{9,1},{17,9},{25,17},{2,26},{10... | collective-permute-start | bytes 786440 | tf_op jit(solution)/shard_map/ppermute | solution.py:200
  67.2 10.9 %collective-permute-start.6 = (bf16[512,256]{1,0:T(8,128)(2,1)S(1)}, bf16[512,256]{1,0:T(8,128)(2,1)S(1)}, u32[]{:S(2)}, u32[]{:S(2)}) collective-permute-start(bf16[512,256]{1,0:T(8,128)(2,1)S(1)} %get-tuple-element.22), channel_id=1, source_target_pairs={{0,8},{8,16},{16,24},{24,0},{1,9},{9,17},{17,25},{25,1},{2,10},{10... | collective-permute-start | bytes 786440 | tf_op jit(solution)/shard_map/ppermute | solution.py:200
  79.1 18.7 %all-to-all-start = ((bf16[8,80,256]{2,1,0:T(8,128)(2,1)}), bf16[8,80,256]{2,1,0:T(8,128)(2,1)S(1)}, u32[]{:S(2)}, u32[]{:S(2)}) async-start(bf16[8,80,256]{2,1,0:T(8,128)(2,1)} %pad_maximum_fusion), calls=%async_computation | async-start | bytes 655360 | tf_op jit(solution)/shard_map/all_to_all | solution.py:258
  97.8 10.9 %collective-permute-start.9 = (bf16[64,256]{1,0:T(8,128)(2,1)S(1)}, bf16[64,256]{1,0:T(8,128)(2,1)S(1)}, u32[]{:S(2)}, u32[]{:S(2)}) collective-permute-start(bf16[64,256]{1,0:T(8,128)(2,1)S(1)} %slice_reduce_fusion), channel_id=1, source_target_pairs={{0,24},{8,0},{16,8},{24,16},{1,25},{9,1},{17,9},{25,17},{2,26},{10... | collective-permute-start | bytes 98312 | tf_op jit(solution)/shard_map/ppermute | solution.py:200
  99.8 9.0 %collective-permute-start.8 = (bf16[64,256]{1,0:T(8,128)(2,1)S(1)}, bf16[64,256]{1,0:T(8,128)(2,1)S(1)}, u32[]{:S(2)}, u32[]{:S(2)}) collective-permute-start(bf16[64,256]{1,0:T(8,128)(2,1)S(1)} %slice_reduce_fusion), channel_id=1, source_target_pairs={{0,16},{8,24},{16,0},{24,8},{1,17},{9,25},{17,1},{25,9},{2,18},{10... | collective-permute-start | bytes 98312 | tf_op jit(solution)/shard_map/ppermute | solution.py:200
  102.0 6.8 %collective-permute-start.7 = (bf16[64,256]{1,0:T(8,128)(2,1)S(1)}, bf16[64,256]{1,0:T(8,128)(2,1)S(1)}, u32[]{:S(2)}, u32[]{:S(2)}) collective-permute-start(bf16[64,256]{1,0:T(8,128)(2,1)S(1)} %slice_reduce_fusion), channel_id=1, source_target_pairs={{0,8},{8,16},{16,24},{24,0},{1,9},{9,17},{17,25},{25,1},{2,10},{10... | collective-permute-start | bytes 98312 | tf_op jit(solution)/shard_map/ppermute | solution.py:200
  127.2 8.6 %copy-start.1 = (bf16[256,256]{1,0:T(8,128)(2,1)S(1)}, bf16[256,256]{1,0:T(8,128)(2,1)}, u32[]{:S(2)}) copy-start(bf16[256,256]{1,0:T(8,128)(2,1)} %w.1) | copy-start | bytes 393220
  127.2 8.5 %collective-permute-start.10 = (bf16[1984,256]{1,0:T(8,128)(2,1)S(1)}, bf16[1984,256]{1,0:T(8,128)(2,1)S(1)}, u32[]{:S(2)}, u32[]{:S(2)}) collective-permute-start(bf16[1984,256]{1,0:T(8,128)(2,1)S(1)} %all_gather.10.r_own), channel_id=1, source_target_pairs={{0,1},{1,0},{2,3},{3,2},{4,5},{5,4},{6,7},{7,6},{8,9},{9,8},{10,11... | collective-permute-start | bytes 3047432 | tf_op jit(solution)/shard_map/ppermute | solution.py:200
  141.5 16.6 %collective-permute-start.11 = (bf16[448,256]{1,0:T(8,128)(2,1)S(1)}, bf16[448,256]{1,0:T(8,128)(2,1)S(1)}, u32[]{:S(2)}, u32[]{:S(2)}) collective-permute-start(bf16[448,256]{1,0:T(8,128)(2,1)S(1)} %get-tuple-element.25), channel_id=1, source_target_pairs={{0,32},{32,64},{64,96},{96,128},{128,160},{160,192},{192,224},{224... | collective-permute-start | bytes 688136 | tf_op jit(solution)/shard_map/ppermute | solution.py:200
  143.4 14.7 %collective-permute-start.12 = (bf16[448,256]{1,0:T(8,128)(2,1)S(1)}, bf16[448,256]{1,0:T(8,128)(2,1)S(1)}, u32[]{:S(2)}, u32[]{:S(2)}) collective-permute-start(bf16[448,256]{1,0:T(8,128)(2,1)S(1)} %get-tuple-element.26), channel_id=1, source_target_pairs={{0,352},{32,0},{64,32},{96,64},{128,96},{160,128},{192,160},{224,1... | collective-permute-start | bytes 688136 | tf_op jit(solution)/shard_map/ppermute | solution.py:200
  148.0 10.1 %collective-permute-start.14 = (bf16[256,256]{1,0:T(8,128)(2,1)S(1)}, bf16[256,256]{1,0:T(8,128)(2,1)S(1)}, u32[]{:S(2)}, u32[]{:S(2)}) collective-permute-start(bf16[256,256]{1,0:T(8,128)(2,1)S(1)} %get-tuple-element.28), channel_id=1, source_target_pairs={{0,320},{32,352},{64,0},{96,32},{128,64},{160,96},{192,128},{224,1... | collective-permute-start | bytes 393224 | tf_op jit(solution)/shard_map/ppermute | solution.py:200
  149.9 7.8 %collective-permute-start.13 = (bf16[192,256]{1,0:T(8,128)(2,1)S(1)}, bf16[192,256]{1,0:T(8,128)(2,1)S(1)}, u32[]{:S(2)}, u32[]{:S(2)}) collective-permute-start(bf16[192,256]{1,0:T(8,128)(2,1)S(1)} %get-tuple-element.27), channel_id=1, source_target_pairs={{0,64},{32,96},{64,128},{96,160},{128,192},{160,224},{192,256},{22... | collective-permute-start | bytes 294920 | tf_op jit(solution)/shard_map/ppermute | solution.py:200

commit v10 on v9

--- a/solution.py
+++ b/solution.py
@@ -229,7 +229,8 @@
     code = jnp.where(live, tile_rows[0, 0] + 4 * tile_cols[0, 0], -1)
     meta = jnp.pad(code.astype(F32), (0, TILE - slots))[None]
 
-    near = jnp.concatenate([own, shift(own, "yh", 1)], axis=0)
+    facing, meta = lax.optimization_barrier((shift(own, "yh", 1), meta))
+    near = jnp.concatenate([own, facing], axis=0)
 
     parcel = ((slots + 3, STRIP, TILE), BF)
     same, other = call(

time: 205 us -> 208 us (1.015)
  transfers between devices with their start and end apart: 16 -> 16, of which waited for: 7 -> 9; matrix products, arithmetic and copies ran while one was open for 0% -> 0% of each run, Pallas kernels for 0% -> 0%
where the time goes in v10:
time: 208 us; the launch traced here: 207 us
  blocking collectives  97.3 us (47%)
  starting transfers between devices  62.9 us (30%)
  waiting for transfers between devices  29.2 us (14%)
  Pallas kernels  11.8 us (6%)
  local copies, waits for them, and re-layouts  3.29 us (2%)
    ppermute x15, starting transfers between devices, shift(): return lax.ppermute(value, axis, [(i, (i + by) % n) for i in range(n)])  52.7 us
    all_gather x1, blocking collectives, on_device(): column = lax.all_gather(near, Z, axis=0, tiled=True)  33.6 us
    all_to_all x1, blocking collectives, on_device(): lax.all_to_all(chunks, ('yh', 'za'), split_axis=0, concat_axis=0, tiled=T...  29.4 us
    ppermute x15, waiting for transfers between devices, shift(): return lax.ppermute(value, axis, [(i, (i + by) % n) for i in range(n)])  19.2 us
    all_gather x1, blocking collectives, on_device(): core_rows = lax.all_gather(group_rows, 'yl', axis=0, tiled=True)  18.4 us
    all_gather x1, blocking collectives, on_device(): grad_weight = lax.all_gather(weight_part, COL, axis=0, tiled=True)  16 us
    pallas_call x5, Pallas kernels, call(): pl.pallas_call(kernel, out_shape=tuple((jax.ShapeDtypeStruct(s, t) for s,...  11.8 us
    all_to_all x1, starting transfers between devices, on_device(): pieces = lax.all_to_all(sent, COL, split_axis=0, concat_axis=0, tiled=True)  10.2 us
  transfers between devices with their start and end apart: 16, of which 9 were waited for; matrix products, arithmetic and copies ran while one was open for 0% of the time, Pallas kernels for 0%

profile of v10, /device:TPU:1, one launch (start us, length us, event | category | flops | bytes accessed | tf_op | source)
XLA Modules:
  0.0 207.2 jit_solution(2480539320051754966)
XLA Ops:
  0.6 8.3 %collective-permute-start = (bf16[64,256]{1,0:T(8,128)(2,1)}, bf16[64,256]{1,0:T(8,128)(2,1)S(1)}, u32[]{:S(2)}, u32[]{:S(2)}) collective-permute-start(bf16[64,256]{1,0:T(8,128)(2,1)} %bitcast.55), channel_id=1, source_target_pairs={{0,384},{384,0},{1,385},{385,1},{2,386},{386,2},{3,387},{387,3},{4... | collective-permute-start | bytes 98312 | tf_op jit(solution)/shard_map/ppermute | solution.py:200
  13.5 4.4 %collective-permute-start.3 = (bf16[35,64,128]{2,1,0:T(8,128)(2,1)S(1)}, bf16[35,64,128]{2,1,0:T(8,128)(2,1)S(1)}, u32[]{:S(2)}, u32[]{:S(2)}) collective-permute-start(bf16[35,64,128]{2,1,0:T(8,128)(2,1)S(1)} %get-tuple-element.20), channel_id=1, source_target_pairs={{0,24},{8,0},{16,8},{24,16},{1,25},{9,1},{17,9},{25,17},{2,26},{10... | collective-permute-start | bytes 1720328 | tf_op jit(solution)/shard_map/ppermute | solution.py:200
  17.9 1.9 collective-permute-start.1
  19.9 3.6 %collective-permute-start.2 = (bf16[35,64,128]{2,1,0:T(8,128)(2,1)S(1)}, bf16[35,64,128]{2,1,0:T(8,128)(2,1)S(1)}, u32[]{:S(2)}, u32[]{:S(2)}) collective-permute-start(bf16[35,64,128]{2,1,0:T(8,128)(2,1)S(1)} %get-tuple-element.21.s0), channel_id=1, source_target_pairs={{0,16},{8,24},{16,0},{24,8},{1,17},{9,25},{17,1},{25,9},{2,18},{10... | collective-permute-start | bytes 1720328 | tf_op jit(solution)/shard_map/ppermute | solution.py:200
  23.5 33.6 %all_gather.9.feats = bf16[1536,256]{1,0:T(8,128)(2,1)S(1)} all-gather(bf16[128,256]{1,0:T(8,128)(2,1)S(1)} %pad_maximum_fusion.5), channel_id=1, replica_groups=mesh['yh'=2,'za'=3,'zb'=4,'x'=4,'yl'=4,'core'=2] {'za','zb'}, dimensions={0}, use_global_device_ids=true | all-gather | bytes 851968 | tf_op jit(solution)/shard_map/all_gather | solution.py:242
  57.2 4.1 %forward_tiles.1 = (f32[512,256]{1,0:T(8,128)S(1)}, bf16[512,256]{1,0:T(8,128)(2,1)S(1)}, bf16[512,256]{1,0:T(8,128)(2,1)S(1)}, bf16[512,256]{1,0:T(8,128)(2,1)S(1)}) custom-call(s32[4,32]{1,0:T(4,128)S(1)} %pad_add_fusion.codes, s32[6]{0:T(128)S(1)} %stack.34.info, bf16[35,64,128]{2,1,0:T(8,128)(2,1)S(1)} %get-tuple-element.21.s0, ...), custom_call_target="tpu_custom_call" | custom-call | tf_op jit(solution)/shard_map/forward_tiles/pallas_call | solution.py:218
  63.2 4.5 %collective-permute-start.5 = (bf16[512,256]{1,0:T(8,128)(2,1)S(1)}, bf16[512,256]{1,0:T(8,128)(2,1)S(1)}, u32[]{:S(2)}, u32[]{:S(2)}) collective-permute-start(bf16[512,256]{1,0:T(8,128)(2,1)S(1)} %get-tuple-element.25), channel_id=1, source_target_pairs={{0,24},{8,0},{16,8},{24,16},{1,25},{9,1},{17,9},{25,17},{2,26},{10... | collective-permute-start | bytes 786440 | tf_op jit(solution)/shard_map/ppermute | solution.py:200
  69.9 3.9 %collective-permute-done.5 = bf16[512,256]{1,0:T(8,128)(2,1)S(1)} collective-permute-done((bf16[512,256]{1,0:T(8,128)(2,1)S(1)}, bf16[512,256]{1,0:T(8,128)(2,1)S(1)}, u32[]{:S(2)}, u32[]{:S(2)}) %collective-permute-start.5) | collective-permute-done | bytes 262176 | tf_op jit(solution)/shard_map/ppermute | solution.py:200
  73.8 4.7 %collective-permute-done.6 = bf16[512,256]{1,0:T(8,128)(2,1)S(1)} collective-permute-done((bf16[512,256]{1,0:T(8,128)(2,1)S(1)}, bf16[512,256]{1,0:T(8,128)(2,1)S(1)}, u32[]{:S(2)}, u32[]{:S(2)}) %collective-permute-start.6) | collective-permute-done | bytes 262176 | tf_op jit(solution)/shard_map/ppermute | solution.py:200
  79.5 10.2 %all-to-all-start = ((bf16[8,80,256]{2,1,0:T(8,128)(2,1)}), bf16[8,80,256]{2,1,0:T(8,128)(2,1)S(1)}, u32[]{:S(2)}, u32[]{:S(2)}) async-start(bf16[8,80,256]{2,1,0:T(8,128)(2,1)} %pad_maximum_fusion), calls=%async_computation | async-start | bytes 655360 | tf_op jit(solution)/shard_map/all_to_all | solution.py:259
  89.7 10.0 %all-to-all-done = bf16[8,80,256]{2,1,0:T(8,128)(2,1)S(1)} async-done(((bf16[8,80,256]{2,1,0:T(8,128)(2,1)}), bf16[8,80,256]{2,1,0:T(8,128)(2,1)S(1)}, u32[]{:S(2)}, u32[]{:S(2)}) %all-to-all-start) | async-done | bytes 327712 | tf_op jit(solution)/shard_map/all_to_all | solution.py:259
  101.6 2.2 %collective-permute-start.8 = (bf16[64,256]{1,0:T(8,128)(2,1)S(1)}, bf16[64,256]{1,0:T(8,128)(2,1)S(1)}, u32[]{:S(2)}, u32[]{:S(2)}) collective-permute-start(bf16[64,256]{1,0:T(8,128)(2,1)S(1)} %slice_reduce_fusion), channel_id=1, source_target_pairs={{0,16},{8,24},{16,0},{24,8},{1,17},{9,25},{17,1},{25,9},{2,18},{10... | collective-permute-start | bytes 98312 | tf_op jit(solution)/shard_map/ppermute | solution.py:200
  103.8 3.1 %collective-permute-start.7 = (bf16[64,256]{1,0:T(8,128)(2,1)S(1)}, bf16[64,256]{1,0:T(8,128)(2,1)S(1)}, u32[]{:S(2)}, u32[]{:S(2)}) collective-permute-start(bf16[64,256]{1,0:T(8,128)(2,1)S(1)} %slice_reduce_fusion), channel_id=1, source_target_pairs={{0,8},{8,16},{16,24},{24,0},{1,9},{9,17},{17,25},{25,1},{2,10},{10... | collective-permute-start | bytes 98312 | tf_op jit(solution)/shard_map/ppermute | solution.py:200
  106.9 3.7 %collective-permute-done.7 = bf16[64,256]{1,0:T(8,128)(2,1)S(1)} collective-permute-done((bf16[64,256]{1,0:T(8,128)(2,1)S(1)}, bf16[64,256]{1,0:T(8,128)(2,1)S(1)}, u32[]{:S(2)}, u32[]{:S(2)}) %collective-permute-start.7) | collective-permute-done | bytes 32800 | tf_op jit(solution)/shard_map/ppermute | solution.py:200
  110.7 18.4 %all_gather.10.r_own = bf16[1984,256]{1,0:T(8,128)(2,1)S(1)} all-gather(bf16[496,256]{1,0:T(8,128)(2,1)S(1)} %fusion.1), channel_id=1, replica_groups=mesh['yh'=2,'za'=3,'zb'=4,'x'=4,'yl'=4,'core'=2] {'yl'}, dimensions={0}, use_global_device_ids=true | all-gather | bytes 1269760 | tf_op jit(solution)/shard_map/all_gather | solution.py:264
  129.0 6.3 %collective-permute-start.10 = (bf16[1984,256]{1,0:T(8,128)(2,1)S(1)}, bf16[1984,256]{1,0:T(8,128)(2,1)S(1)}, u32[]{:S(2)}, u32[]{:S(2)}) collective-permute-start(bf16[1984,256]{1,0:T(8,128)(2,1)S(1)} %all_gather.10.r_own), channel_id=1, source_target_pairs={{0,1},{1,0},{2,3},{3,2},{4,5},{5,4},{6,7},{7,6},{8,9},{9,8},{10,11... | collective-permute-start | bytes 3047432 | tf_op jit(solution)/shard_map/ppermute | solution.py:200
  135.4 2.2 %collective-permute-done.10.r_other = bf16[1984,256]{1,0:T(8,128)(2,1)S(1)} collective-permute-done((bf16[1984,256]{1,0:T(8,128)(2,1)S(1)}, bf16[1984,256]{1,0:T(8,128)(2,1)S(1)}, u32[]{:S(2)}, u32[]{:S(2)}) %collective-permute-start.10) | collective-permute-done | bytes 1015840 | tf_op jit(solution)/shard_map/ppermute | solution.py:200
  137.6 5.6 %backward_tiles.1 = (bf16[64,256]{1,0:T(8,128)(2,1)}, f32[416,256]{1,0:T(8,128)S(1)}, bf16[448,256]{1,0:T(8,128)(2,1)S(1)}, bf16[448,256]{1,0:T(8,128)(2,1)S(1)}...) custom-call(s32[4,32]{1,0:T(4,128)S(1)} %pad_add_fusion.codes, s32[6]{0:T(128)S(1)} %stack.34.info, ...), custom_call_target="tpu_custom_call" | custom-call | tf_op jit(solution)/shard_map/backward_tiles/pallas_call | solution.py:218
  143.2 2.3 %collective-permute-start.11 = (bf16[448,256]{1,0:T(8,128)(2,1)S(1)}, bf16[448,256]{1,0:T(8,128)(2,1)S(1)}, u32[]{:S(2)}, u32[]{:S(2)}) collective-permute-start(bf16[448,256]{1,0:T(8,128)(2,1)S(1)} %get-tuple-element.29), channel_id=1, source_target_pairs={{0,32},{32,64},{64,96},{96,128},{128,160},{160,192},{192,224},{224... | collective-permute-start | bytes 688136 | tf_op jit(solution)/shard_map/ppermute | solution.py:200
  145.6 4.1 %collective-permute-start.12 = (bf16[448,256]{1,0:T(8,128)(2,1)S(1)}, bf16[448,256]{1,0:T(8,128)(2,1)S(1)}, u32[]{:S(2)}, u32[]{:S(2)}) collective-permute-start(bf16[448,256]{1,0:T(8,128)(2,1)S(1)} %get-tuple-element.30), channel_id=1, source_target_pairs={{0,352},{32,0},{64,32},{96,64},{128,96},{160,128},{192,160},{224,1... | collective-permute-start | bytes 688136 | tf_op jit(solution)/shard_map/ppermute | solution.py:200
  151.6 4.3 %collective-permute-start.13 = (bf16[192,256]{1,0:T(8,128)(2,1)S(1)}, bf16[192,256]{1,0:T(8,128)(2,1)S(1)}, u32[]{:S(2)}, u32[]{:S(2)}) collective-permute-start(bf16[192,256]{1,0:T(8,128)(2,1)S(1)} %get-tuple-element.31), channel_id=1, source_target_pairs={{0,64},{32,96},{64,128},{96,160},{128,192},{160,224},{192,256},{22... | collective-permute-start | bytes 294920 | tf_op jit(solution)/shard_map/ppermute | solution.py:200
  155.9 3.3 %collective-permute-done.13.fore = bf16[192,256]{1,0:T(8,128)(2,1)S(1)} collective-permute-done((bf16[192,256]{1,0:T(8,128)(2,1)S(1)}, bf16[192,256]{1,0:T(8,128)(2,1)S(1)}, u32[]{:S(2)}, u32[]{:S(2)}) %collective-permute-start.13) | collective-permute-done | bytes 98336 | tf_op jit(solution)/shard_map/ppermute | solution.py:200
  160.4 29.4 %all_to_all.10.chunks = bf16[6,128,256]{2,1,0:T(8,128)(2,1)S(1)} all-to-all(bf16[6,128,256]{2,1,0:T(8,128)(2,1)S(1)} %near_sum.1), channel_id=1, replica_groups=mesh['yh'=2,'za'=3,'zb'=4,'x'=4,'yl'=4,'core'=2] {'yh','za'}, dimensions={0} | all-to-all | bytes 786432 | tf_op jit(solution)/shard_map/all_to_all | solution.py:295
  190.5 16.0 %all_gather.11 = f32[256,256]{1,0:T(8,128)S(1)} all-gather(f32[32,256]{1,0:T(8,128)S(1)} %get-tuple-element.34), channel_id=1, replica_groups=mesh['yh'=2,'za'=3,'zb'=4,'x'=4,'yl'=4,'core'=2] {'yl','core'}, dimensions={0}, use_global_device_ids=true | all-gather | bytes 294912 | tf_op jit(solution)/shard_map/all_gather | solution.py:305
  (54 shorter events, 15.4 us)
Async XLA Ops:
  0.6 9.8 %collective-permute-start = (bf16[64,256]{1,0:T(8,128)(2,1)}, bf16[64,256]{1,0:T(8,128)(2,1)S(1)}, u32[]{:S(2)}, u32[]{:S(2)}) collective-permute-start(bf16[64,256]{1,0:T(8,128)(2,1)} %bitcast.55), channel_id=1, source_target_pairs={{0,384},{384,0},{1,385},{385,1},{2,386},{386,2},{3,387},{387,3},{4... | collective-permute-start | bytes 98312 | tf_op jit(solution)/shard_map/ppermute | solution.py:200
  9.6 0.7 copy-start.4
  9.6 0.7 copy-start.5
  10.3 0.8 copy-start.2
  11.0 1.2 copy-start
  12.2 11.2 %copy-start.3 = (bf16[1,64,256]{2,1,0:T(8,128)(2,1)S(1)}, bf16[1,64,256]{2,1,0:T(8,128)(2,1)}, u32[]{:S(2)}) copy-start(bf16[1,64,256]{2,1,0:T(8,128)(2,1)} %param.7) | copy-start | bytes 98308
  13.5 43.6 %collective-permute-start.3 = (bf16[35,64,128]{2,1,0:T(8,128)(2,1)S(1)}, bf16[35,64,128]{2,1,0:T(8,128)(2,1)S(1)}, u32[]{:S(2)}, u32[]{:S(2)}) collective-permute-start(bf16[35,64,128]{2,1,0:T(8,128)(2,1)S(1)} %get-tuple-element.20), channel_id=1, source_target_pairs={{0,24},{8,0},{16,8},{24,16},{1,25},{9,1},{17,9},{25,17},{2,26},{10... | collective-permute-start | bytes 1720328 | tf_op jit(solution)/shard_map/ppermute | solution.py:200
  17.9 39.2 %collective-permute-start.1 = (bf16[35,64,128]{2,1,0:T(8,128)(2,1)S(1)}, bf16[35,64,128]{2,1,0:T(8,128)(2,1)S(1)}, u32[]{:S(2)}, u32[]{:S(2)}) collective-permute-start(bf16[35,64,128]{2,1,0:T(8,128)(2,1)S(1)} %get-tuple-element.20), channel_id=1, source_target_pairs={{0,8},{8,16},{16,24},{24,0},{1,9},{9,17},{17,25},{25,1},{2,10},{10... | collective-permute-start | bytes 1720328 | tf_op jit(solution)/shard_map/ppermute | solution.py:200
  19.9 37.3 %collective-permute-start.2 = (bf16[35,64,128]{2,1,0:T(8,128)(2,1)S(1)}, bf16[35,64,128]{2,1,0:T(8,128)(2,1)S(1)}, u32[]{:S(2)}, u32[]{:S(2)}) collective-permute-start(bf16[35,64,128]{2,1,0:T(8,128)(2,1)S(1)} %get-tuple-element.21.s0), channel_id=1, source_target_pairs={{0,16},{8,24},{16,0},{24,8},{1,17},{9,25},{17,1},{25,9},{2,18},{10... | collective-permute-start | bytes 1720328 | tf_op jit(solution)/shard_map/ppermute | solution.py:200
  61.3 8.6 %collective-permute-start.4 = (bf16[512,256]{1,0:T(8,128)(2,1)S(1)}, bf16[512,256]{1,0:T(8,128)(2,1)S(1)}, u32[]{:S(2)}, u32[]{:S(2)}) collective-permute-start(bf16[512,256]{1,0:T(8,128)(2,1)S(1)} %get-tuple-element.24), channel_id=1, source_target_pairs={{0,16},{8,24},{16,0},{24,8},{1,17},{9,25},{17,1},{25,9},{2,18},{10... | collective-permute-start | bytes 786440 | tf_op jit(solution)/shard_map/ppermute | solution.py:200
  63.2 10.6 %collective-permute-start.5 = (bf16[512,256]{1,0:T(8,128)(2,1)S(1)}, bf16[512,256]{1,0:T(8,128)(2,1)S(1)}, u32[]{:S(2)}, u32[]{:S(2)}) collective-permute-start(bf16[512,256]{1,0:T(8,128)(2,1)S(1)} %get-tuple-element.25), channel_id=1, source_target_pairs={{0,24},{8,0},{16,8},{24,16},{1,25},{9,1},{17,9},{25,17},{2,26},{10... | collective-permute-start | bytes 786440 | tf_op jit(solution)/shard_map/ppermute | solution.py:200
  67.7 10.8 %collective-permute-start.6 = (bf16[512,256]{1,0:T(8,128)(2,1)S(1)}, bf16[512,256]{1,0:T(8,128)(2,1)S(1)}, u32[]{:S(2)}, u32[]{:S(2)}) collective-permute-start(bf16[512,256]{1,0:T(8,128)(2,1)S(1)} %get-tuple-element.26), channel_id=1, source_target_pairs={{0,8},{8,16},{16,24},{24,0},{1,9},{9,17},{17,25},{25,1},{2,10},{10... | collective-permute-start | bytes 786440 | tf_op jit(solution)/shard_map/ppermute | solution.py:200
  79.5 20.2 %all-to-all-start = ((bf16[8,80,256]{2,1,0:T(8,128)(2,1)}), bf16[8,80,256]{2,1,0:T(8,128)(2,1)S(1)}, u32[]{:S(2)}, u32[]{:S(2)}) async-start(bf16[8,80,256]{2,1,0:T(8,128)(2,1)} %pad_maximum_fusion), calls=%async_computation | async-start | bytes 655360 | tf_op jit(solution)/shard_map/all_to_all | solution.py:259
  99.7 10.9 %collective-permute-start.9 = (bf16[64,256]{1,0:T(8,128)(2,1)S(1)}, bf16[64,256]{1,0:T(8,128)(2,1)S(1)}, u32[]{:S(2)}, u32[]{:S(2)}) collective-permute-start(bf16[64,256]{1,0:T(8,128)(2,1)S(1)} %slice_reduce_fusion), channel_id=1, source_target_pairs={{0,24},{8,0},{16,8},{24,16},{1,25},{9,1},{17,9},{25,17},{2,26},{10... | collective-permute-start | bytes 98312 | tf_op jit(solution)/shard_map/ppermute | solution.py:200
  101.6 9.0 %collective-permute-start.8 = (bf16[64,256]{1,0:T(8,128)(2,1)S(1)}, bf16[64,256]{1,0:T(8,128)(2,1)S(1)}, u32[]{:S(2)}, u32[]{:S(2)}) collective-permute-start(bf16[64,256]{1,0:T(8,128)(2,1)S(1)} %slice_reduce_fusion), channel_id=1, source_target_pairs={{0,16},{8,24},{16,0},{24,8},{1,17},{9,25},{17,1},{25,9},{2,18},{10... | collective-permute-start | bytes 98312 | tf_op jit(solution)/shard_map/ppermute | solution.py:200
  103.8 6.8 %collective-permute-start.7 = (bf16[64,256]{1,0:T(8,128)(2,1)S(1)}, bf16[64,256]{1,0:T(8,128)(2,1)S(1)}, u32[]{:S(2)}, u32[]{:S(2)}) collective-permute-start(bf16[64,256]{1,0:T(8,128)(2,1)S(1)} %slice_reduce_fusion), channel_id=1, source_target_pairs={{0,8},{8,16},{16,24},{24,0},{1,9},{9,17},{17,25},{25,1},{2,10},{10... | collective-permute-start | bytes 98312 | tf_op jit(solution)/shard_map/ppermute | solution.py:200
  129.0 8.5 %copy-start.1 = (bf16[256,256]{1,0:T(8,128)(2,1)S(1)}, bf16[256,256]{1,0:T(8,128)(2,1)}, u32[]{:S(2)}) copy-start(bf16[256,256]{1,0:T(8,128)(2,1)} %w.1) | copy-start | bytes 393220
  129.0 8.5 %collective-permute-start.10 = (bf16[1984,256]{1,0:T(8,128)(2,1)S(1)}, bf16[1984,256]{1,0:T(8,128)(2,1)S(1)}, u32[]{:S(2)}, u32[]{:S(2)}) collective-permute-start(bf16[1984,256]{1,0:T(8,128)(2,1)S(1)} %all_gather.10.r_own), channel_id=1, source_target_pairs={{0,1},{1,0},{2,3},{3,2},{4,5},{5,4},{6,7},{7,6},{8,9},{9,8},{10,11... | collective-permute-start | bytes 3047432 | tf_op jit(solution)/shard_map/ppermute | solution.py:200
  143.2 17.1 %collective-permute-start.11 = (bf16[448,256]{1,0:T(8,128)(2,1)S(1)}, bf16[448,256]{1,0:T(8,128)(2,1)S(1)}, u32[]{:S(2)}, u32[]{:S(2)}) collective-permute-start(bf16[448,256]{1,0:T(8,128)(2,1)S(1)} %get-tuple-element.29), channel_id=1, source_target_pairs={{0,32},{32,64},{64,96},{96,128},{128,160},{160,192},{192,224},{224... | collective-permute-start | bytes 688136 | tf_op jit(solution)/shard_map/ppermute | solution.py:200
  145.6 14.7 %collective-permute-start.12 = (bf16[448,256]{1,0:T(8,128)(2,1)S(1)}, bf16[448,256]{1,0:T(8,128)(2,1)S(1)}, u32[]{:S(2)}, u32[]{:S(2)}) collective-permute-start(bf16[448,256]{1,0:T(8,128)(2,1)S(1)} %get-tuple-element.30), channel_id=1, source_target_pairs={{0,352},{32,0},{64,32},{96,64},{128,96},{160,128},{192,160},{224,1... | collective-permute-start | bytes 688136 | tf_op jit(solution)/shard_map/ppermute | solution.py:200
  149.7 10.6 %collective-permute-start.14 = (bf16[256,256]{1,0:T(8,128)(2,1)S(1)}, bf16[256,256]{1,0:T(8,128)(2,1)S(1)}, u32[]{:S(2)}, u32[]{:S(2)}) collective-permute-start(bf16[256,256]{1,0:T(8,128)(2,1)S(1)} %get-tuple-element.32), channel_id=1, source_target_pairs={{0,320},{32,352},{64,0},{96,32},{128,64},{160,96},{192,128},{224,1... | collective-permute-start | bytes 393224 | tf_op jit(solution)/shard_map/ppermute | solution.py:200
  151.6 7.6 %collective-permute-start.13 = (bf16[192,256]{1,0:T(8,128)(2,1)S(1)}, bf16[192,256]{1,0:T(8,128)(2,1)S(1)}, u32[]{:S(2)}, u32[]{:S(2)}) collective-permute-start(bf16[192,256]{1,0:T(8,128)(2,1)S(1)} %get-tuple-element.31), channel_id=1, source_target_pairs={{0,64},{32,96},{64,128},{96,160},{128,192},{160,224},{192,256},{22... | collective-permute-start | bytes 294920 | tf_op jit(solution)/shard_map/ppermute | solution.py:200
